TPU v7x, 256 devices: a whole 4x4x8 slice. The times are simulated.
256 devices in a mesh: phase: 16 (over x_hi, z), space: 16 (over y, x_lo, core).
Axes of the slice: x: 4 (x_hi: 2, x_lo: 2; x = x_hi * 2 + x_lo), y: 4, z: 8, core: 2. Of those that a mesh axis runs over, the one named last changes fastest.
Arguments:
- previous: float32 [32, 2, 5, 128, 1024], P('phase', None, None, 'space'), may hold values from -6 to 6
- forcing: float32 [32, 2, 5, 128, 1024], P('phase', None, None, 'space'), may hold values from -6 to 6
- jacobians: float32 [4, 5, 5], replicated, may hold values from -2.5 to 2.5
- coupling: float32 [4, 128, 1024], P(None, 'space'), may hold values from 0.1 to 0.3
- diagonal: float32 [128, 1024], P('space'), may hold values from 3 to 6
- inertia: float32 [128, 1024], P('space'), may hold values from 0.5 to 4
- pressure_weights: float32 [5], replicated, may hold values from -1 to 1
- surface_cells: int32 [131072], P('space'), may hold values from 0 to 8191
- modal_weights: float32 [131072], P('space'), may hold values from -0.015625 to 0.015625
- phase_index: int32 [32], replicated, may hold values from 0 to 31, each once
Outputs:
- final_state: float32 [32, 2, 5, 128, 1024], P('phase', None, None, 'space')
- influence: float32 [32, 2, 131072], P('phase', None, 'space')
- modal_work: float32 [32, 2], P('phase')
Inputs may be any that keep to these rules, and one draw needn't show every extreme that they name: `phase_index`: each number from 0 to 31 appears once. `surface_cells`: entry s names the cell (row within the block) * 1024 + cell within the row, of the block of rows that begins at row (s // 8192) * 8.
All inputs are finite; a program needn't handle non-finite values.
Results may differ from a plain program's by a relative error of at most 0.0003.
Values sent between devices are 32-bit elements; how exact they have to be, the bound alone decides.
No kernel may reach another device: no remote copies, remote signals or barrier semaphores. Data moves between devices by JAX's collectives and lax.ppermute only.
A program may use at most 128 MiB of HBM per device.

v0:
```python
import functools
import math

import jax
import jax.numpy as jnp
from jax import lax
from jax.experimental import pallas as pl
from jax.experimental.pallas import tpu as pltpu
from jax.sharding import PartitionSpec as P

ITERS = 6
WIDTH = 2
RELAX = 0.8
LANES = 128
WIDE = 256
HIGHEST = lax.Precision.HIGHEST

VMEM = pl.BlockSpec(memory_space=pltpu.VMEM)
SMEM = pl.BlockSpec(memory_space=pltpu.SMEM)
HBM = pl.BlockSpec(memory_space=pltpu.HBM)


def call(kernel, name, out_shapes, scratch, flops, operands, in_specs, out_specs=None):
    return pl.pallas_call(
        kernel,
        name=name,
        out_shape=[jax.ShapeDtypeStruct(s, d) for s, d in out_shapes],
        in_specs=in_specs,
        out_specs=out_specs or [VMEM] * len(out_shapes),
        scratch_shapes=scratch,
        compiler_params=pltpu.CompilerParams(vmem_limit_bytes=40 * 1024 * 1024),
        cost_estimate=pl.CostEstimate(
            flops=flops, bytes_accessed=1 << 20, transcendentals=0
        ),
    )(*operands)


def pack_kernel(
    x_hbm, f_hbm, cpl_hbm, diag_hbm, inert_hbm, coef_ref, up_ref, down_ref, x_ref, f_ref, diag_ref, inert_ref, sems
):
    copies = [
        pltpu.make_async_copy(src, dst, sems.at[i])
        for i, (src, dst) in enumerate(
            [(x_hbm.at[p, c], x_ref.at[p, c]) for p in range(2) for c in range(2)]
            + [
                (diag_hbm, diag_ref),
                (inert_hbm, inert_ref),
                (cpl_hbm, coef_ref.at[0:4]),
            ]
            + [(f_hbm.at[p, c], f_ref.at[p, c]) for p in range(2) for c in range(2)]
        )
    ]
    for copy in copies:
        copy.start()
    for i in range(4):
        p, c = i // 2, i % 2
        copies[i].wait()
        for v in range(5):
            for r in range(2):
                at = 8 * v + 4 * p + 2 * r + c
                up_ref[at : at + 1, :] = x_ref[p, c, v, 6 + r : 7 + r, :]
                down_ref[at : at + 1, :] = x_ref[p, c, v, r : r + 1, :]
    for copy in copies[4:7]:
        copy.wait()
    diag = diag_ref[...]
    inert = inert_ref[...]
    scale = RELAX / (diag * diag + inert * inert)
    coef_ref[4] = diag * scale
    coef_ref[5] = inert * scale
    for i in range(6):
        up_ref[60 + i : 61 + i, :] = coef_ref[i, 7:8, :]
        down_ref[60 + i : 61 + i, :] = coef_ref[i, 0:1, :]
    for i in range(4):
        p, c = i // 2, i % 2
        copies[7 + i].wait()
        for v in range(5):
            at = 40 + 4 * v + 2 * p + c
            up_ref[at : at + 1, :] = f_ref[p, c, v, 7:8, :]
            down_ref[at : at + 1, :] = f_ref[p, c, v, 0:1, :]


def tables_kernel(jac_ref, rot_ref, own_ref, plain_ref, lo_ref, hi_ref):
    def split(a):
        high = a.astype(jnp.bfloat16).astype(jnp.float32)
        return jnp.concatenate([high, high, a - high], axis=1).astype(jnp.bfloat16)

    j = lax.broadcasted_iota(jnp.int32, (8, 48), 0)
    k = lax.broadcasted_iota(jnp.int32, (8, 48), 1)
    tiles = []
    for d in range(4):
        near = (jnp.where(j == 0, -99, j - 1), jnp.where(j == 7, -99, j + 1), j, j)[d]
        for v in range(5):
            total = jnp.zeros((8, 48), jnp.float32)
            for w in range(5):
                total = jnp.where(k == 8 * w + near, jac_ref[d, v, w], total)
            tiles.append(total)
    own_ref[...] = split(jnp.concatenate(tiles, axis=0))

    row = lax.broadcasted_iota(jnp.int32, (8, 80), 0)
    col = lax.broadcasted_iota(jnp.int32, (8, 80), 1)
    second = col >= 40
    inner = jnp.where(second, col - 40, col)
    var = inner >> 3
    from_row = jnp.where(second, 2, 0) + ((inner >> 1) & 1)
    to_row = 1 + ((row >> 1) & 1)
    part, from_part = row & 1, inner & 1
    phase = row >> 2
    same_phase = phase == ((inner >> 2) & 1)

    def turn(c, s):
        cos = jnp.where(phase == 0, rot_ref[c], rot_ref[4 + c])
        sin = jnp.where(phase == 0, rot_ref[s], rot_ref[4 + s])
        return jnp.where(part == from_part, cos, jnp.where(part == 0, -sin, sin))

    straight = jnp.where(part == from_part, 1.0, 0.0)
    factors = (
        straight,
        jnp.where(second, straight, turn(0, 1)),
        jnp.where(second, turn(2, 3), straight),
    )
    tiles = [[], [], []]
    for d in range(5):
        near = to_row + (-1, 1, 0, 0, 0)[d]
        here = same_phase & (from_row == near)
        for v in range(5):
            if d == 4:
                value = jnp.where(var == v, 1.0 - RELAX, 0.0)
            else:
                value = jnp.zeros((8, 80), jnp.float32)
                for w in range(5):
                    value = jnp.where(var == w, jac_ref[d, v, w], value)
            value = jnp.where(here, value, 0.0)
            for i in range(3):
                tiles[i].append(value * factors[i])
    for i, ref in enumerate((plain_ref, lo_ref, hi_ref)):
        ref[...] = split(jnp.concatenate(tiles[i], axis=0))


def hot_kernel(idx_ref, weight_ref, hot_ref, cell_ref, sum_ref):
    shape = hot_ref.shape[1:]
    chunk = shape[1]
    groups = cell_ref.shape[1] // WIDE
    rows = 8 * groups
    sum_ref[...] = jnp.zeros_like(sum_ref)

    def one(d, _):
        idx = idx_ref[d]
        low = jnp.broadcast_to(idx & (WIDE - 1), shape)
        hot = jnp.where(lax.broadcasted_iota(jnp.int32, shape, 0) == low, 1.0, 0.0).astype(jnp.bfloat16)
        hot_ref[d] = hot
        top = jnp.broadcast_to(idx >> 8, (rows, chunk))
        row = lax.broadcasted_iota(jnp.int32, (rows, chunk), 0)
        weight = jnp.where(top == (row & 7) * groups + (row >> 3), jnp.broadcast_to(weight_ref[d], (rows, chunk)), 0.0)
        parts = []
        for _ in range(3):
            part = weight.astype(jnp.bfloat16).astype(jnp.float32)
            parts.append(part)
            weight = weight - part
        sum_ref[...] += lax.dot_general(
            jnp.concatenate(parts, axis=0).astype(jnp.bfloat16),
            hot,
            (((1,), (1,)), ((), ())),
            preferred_element_type=jnp.float32,
        )
        return 0

    lax.fori_loop(0, hot_ref.shape[0], one, 0, unroll=2)
    for g in range(groups):
        total = sum_ref[8 * g : 8 * g + 8, :]
        for i in range(1, 3):
            total = total + sum_ref[rows * i + 8 * g : rows * i + 8 * g + 8, :]
        cell_ref[:, g * WIDE : (g + 1) * WIDE] = total


def multiply(table, b):
    high = b.astype(jnp.bfloat16)
    low = (b - high.astype(jnp.float32)).astype(jnp.bfloat16)
    return jnp.dot(
        table,
        jnp.concatenate([high, low, high], axis=0),
        preferred_element_type=jnp.float32,
    )


def remainder(y, coef, forcing):
    cells = forcing.shape[-1]
    lane = lax.broadcasted_iota(jnp.int32, (8, cells), 1)
    before = jnp.where(lane == 0, 0.0, pltpu.roll(y[2], 1, 1))
    after = jnp.where(lane == cells - 1, 0.0, pltpu.roll(y[3], cells - 1, 1))
    return forcing - coef[0] * y[0] - coef[1] * y[1] - coef[2] * before - coef[3] * after


def pre_kernel(first, x_ref, f_ref, coef_ref, own_ref, *refs):
    if first:
        next_ref, mid_ref, ef_ref, ecoef_ref, b_ref, y_ref = refs
    else:
        edge_refs, (next_ref, mid_ref, b_ref, y_ref) = refs[:2], refs[2:]
    cells = x_ref.shape[-1]
    if first:
        row = lax.broadcasted_iota(jnp.int32, (8, cells), 0)
        for h in range(2):
            for i in range(6):
                tile = jnp.where(
                    (row >> 1) & 1 == 0,
                    jnp.broadcast_to(coef_ref[i, 6 * h : 6 * h + 1, :], (8, cells)),
                    jnp.broadcast_to(coef_ref[i, 6 * h + 1 : 6 * h + 2, :], (8, cells)),
                )
                ecoef_ref[h, i] = jnp.where(row & 1 == 0, tile, -tile) if i == 5 else tile
            for n in range(20):
                p, c, v = n // 10, n // 5 % 2, n % 5
                for r in range(2):
                    at = 4 * p + 2 * r + c
                    ef_ref[h, v, at : at + 1, :] = f_ref[p, c, v, 6 * h + r : 6 * h + r + 1, :]
    for c in range(2):
        b_ref[c, 40:48, :] = jnp.zeros((8, cells), jnp.float32)
    coef = [coef_ref[i] for i in range(6)]
    for p in range(2):
        for c in range(2):
            b_ref[c, 0:40, :] = x_ref[p, c].reshape(40, cells)
            if not first:
                for h in range(2):
                    for v in range(5):
                        for r in range(2):
                            at, to = 8 * v + 4 * p + 2 * r + c, 8 * v + 6 * h + r
                            b_ref[c, to : to + 1, :] = edge_refs[h][at : at + 1, :]
        for sweep in range(2):
            for c in range(2):
                y_ref[c] = multiply(own_ref[...], b_ref[c])
            for v in range(5):
                re, im = (
                    remainder(
                        [y_ref[c, 40 * d + 8 * v : 40 * d + 8 * v + 8, :] for d in range(4)],
                        coef,
                        f_ref[p, c, v],
                    )
                    for c in range(2)
                )
                add = (coef[4] * re + coef[5] * im, coef[4] * im - coef[5] * re)
                for c in range(2):
                    new = (1.0 - RELAX) * b_ref[c, 8 * v : 8 * v + 8, :] + add[c]
                    if sweep == 0:
                        b_ref[c, 8 * v : 8 * v + 8, :] = new
                        for h in range(2):
                            for r in range(2):
                                at = 8 * v + 4 * p + 2 * r + c
                                mid_ref[h, at : at + 1, :] = new[4 * h + r + 1 : 4 * h + r + 2, :]
                    else:
                        next_ref[p, c, v] = new


def post_kernel(first, last, rot_ref, plain_ref, lo_turn_ref, hi_turn_ref, ef_ref, ecoef_ref, lo_ref, hi_ref, up_ref, down_ref, mid_ref, *refs):
    if first:
        down_out, up_out, gf_ref, gcoef_ref = refs
    elif last:
        gf_ref, gcoef_ref, cell_ref, part_work_ref, pw_ref, down_out, up_out, press_ref, work_ref = refs
    else:
        gf_ref, gcoef_ref, down_out, up_out = refs
    cells = lo_ref.shape[-1]
    row = lax.broadcasted_iota(jnp.int32, (8, cells), 0)

    if first:
        for h in range(2):
            rows = (lo_ref, down_ref) if h == 0 else (up_ref, hi_ref)
            for i in range(6):
                tile = jnp.where(
                    (row >> 1) & 1 == 0,
                    jnp.broadcast_to(rows[0][60 + i : 61 + i, :], (8, cells)),
                    jnp.broadcast_to(rows[1][60 + i : 61 + i, :], (8, cells)),
                )
                gcoef_ref[h, i] = jnp.where(row & 1 == 0, tile, -tile) if i == 5 else tile
            ghost, base = (lo_ref, 0) if h == 0 else (hi_ref, 2)
            for v in range(5):
                for p in range(2):
                    cos, sin = rot_ref[4 * p + base], rot_ref[4 * p + base + 1]
                    at = 40 + 4 * v + 2 * p
                    re = ghost[at : at + 1, :]
                    im = ghost[at + 1 : at + 2, :]
                    turned = (cos * re - sin * im, sin * re + cos * im)
                    to = 4 * p + 2 * h
                    gf_ref[h, v, to : to + 1, :] = turned[0]
                    gf_ref[h, v, to + 1 : to + 2, :] = turned[1]
                    to = 4 * p + 2 - 2 * h
                    gf_ref[h, v, to : to + 2, :] = (down_ref if h == 0 else up_ref)[at : at + 2, :]

    def sweep(table, b, coef, forcing):
        y = multiply(table[...], b)
        new = []
        for v in range(5):
            at = [40 * d + 8 * v for d in range(5)]
            rest = remainder([y[at[d] : at[d] + 8] for d in range(4)], coef, forcing[v])
            partner = jnp.where(row & 1 == 0, pltpu.roll(rest, 7, 0), pltpu.roll(rest, 1, 0))
            new.append(y[at[4] : at[4] + 8] + coef[4] * rest + coef[5] * partner)
        return jnp.concatenate(new, axis=0)

    mids = []
    for h in range(2):
        pair = (up_ref, hi_ref) if h else (lo_ref, down_ref)
        mids.append(
            sweep(
                hi_turn_ref if h else lo_turn_ref,
                jnp.concatenate([ref[0:40, :] for ref in pair], axis=0),
                [gcoef_ref[h, i] for i in range(6)],
                [gf_ref[h, v] for v in range(5)],
            )
        )
    for h in range(2):
        new = sweep(
            plain_ref,
            jnp.concatenate([mid_ref[1], mids[1]] if h else [mids[0], mid_ref[0]], axis=0),
            [ecoef_ref[h, i] for i in range(6)],
            [ef_ref[h, v] for v in range(5)],
        )
        (up_out if h else down_out)[...] = new
        if last:
            press = pw_ref[0] * new[0:8]
            for v in range(1, 5):
                press = press + pw_ref[v] * new[8 * v : 8 * v + 8]
            press_ref[h] = press
            weight = jnp.where(
                (row >> 1) & 1 == 0,
                jnp.broadcast_to(cell_ref[6 * h : 6 * h + 1, :], (8, cells)),
                jnp.broadcast_to(cell_ref[6 * h + 1 : 6 * h + 2, :], (8, cells)),
            )
            work = weight * press if h == 0 else work + weight * press
    if last:
        work = jnp.broadcast_to(jnp.sum(work, axis=1, keepdims=True), (8, LANES))
        both = work + pltpu.roll(work, 6, 0)
        work_ref[0:2, :] = both[0:2] + part_work_ref[0:2, :]
        work_ref[2:4, :] = both[4:6] + part_work_ref[2:4, :]


def inner_kernel(pw_ref, x_ref, idx_ref, hot_ref, cell_ref, out_ref, work_ref, table_ref):
    cells = x_ref.shape[-1]
    chunk = idx_ref.shape[-1]
    parts = idx_ref.shape[0]
    groups = cells // WIDE
    half = 16 * groups
    row = lax.broadcasted_iota(jnp.int32, (8, cells), 0)
    kept = (row >= 2) & (row < 6)
    press = []
    for i in range(4):
        value = pw_ref[0] * x_ref[i // 2, i % 2, 0]
        for v in range(1, 5):
            value = value + pw_ref[v] * x_ref[i // 2, i % 2, v]
        value = jnp.where(kept, value, 0.0)
        press.append(value)
        work = jnp.sum(jnp.sum(value * cell_ref[...], axis=1, keepdims=True), axis=0, keepdims=True)
        work_ref[i : i + 1, :] = jnp.broadcast_to(work, (1, LANES))
    for i in range(2):
        value = press[2 * i] + pltpu.roll(press[2 * i + 1], 4, 0)
        high = value.astype(jnp.bfloat16).astype(jnp.float32)
        for g in range(groups):
            at = (i * groups + g) * 8
            table_ref[at : at + 8, :] = high[:, g * WIDE : (g + 1) * WIDE]
            table_ref[half + at : half + at + 8, :] = (value - high)[:, g * WIDE : (g + 1) * WIDE]
    table = table_ref[...].astype(jnp.bfloat16)
    row = lax.broadcasted_iota(jnp.int32, (8, chunk), 0)
    place = jnp.where((row >= 2) & (row < 6), row, (row + 4) & 7) * groups
    mine = (row >= 2) & (row < 6)

    def one(d, _):
        both = jnp.dot(table, hot_ref[d], preferred_element_type=jnp.float32)
        found = both[:half] + both[half:]
        top = jnp.broadcast_to(idx_ref[d] >> 8, (8, chunk))
        res = []
        for i in range(2):
            total = jnp.zeros((8, chunk), jnp.float32)
            for g in range(groups):
                at = (i * groups + g) * 8
                total = jnp.where(top == place + g, found[at : at + 8], total)
            res.append(jnp.sum(jnp.where(mine, total, 0.0), axis=0, keepdims=True))
            res.append(jnp.sum(jnp.where(mine, 0.0, total), axis=0, keepdims=True))
        out_ref[d] = jnp.concatenate(res, axis=0)
        return 0

    lax.fori_loop(0, parts, one, 0, unroll=4)


def surface_kernel(press_ref, idx_ref, hot_ref, inner_ref, work_ref, out_ref):
    cells = press_ref.shape[-1]
    chunk = idx_ref.shape[-1]
    parts = idx_ref.shape[0]
    groups = cells // WIDE
    half = 16 * groups
    tiles = [press_ref[h, :, g * WIDE : (g + 1) * WIDE] for h in range(2) for g in range(groups)]
    value = jnp.concatenate(tiles, axis=0)
    high = value.astype(jnp.bfloat16)
    low = (value - high.astype(jnp.float32)).astype(jnp.bfloat16)
    table = jnp.concatenate([high, low], axis=0)
    row = lax.broadcasted_iota(jnp.int32, (8, chunk), 0)
    place = ((row >> 1) & 1) * groups

    def one(d, _):
        both = jnp.dot(table, hot_ref[d], preferred_element_type=jnp.float32)
        found = both[:half] + both[half:]
        top = jnp.broadcast_to(idx_ref[d] >> 8, (8, chunk))
        total = jnp.zeros((8, chunk), jnp.float32)
        for h in range(2):
            for g in range(groups):
                at = (h * groups + g) * 8
                total = jnp.where(top == place + (6 * h * groups + g), found[at : at + 8], total)
        total = total + pltpu.roll(total, 6, 0)
        out_ref[d, 0:2, 0:chunk] = inner_ref[d, 0:2, :] + total[0:2]
        out_ref[d, 2:4, 0:chunk] = inner_ref[d, 2:4, :] + total[4:6]
        out_ref[d, :, chunk : chunk + LANES] = work_ref[...]
        return 0

    lax.fori_loop(0, parts, one, 0, unroll=4)


def merge_kernel(x_ref, down_ref, up_ref, out_ref):
    for n in range(20):
        p, c, v = n // 10, n // 5 % 2, n % 5
        out_ref[p, c, v] = x_ref[p, c, v]
        for h, ref in enumerate((down_ref, up_ref)):
            for r in range(2):
                at, to = 8 * v + 4 * p + 2 * r + c, 6 * h + r
                out_ref[p, c, v, to : to + 1, :] = ref[at : at + 1, :]


def work_kernel(table_ref, x_ref, work_ref):
    chunk = x_ref.shape[-1] - LANES
    rows = jnp.concatenate([x_ref[d, :, chunk:] for d in range(x_ref.shape[0])], axis=0)
    work_ref[...] = jnp.dot(
        table_ref[...], rows, precision=HIGHEST, preferred_element_type=jnp.float32
    )


def phase_kernel(table_ref, x_ref, out_ref):
    parts = x_ref.shape[0]
    chunk = out_ref.shape[-1]
    rows = jnp.concatenate([x_ref[d, :, 0:chunk] for d in range(parts)], axis=0)
    y = jnp.dot(table_ref[...], rows, precision=HIGHEST, preferred_element_type=jnp.float32)
    for d in range(parts):
        out_ref[d] = y[4 * d : 4 * d + 4]


def place_kernel(x_ref, work_ref, out_ref, modal_ref):
    chunk = x_ref.shape[-1]
    for d in range(x_ref.shape[0]):
        for m in range(2):
            out_ref[m, :, d * chunk : (d + 1) * chunk] = x_ref[d, 2 * m : 2 * m + 2, :]
    lane = lax.broadcasted_iota(jnp.int32, (1, 2), 1)
    for m in range(2):
        re = jnp.broadcast_to(work_ref[2 * m : 2 * m + 1, 0:1], (1, 2))
        im = jnp.broadcast_to(work_ref[2 * m + 1 : 2 * m + 2, 0:1], (1, 2))
        modal_ref[m : m + 1, :] = jnp.where(lane == 0, re, im)


def phase_table(phase_index, blades):
    ids = jnp.arange(blades, dtype=jnp.int32)
    turns = ids[:, None] * phase_index[None, :] % blades
    angle = 2.0 * math.pi / blades * turns.astype(jnp.float32)
    cos, sin = jnp.cos(angle) / blades, jnp.sin(angle) / blades
    top = jnp.stack([cos, -sin], axis=2).reshape(blades, 2 * blades)
    bottom = jnp.stack([sin, cos], axis=2).reshape(blades, 2 * blades)
    return jnp.stack([top, bottom], axis=1).reshape(2 * blades, 2 * blades)


def per_device(
    previous,
    forcing,
    jacobians,
    coupling,
    diagonal,
    inertia,
    pressure_weights,
    surface_cells,
    modal_weights,
    phase_index,
):
    f32 = jnp.float32
    blades = phase_index.shape[0]
    cells = previous.shape[-1]
    entries = surface_cells.shape[0]
    devices = lax.axis_size("phase")
    count = lax.axis_size("space")
    here = lax.axis_index("space")
    forward = [(i, (i + 1) % count) for i in range(count)]
    backward = [((i + 1) % count, i) for i in range(count)]

    local_index = lax.dynamic_slice_in_dim(phase_index, lax.axis_index("phase") * 2, 2)
    angles = 2.0 * math.pi / blades * local_index.astype(f32)
    cos, sin = jnp.cos(angles), jnp.sin(angles)
    low_end, high_end = here == 0, here == count - 1
    turn = jnp.stack(
        [
            jnp.where(low_end, cos, 1.0),
            jnp.where(low_end, -sin, 0.0),
            jnp.where(high_end, cos, 1.0),
            jnp.where(high_end, sin, 0.0),
        ],
        axis=1,
    ).reshape(8)
    table = phase_table(phase_index, blades)
    chunk = entries // devices
    idx = surface_cells.reshape(devices, 1, chunk)

    coef, up, down, state, forcing = call(
        pack_kernel,
        "pack",
        [((6, 8, cells), f32), ((66, cells), f32), ((66, cells), f32)]
        + [(previous.shape, f32)] * 2,
        [
            pltpu.VMEM((8, cells), f32),
            pltpu.VMEM((8, cells), f32),
            pltpu.SemaphoreType.DMA((11,)),
        ],
        1 << 20,
        [
            pltpu.with_memory_space_constraint(a, pltpu.HBM)
            for a in (previous, forcing, coupling, diagonal, inertia)
        ],
        [HBM] * 5,
    )
    bf16 = jnp.bfloat16
    own, *tables = call(
        tables_kernel,
        "tables",
        [((160, 144), bf16)] + [((200, 240), bf16)] * 3,
        [],
        1 << 20,
        [jacobians, turn],
        [SMEM] * 2,
    )
    hot, cell_weight = call(
        hot_kernel,
        "onehot",
        [((devices, WIDE, chunk), bf16), ((8, cells), f32)],
        [pltpu.VMEM((96 * cells // 1024, WIDE), f32)],
        8 << 20,
        [idx, modal_weights.reshape(devices, 1, chunk)],
        [VMEM] * 2,
    )
    steps = ITERS // WIDTH
    edge_shape = (2, 5, 8, cells)
    for step in range(steps):
        first, last = step == 0, step == steps - 1
        lo = lax.ppermute(up, "space", forward)
        hi = lax.ppermute(down, "space", backward)
        operands = [state, forcing, coef, own] + ([] if first else [down, up])
        got = call(
            functools.partial(pre_kernel, first),
            "pre",
            [(previous.shape, f32), ((2, 40, cells), f32)]
            + ([(edge_shape, f32), ((2, 6, 8, cells), f32)] if first else []),
            [pltpu.VMEM((2, 48, cells), f32), pltpu.VMEM((2, 160, cells), f32)],
            40 << 20,
            operands,
            [VMEM] * len(operands),
        )
        state, mid = got[:2]
        if first:
            edges = got[2:]
            ghosts = ()
        if step == 1:
            mid, hot, cell_weight = lax.optimization_barrier((mid, hot, cell_weight))
        outs = [((40, cells), f32)] * 2
        operands = [turn, *tables, *edges, lo, hi, up, down, mid, *ghosts]
        specs = [SMEM] + [VMEM] * (len(operands) - 1)
        if first:
            outs += [(edge_shape, f32), ((2, 6, 8, cells), f32)]
        if last:
            inner, inner_work = call(
                inner_kernel,
                "inner",
                [((devices, 4, chunk), f32), ((4, LANES), f32)],
                [pltpu.VMEM((128, WIDE), f32)],
                20 << 20,
                [pressure_weights, state, idx, hot, cell_weight],
                [SMEM] + [VMEM] * 4,
            )
            outs += [((2, 8, cells), f32), ((4, LANES), f32)]
            operands += [cell_weight, inner_work, pressure_weights]
            specs += [VMEM, VMEM, SMEM]
        down, up, *got = call(
            functools.partial(post_kernel, first, last),
            "post",
            outs,
            [],
            20 << 20,
            operands,
            specs,
        )
        if first:
            ghosts = got
    press, work = got
    (mine,) = call(
        surface_kernel,
        "surface",
        [((devices, 4, chunk + LANES), f32)],
        [],
        1 << 28,
        [press, idx, hot, inner, work],
        [VMEM] * 5,
    )
    (state,) = call(
        merge_kernel, "merge", [(previous.shape, f32)], [], 1 << 20, [state, down, up], [VMEM] * 3
    )

    every = lax.all_to_all(mine, "phase", 0, 0, tiled=True)
    every, state = lax.optimization_barrier((every, state))
    own_table = lax.dynamic_slice_in_dim(table, lax.axis_index("phase") * 4, 4)
    (work,) = call(
        work_kernel, "work", [((4, LANES), f32)], [], 1 << 16, [own_table, every], [VMEM] * 2
    )
    work, ready = lax.optimization_barrier((work, every))

    def across(bits):
        return lax.ppermute(work, "space", [(i, i ^ bits) for i in range(count)])

    work = (work + across(4)) + (across(8) + across(12))
    work = (work + across(1)) + (across(2) + across(3))
    (turned,) = call(
        phase_kernel,
        "phases",
        [((devices, 4, chunk), f32)],
        [],
        1 << 24,
        [table, ready],
        [VMEM] * 2,
    )
    blocks = lax.all_to_all(turned, "phase", 0, 0, tiled=True)
    influence, modal_work = call(
        place_kernel,
        "place",
        [((2, 2, entries), f32), ((2, 2), f32)],
        [],
        1 << 16,
        [blocks, work],
        [VMEM] * 2,
    )
    return state, influence, modal_work


def solution(mesh):
    in_specs = (
        P("phase", None, None, "space", None),
        P("phase", None, None, "space", None),
        P(),
        P(None, "space", None),
        P("space", None),
        P("space", None),
        P(),
        P("space"),
        P("space"),
        P(),
    )
    out_specs = (P("phase", None, None, "space", None), P("phase", None, "space"), P("phase", None))
    return jax.shard_map(
        per_device, mesh=mesh, in_specs=in_specs, out_specs=out_specs, check_vma=False
    )
```

profile of v0, /device:TPU:32, one launch (start us, length us, event | category | flops | bytes accessed | tf_op | source)
XLA Modules:
  0.0 75.6 jit_solution(12250136965625348106)
XLA Ops:
  0.7 1.6 %pack.1 = (f32[6,8,1024]{2,1,0:T(8,128)S(1)}, f32[66,1024]{1,0:T(8,128)S(1)}, f32[66,1024]{1,0:T(8,128)S(1)}, f32[2,2,5,8,1024]{4,3,2,1,0:T(8,128)S(1)}, f32[2,2,5,8,1024]{4,3,2,1,0:T(8,128)S(1)}) custom-call(f32[2,2,5,8,1024]{4,3,2,1,0:T(8,128)} %x_hbm.1, f32[2,2,5,8,1024]{4,3,2,1,0:T(8,128)} %f_hbm.1, f32[4,8,1024]{2,1,0:T(8,128)} %cpl_hbm.1, ...), custom_call_target="tpu_custom_call" | custom-call | flops 1048576 | bytes 1048576 | tf_op jit(solution)/shard_map/pack/pallas_call | solution.py:24
  2.3 3.8 %collective-permute-start.1 = (f32[66,1024]{1,0:T(8,128)S(1)}, f32[66,1024]{1,0:T(8,128)S(1)}, u32[]{:S(2)}, u32[]{:S(2)}) collective-permute-start(f32[66,1024]{1,0:T(8,128)S(1)} %get-tuple-element.53.down_ref), channel_id=1, source_target_pairs={{1,0},{2,1},{3,2},{4,3},{5,4},{6,5},{7,6},{8,7},{9,8},{10,9},{11,1... | collective-permute-start | bytes 811016 | tf_op jit(solution)/shard_map/ppermute | solution.py:540
  7.8 1.0 %tables.1 = (bf16[160,144]{1,0:T(8,128)(2,1)S(1)}, bf16[200,240]{1,0:T(8,128)(2,1)S(1)}, bf16[200,240]{1,0:T(8,128)(2,1)S(1)}, bf16[200,240]{1,0:T(8,128)(2,1)S(1)}) custom-call(f32[4,5,5]{2,1,0:T(8,128)S(1)} %copy.19.jac_ref, f32[8]{0:T(128)S(1)} %reshape.140.rot_ref), custom_call_target="tpu_custom_call" | custom-call | flops 1048576 | bytes 1048576 | tf_op jit(solution)/shard_map/tables/pallas_call | solution.py:24
  8.9 1.8 %pre.3 = (f32[2,2,5,8,1024]{4,3,2,1,0:T(8,128)S(1)}, f32[2,40,1024]{2,1,0:T(8,128)S(1)}, f32[2,5,8,1024]{3,2,1,0:T(8,128)S(1)}, f32[2,6,8,1024]{3,2,1,0:T(8,128)S(1)}) custom-call(f32[2,2,5,8,1024]{4,3,2,1,0:T(8,128)S(1)} %get-tuple-element.46.x_ref, f32[2,2,5,8,1024]{4,3,2,1,0:T(8,128)S(1)} %get-tuple-element.47.f_ref, ...), custom_call_target="tpu_custom_call" | custom-call | flops 41943040 | bytes 1048576 | tf_op jit(solution)/shard_map/pre/pallas_call | solution.py:24
  11.5 1.5 %post.3 = (f32[40,1024]{1,0:T(8,128)S(1)}, f32[40,1024]{1,0:T(8,128)S(1)}, f32[2,5,8,1024]{3,2,1,0:T(8,128)S(1)}, f32[2,6,8,1024]{3,2,1,0:T(8,128)S(1)}) custom-call(f32[8]{0:T(128)S(1)} %reshape.140.rot_ref, bf16[200,240]{1,0:T(8,128)(2,1)S(1)} %get-tuple-element.43.plain_ref, bf16[200,240]{1,0:T(8,128)(2,1)S(1)} %get-tuple-element.44.lo_turn_ref, ...), custom_call_target="tpu_custom_call" | custom-call | flops 20971520 | bytes 1048576 | tf_op jit(solution)/shard_map/post/pallas_call | solution.py:24
  13.1 1.0 %collective-permute-start.2 = (f32[40,1024]{1,0:T(8,128)S(1)}, f32[40,1024]{1,0:T(8,128)S(1)}, u32[]{:S(2)}, u32[]{:S(2)}) collective-permute-start(f32[40,1024]{1,0:T(8,128)S(1)} %get-tuple-element.55.refs_1_.up_ref), channel_id=1, source_target_pairs={{0,1},{1,2},{2,3},{3,4},{4,5},{5,6},{6,7},{7,8},{8,9},{9,10},{10,1... | collective-permute-start | bytes 491528 | tf_op jit(solution)/shard_map/ppermute | solution.py:539
  14.1 2.9 %collective-permute-start.3 = (f32[40,1024]{1,0:T(8,128)S(1)}, f32[40,1024]{1,0:T(8,128)S(1)}, u32[]{:S(2)}, u32[]{:S(2)}) collective-permute-start(f32[40,1024]{1,0:T(8,128)S(1)} %get-tuple-element.56.refs_0_.down_ref), channel_id=1, source_target_pairs={{1,0},{2,1},{3,2},{4,3},{5,4},{6,5},{7,6},{8,7},{9,8},{10,9},{11,1... | collective-permute-start | bytes 491528 | tf_op jit(solution)/shard_map/ppermute | solution.py:540
  17.0 3.0 %onehot.1 = (bf16[16,256,512]{2,1,0:T(8,128)(2,1)S(1)}, f32[8,1024]{1,0:T(8,128)S(1)}) custom-call(s32[16,1,512]{2,1,0:T(1,128)S(1)} %bitcast.13, f32[16,1,512]{2,1,0:T(1,128)S(1)} %bitcast.18), custom_call_target="tpu_custom_call" | custom-call | flops 8388608 | bytes 1048576 | tf_op jit(solution)/shard_map/onehot/pallas_call | solution.py:24
  20.1 1.8 %pre.4 = (f32[2,2,5,8,1024]{4,3,2,1,0:T(8,128)S(1)}, f32[2,40,1024]{2,1,0:T(8,128)S(1)}) custom-call(f32[2,2,5,8,1024]{4,3,2,1,0:T(8,128)S(1)} %get-tuple-element.57.x_ref, f32[2,2,5,8,1024]{4,3,2,1,0:T(8,128)S(1)} %get-tuple-element.47.f_ref, f32[6,8,1024]{2,1,0:T(8,128)S(1)} %get-tuple-element.48.coef_ref, bf16[160,144]{1,0:T(8,128)(2,1)S(1)} %get-tuple-element.49.own_ref, ...), custom_call_target="tpu_custom_call" | custom-call | flops 41943040 | bytes 1048576 | tf_op jit(solution)/shard_map/pre/pallas_call | solution.py:24
  21.9 1.4 %post.4 = (f32[40,1024]{1,0:T(8,128)S(1)}, f32[40,1024]{1,0:T(8,128)S(1)}) custom-call(f32[8]{0:T(128)S(1)} %reshape.140.rot_ref, bf16[200,240]{1,0:T(8,128)(2,1)S(1)} %get-tuple-element.43.plain_ref, bf16[200,240]{1,0:T(8,128)(2,1)S(1)} %get-tuple-element.44.lo_turn_ref, bf16[200,240]{1,0:T(8,128)(2,1)S(1)} %get-tuple-element.45.hi_turn_ref, ...), custom_call_target="tpu_custom_call" | custom-call | flops 20971520 | bytes 1048576 | tf_op jit(solution)/shard_map/post/pallas_call | solution.py:24
  23.4 3.8 %collective-permute-start.5 = (f32[40,1024]{1,0:T(8,128)S(1)}, f32[40,1024]{1,0:T(8,128)S(1)}, u32[]{:S(2)}, u32[]{:S(2)}) collective-permute-start(f32[40,1024]{1,0:T(8,128)S(1)} %get-tuple-element.65.refs_0_.down_ref), channel_id=1, source_target_pairs={{1,0},{2,1},{3,2},{4,3},{5,4},{6,5},{7,6},{8,7},{9,8},{10,9},{11,1... | collective-permute-start | bytes 491528 | tf_op jit(solution)/shard_map/ppermute | solution.py:540
  27.3 1.8 %pre.5 = (f32[2,2,5,8,1024]{4,3,2,1,0:T(8,128)S(1)}, f32[2,40,1024]{2,1,0:T(8,128)S(1)}) custom-call(f32[2,2,5,8,1024]{4,3,2,1,0:T(8,128)S(1)} %get-tuple-element.66.x_ref, f32[2,2,5,8,1024]{4,3,2,1,0:T(8,128)S(1)} %get-tuple-element.47.f_ref, f32[6,8,1024]{2,1,0:T(8,128)S(1)} %get-tuple-element.48.coef_ref, bf16[160,144]{1,0:T(8,128)(2,1)S(1)} %get-tuple-element.49.own_ref, ...), custom_call_target="tpu_custom_call" | custom-call | flops 41943040 | bytes 1048576 | tf_op jit(solution)/shard_map/pre/pallas_call | solution.py:24
  29.1 2.0 %inner.1 = (f32[16,4,512]{2,1,0:T(4,128)S(1)}, f32[4,128]{1,0:T(4,128)S(1)}) custom-call(f32[5]{0:T(128)S(1)} %copy-done.2, f32[2,2,5,8,1024]{4,3,2,1,0:T(8,128)S(1)} %get-tuple-element.69.x_ref, s32[16,1,512]{2,1,0:T(1,128)S(1)} %bitcast.14, bf16[16,256,512]{2,1,0:T(8,128)(2,1)S(1)} %get-tuple-element.70.hot_ref, ...), custom_call_target="tpu_custom_call" | custom-call | flops 20971520 | bytes 1048576 | tf_op jit(solution)/shard_map/inner/pallas_call | solution.py:24
  31.1 1.5 %post.5 = (f32[40,1024]{1,0:T(8,128)S(1)}, f32[40,1024]{1,0:T(8,128)S(1)}, f32[2,8,1024]{2,1,0:T(8,128)S(1)}, f32[4,128]{1,0:T(4,128)S(1)}) custom-call(f32[8]{0:T(128)S(1)} %reshape.140.rot_ref, bf16[200,240]{1,0:T(8,128)(2,1)S(1)} %get-tuple-element.43.plain_ref, bf16[200,240]{1,0:T(8,128)(2,1)S(1)} %get-tuple-element.44.lo_turn_ref, ...), custom_call_target="tpu_custom_call" | custom-call | flops 20971520 | bytes 1048576 | tf_op jit(solution)/shard_map/post/pallas_call | solution.py:24
  32.6 1.9 %surface.1 = f32[16,4,640]{2,1,0:T(4,128)} custom-call(f32[2,8,1024]{2,1,0:T(8,128)S(1)} %get-tuple-element.72.press_ref, s32[16,1,512]{2,1,0:T(1,128)S(1)} %bitcast.15, bf16[16,256,512]{2,1,0:T(8,128)(2,1)S(1)} %get-tuple-element.70.hot_ref, f32[16,4,512]{2,1,0:T(4,128)S(1)} %get-tuple-element.73.inner_ref, f32[4,128]{1,0:T(4,128)S(1)} %get-tuple-element.74.work_ref), custom_call_target="tpu_custom_call" | custom-call | flops 268435456 | bytes 1048576 | tf_op jit(solution)/shard_map/surface/pallas_call | solution.py:24
  34.6 11.3 %all-to-all-start = ((f32[16,4,640]{2,1,0:T(4,128)}), f32[16,4,640]{2,1,0:T(4,128)S(1)}, u32[]{:S(2)}, u32[]{:S(2)}) async-start(f32[16,4,640]{2,1,0:T(4,128)} %surface.1), calls=%async_computation | async-start | bytes 327680 | tf_op jit(solution)/shard_map/all_to_all | solution.py:601
  46.2 1.0 %merge.1 = f32[2,2,5,8,1024]{4,3,2,1,0:T(8,128)} custom-call(f32[2,2,5,8,1024]{4,3,2,1,0:T(8,128)S(1)} %get-tuple-element.69.x_ref, f32[40,1024]{1,0:T(8,128)S(1)} %get-tuple-element.75.down_ref, f32[40,1024]{1,0:T(8,128)S(1)} %get-tuple-element.76.up_ref), custom_call_target="tpu_custom_call" | custom-call | flops 1048576 | bytes 1048576 | tf_op jit(solution)/shard_map/merge/pallas_call | solution.py:24
  47.2 8.6 %all-to-all-done.x_ref = f32[16,4,640]{2,1,0:T(4,128)S(1)} async-done(((f32[16,4,640]{2,1,0:T(4,128)}), f32[16,4,640]{2,1,0:T(4,128)S(1)}, u32[]{:S(2)}, u32[]{:S(2)}) %all-to-all-start) | async-done | bytes 163872 | tf_op jit(solution)/shard_map/all_to_all | solution.py:601
  55.9 2.3 %collective-permute-start.7 = (f32[4,128]{1,0:T(4,128)S(1)}, f32[4,128]{1,0:T(4,128)S(1)}, u32[]{:S(2)}, u32[]{:S(2)}) collective-permute-start(f32[4,128]{1,0:T(4,128)S(1)} %work.1), channel_id=1, source_target_pairs={{0,8},{1,9},{2,10},{3,11},{4,12},{5,13},{6,14},{7,15},{8,0},{9,1},... | collective-permute-start | bytes 6152 | tf_op jit(solution)/shard_map/ppermute | solution.py:610
  58.2 2.4 %collective-permute-start.8 = (f32[4,128]{1,0:T(4,128)S(1)}, f32[4,128]{1,0:T(4,128)S(1)}, u32[]{:S(2)}, u32[]{:S(2)}) collective-permute-start(f32[4,128]{1,0:T(4,128)S(1)} %work.1), channel_id=1, source_target_pairs={{0,12},{1,13},{2,14},{3,15},{4,8},{5,9},{6,10},{7,11},{8,4},{9,5},... | collective-permute-start | bytes 6152 | tf_op jit(solution)/shard_map/ppermute | solution.py:610
  61.5 3.9 %all-to-all-start.1 = ((f32[16,4,512]{2,1,0:T(4,128)}), f32[16,4,512]{2,1,0:T(4,128)S(1)}, u32[]{:S(2)}, u32[]{:S(2)}) async-start(f32[16,4,512]{2,1,0:T(4,128)} %phases.1), calls=%async_computation.1 | async-start | bytes 262144 | tf_op jit(solution)/shard_map/all_to_all | solution.py:623
  65.6 2.0 %collective-permute-start.9 = (f32[4,128]{1,0:T(4,128)S(1)}, f32[4,128]{1,0:T(4,128)S(1)}, u32[]{:S(2)}, u32[]{:S(2)}) collective-permute-start(f32[4,128]{1,0:T(4,128)S(1)} %add_add_fusion.1), channel_id=1, source_target_pairs={{0,1},{1,0},{2,3},{3,2},{4,5},{5,4},{6,7},{7,6},{8,9},{9,8},{10,11... | collective-permute-start | bytes 6152 | tf_op jit(solution)/shard_map/ppermute | solution.py:610
  67.6 1.4 %collective-permute-done.10 = f32[4,128]{1,0:T(4,128)S(1)} collective-permute-done((f32[4,128]{1,0:T(4,128)S(1)}, f32[4,128]{1,0:T(4,128)S(1)}, u32[]{:S(2)}, u32[]{:S(2)}) %collective-permute-start.10) | collective-permute-done | bytes 2080 | tf_op jit(solution)/shard_map/ppermute | solution.py:610
  69.1 5.8 %all-to-all-done.1.x_ref = f32[16,4,512]{2,1,0:T(4,128)S(1)} async-done(((f32[16,4,512]{2,1,0:T(4,128)}), f32[16,4,512]{2,1,0:T(4,128)S(1)}, u32[]{:S(2)}, u32[]{:S(2)}) %all-to-all-start.1) | async-done | bytes 131104 | tf_op jit(solution)/shard_map/all_to_all | solution.py:623
  (41 shorter events, 5.1 us)
Async XLA Ops:
  0.6 16.4 %copy-start = (s32[8192]{0:T(1024)S(1)}, s32[8192]{0:T(1024)}, u32[]{:S(2)}) copy-start(s32[8192]{0:T(1024)} %param.17) | copy-start | bytes 98308
  0.6 16.4 %copy-start.1 = (f32[8192]{0:T(1024)S(1)}, f32[8192]{0:T(1024)}, u32[]{:S(2)}) copy-start(f32[8192]{0:T(1024)} %param.18) | copy-start | bytes 98308
  2.2 9.3 %collective-permute-start = (f32[66,1024]{1,0:T(8,128)S(1)}, f32[66,1024]{1,0:T(8,128)S(1)}, u32[]{:S(2)}, u32[]{:S(2)}) collective-permute-start(f32[66,1024]{1,0:T(8,128)S(1)} %get-tuple-element.52.up_ref), channel_id=1, source_target_pairs={{0,1},{1,2},{2,3},{3,4},{4,5},{5,6},{6,7},{7,8},{8,9},{9,10},{10,1... | collective-permute-start | bytes 811016 | tf_op jit(solution)/shard_map/ppermute | solution.py:539
  2.3 9.2 %collective-permute-start.1 = (f32[66,1024]{1,0:T(8,128)S(1)}, f32[66,1024]{1,0:T(8,128)S(1)}, u32[]{:S(2)}, u32[]{:S(2)}) collective-permute-start(f32[66,1024]{1,0:T(8,128)S(1)} %get-tuple-element.53.down_ref), channel_id=1, source_target_pairs={{1,0},{2,1},{3,2},{4,3},{5,4},{6,5},{7,6},{8,7},{9,8},{10,9},{11,1... | collective-permute-start | bytes 811016 | tf_op jit(solution)/shard_map/ppermute | solution.py:540
  8.9 18.4 %copy-start.3 = (s32[32]{0:T(128)S(1)}, s32[32]{0:T(128)}, u32[]{:S(2)}) copy-start(s32[32]{0:T(128)} %param.19) | copy-start | bytes 388
  11.5 17.6 %copy-start.2 = (f32[5]{0:T(128)S(1)}, f32[5]{0:T(128)}, u32[]{:S(2)}) copy-start(f32[5]{0:T(128)} %refs_4_.1) | copy-start | bytes 64
  13.1 8.8 %collective-permute-start.2 = (f32[40,1024]{1,0:T(8,128)S(1)}, f32[40,1024]{1,0:T(8,128)S(1)}, u32[]{:S(2)}, u32[]{:S(2)}) collective-permute-start(f32[40,1024]{1,0:T(8,128)S(1)} %get-tuple-element.55.refs_1_.up_ref), channel_id=1, source_target_pairs={{0,1},{1,2},{2,3},{3,4},{4,5},{5,6},{6,7},{7,8},{8,9},{9,10},{10,1... | collective-permute-start | bytes 491528 | tf_op jit(solution)/shard_map/ppermute | solution.py:539
  14.1 7.8 %collective-permute-start.3 = (f32[40,1024]{1,0:T(8,128)S(1)}, f32[40,1024]{1,0:T(8,128)S(1)}, u32[]{:S(2)}, u32[]{:S(2)}) collective-permute-start(f32[40,1024]{1,0:T(8,128)S(1)} %get-tuple-element.56.refs_0_.down_ref), channel_id=1, source_target_pairs={{1,0},{2,1},{3,2},{4,3},{5,4},{6,5},{7,6},{8,7},{9,8},{10,9},{11,1... | collective-permute-start | bytes 491528 | tf_op jit(solution)/shard_map/ppermute | solution.py:540
  23.3 7.8 %collective-permute-start.4 = (f32[40,1024]{1,0:T(8,128)S(1)}, f32[40,1024]{1,0:T(8,128)S(1)}, u32[]{:S(2)}, u32[]{:S(2)}) collective-permute-start(f32[40,1024]{1,0:T(8,128)S(1)} %get-tuple-element.64.refs_1_.up_ref), channel_id=1, source_target_pairs={{0,1},{1,2},{2,3},{3,4},{4,5},{5,6},{6,7},{7,8},{8,9},{9,10},{10,1... | collective-permute-start | bytes 491528 | tf_op jit(solution)/shard_map/ppermute | solution.py:539
  23.4 7.7 %collective-permute-start.5 = (f32[40,1024]{1,0:T(8,128)S(1)}, f32[40,1024]{1,0:T(8,128)S(1)}, u32[]{:S(2)}, u32[]{:S(2)}) collective-permute-start(f32[40,1024]{1,0:T(8,128)S(1)} %get-tuple-element.65.refs_0_.down_ref), channel_id=1, source_target_pairs={{1,0},{2,1},{3,2},{4,3},{5,4},{6,5},{7,6},{8,7},{9,8},{10,9},{11,1... | collective-permute-start | bytes 491528 | tf_op jit(solution)/shard_map/ppermute | solution.py:540
  34.6 21.2 %all-to-all-start = ((f32[16,4,640]{2,1,0:T(4,128)}), f32[16,4,640]{2,1,0:T(4,128)S(1)}, u32[]{:S(2)}, u32[]{:S(2)}) async-start(f32[16,4,640]{2,1,0:T(4,128)} %surface.1), calls=%async_computation | async-start | bytes 327680 | tf_op jit(solution)/shard_map/all_to_all | solution.py:601
  55.9 9.5 %collective-permute-start.6 = (f32[4,128]{1,0:T(4,128)S(1)}, f32[4,128]{1,0:T(4,128)S(1)}, u32[]{:S(2)}, u32[]{:S(2)}) collective-permute-start(f32[4,128]{1,0:T(4,128)S(1)} %work.1), channel_id=1, source_target_pairs={{0,4},{1,5},{2,6},{3,7},{4,0},{5,1},{6,2},{7,3},{8,12},{9,13},{10,... | collective-permute-start | bytes 6152 | tf_op jit(solution)/shard_map/ppermute | solution.py:610
  55.9 9.5 %collective-permute-start.7 = (f32[4,128]{1,0:T(4,128)S(1)}, f32[4,128]{1,0:T(4,128)S(1)}, u32[]{:S(2)}, u32[]{:S(2)}) collective-permute-start(f32[4,128]{1,0:T(4,128)S(1)} %work.1), channel_id=1, source_target_pairs={{0,8},{1,9},{2,10},{3,11},{4,12},{5,13},{6,14},{7,15},{8,0},{9,1},... | collective-permute-start | bytes 6152 | tf_op jit(solution)/shard_map/ppermute | solution.py:610
  58.2 7.2 %collective-permute-start.8 = (f32[4,128]{1,0:T(4,128)S(1)}, f32[4,128]{1,0:T(4,128)S(1)}, u32[]{:S(2)}, u32[]{:S(2)}) collective-permute-start(f32[4,128]{1,0:T(4,128)S(1)} %work.1), channel_id=1, source_target_pairs={{0,12},{1,13},{2,14},{3,15},{4,8},{5,9},{6,10},{7,11},{8,4},{9,5},... | collective-permute-start | bytes 6152 | tf_op jit(solution)/shard_map/ppermute | solution.py:610
  61.5 13.4 %all-to-all-start.1 = ((f32[16,4,512]{2,1,0:T(4,128)}), f32[16,4,512]{2,1,0:T(4,128)S(1)}, u32[]{:S(2)}, u32[]{:S(2)}) async-start(f32[16,4,512]{2,1,0:T(4,128)} %phases.1), calls=%async_computation.1 | async-start | bytes 262144 | tf_op jit(solution)/shard_map/all_to_all | solution.py:623
  65.4 3.7 %collective-permute-start.10 = (f32[4,128]{1,0:T(4,128)S(1)}, f32[4,128]{1,0:T(4,128)S(1)}, u32[]{:S(2)}, u32[]{:S(2)}) collective-permute-start(f32[4,128]{1,0:T(4,128)S(1)} %add_add_fusion.1), channel_id=1, source_target_pairs={{0,2},{1,3},{2,0},{3,1},{4,6},{5,7},{6,4},{7,5},{8,10},{9,11},{10,... | collective-permute-start | bytes 6152 | tf_op jit(solution)/shard_map/ppermute | solution.py:610
  65.5 3.6 %collective-permute-start.11 = (f32[4,128]{1,0:T(4,128)S(1)}, f32[4,128]{1,0:T(4,128)S(1)}, u32[]{:S(2)}, u32[]{:S(2)}) collective-permute-start(f32[4,128]{1,0:T(4,128)S(1)} %add_add_fusion.1), channel_id=1, source_target_pairs={{0,3},{1,2},{2,1},{3,0},{4,7},{5,6},{6,5},{7,4},{8,11},{9,10},{10,... | collective-permute-start | bytes 6152 | tf_op jit(solution)/shard_map/ppermute | solution.py:610
  65.6 3.5 %collective-permute-start.9 = (f32[4,128]{1,0:T(4,128)S(1)}, f32[4,128]{1,0:T(4,128)S(1)}, u32[]{:S(2)}, u32[]{:S(2)}) collective-permute-start(f32[4,128]{1,0:T(4,128)S(1)} %add_add_fusion.1), channel_id=1, source_target_pairs={{0,1},{1,0},{2,3},{3,2},{4,5},{5,4},{6,7},{7,6},{8,9},{9,8},{10,11... | collective-permute-start | bytes 6152 | tf_op jit(solution)/shard_map/ppermute | solution.py:610
where the time goes:
time: 76 us; the launch traced here: 75.6 us
  starting transfers between devices  33.9 us (45%)
  Pallas kernels  22 us (29%)
  waiting for transfers between devices  16.7 us (22%)
  local copies, waits for them, and re-layouts  1.15 us (2%)
  other arithmetic  0.9 us (1%)
  between operations  0.87 us (1%)
    pallas_call x15, Pallas kernels, call(): pl.pallas_call(kernel, name=name, out_shape=[jax.ShapeDtypeStruct(s, d) f...  22 us
    all_to_all x1, starting transfers between devices, per_device(): every = lax.all_to_all(mine, 'phase', 0, 0, tiled=True)  11.3 us
    ppermute x3, starting transfers between devices, per_device(): hi = lax.ppermute(down, 'space', backward)  10.6 us
    all_to_all x1, waiting for transfers between devices, per_device(): every = lax.all_to_all(mine, 'phase', 0, 0, tiled=True)  8.57 us
    ppermute x6, starting transfers between devices, across(): return lax.ppermute(work, 'space', [(i, i ^ bits) for i in range(count)])  6.92 us
    all_to_all x1, waiting for transfers between devices, per_device(): blocks = lax.all_to_all(turned, 'phase', 0, 0, tiled=True)  5.79 us
    all_to_all x1, starting transfers between devices, per_device(): blocks = lax.all_to_all(turned, 'phase', 0, 0, tiled=True)  3.88 us
  transfers between devices with their start and end apart: 14, of which 4 were waited for; matrix products, arithmetic and copies ran while one was open for 3% of the time, Pallas kernels for 17%

commit v1 on v0

--- a/solution.py
+++ b/solution.py
@@ -164,7 +164,7 @@
         )
         return 0
 
-    lax.fori_loop(0, hot_ref.shape[0], one, 0, unroll=2)
+    lax.fori_loop(0, hot_ref.shape[0], one, 0, unroll=4)
     for g in range(groups):
         total = sum_ref[8 * g : 8 * g + 8, :]
         for i in range(1, 3):
@@ -373,7 +373,7 @@
         out_ref[d] = jnp.concatenate(res, axis=0)
         return 0
 
-    lax.fori_loop(0, parts, one, 0, unroll=4)
+    lax.fori_loop(0, parts, one, 0, unroll=16)
 
 
 def surface_kernel(press_ref, idx_ref, hot_ref, inner_ref, work_ref, out_ref):
@@ -405,7 +405,7 @@
         out_ref[d, :, chunk : chunk + LANES] = work_ref[...]
         return 0
 
-    lax.fori_loop(0, parts, one, 0, unroll=4)
+    lax.fori_loop(0, parts, one, 0, unroll=16)
 
 
 def merge_kernel(x_ref, down_ref, up_ref, out_ref):
@@ -421,16 +421,21 @@
 def work_kernel(table_ref, x_ref, work_ref):
     chunk = x_ref.shape[-1] - LANES
     rows = jnp.concatenate([x_ref[d, :, chunk:] for d in range(x_ref.shape[0])], axis=0)
-    work_ref[...] = jnp.dot(
+    work = jnp.dot(
         table_ref[...], rows, precision=HIGHEST, preferred_element_type=jnp.float32
     )
+    for i in range(work_ref.shape[1] // LANES):
+        work_ref[:, i * LANES : (i + 1) * LANES] = work
 
 
 def phase_kernel(table_ref, x_ref, out_ref):
     parts = x_ref.shape[0]
     chunk = out_ref.shape[-1]
+    table = table_ref[...]
+    high = table.astype(jnp.bfloat16).astype(jnp.float32)
+    table = jnp.concatenate([high, high, table - high], axis=1).astype(jnp.bfloat16)
     rows = jnp.concatenate([x_ref[d, :, 0:chunk] for d in range(parts)], axis=0)
-    y = jnp.dot(table_ref[...], rows, precision=HIGHEST, preferred_element_type=jnp.float32)
+    y = multiply(table, rows)
     for d in range(parts):
         out_ref[d] = y[4 * d : 4 * d + 4]
 
@@ -602,14 +607,15 @@
     every, state = lax.optimization_barrier((every, state))
     own_table = lax.dynamic_slice_in_dim(table, lax.axis_index("phase") * 4, 4)
     (work,) = call(
-        work_kernel, "work", [((4, LANES), f32)], [], 1 << 16, [own_table, every], [VMEM] * 2
+        work_kernel, "work", [((4, 2048), f32)], [], 1 << 16, [own_table, every], [VMEM] * 2
     )
     work, ready = lax.optimization_barrier((work, every))
 
     def across(bits):
         return lax.ppermute(work, "space", [(i, i ^ bits) for i in range(count)])
 
-    work = (work + across(4)) + (across(8) + across(12))
+    work = (work + across(8))[:, :LANES]
+    work = work + across(4)
     work = (work + across(1)) + (across(2) + across(3))
     (turned,) = call(
         phase_kernel,

time: 76 us -> 71.9 us (0.946)
  the two profiles are of different devices: /device:TPU:32 before, /device:TPU:1 now
where the time goes in v1:
time: 71.9 us; the launch traced here: 71 us
  starting transfers between devices  31.7 us (44%)
  Pallas kernels  20.3 us (28%)
  waiting for transfers between devices  16.1 us (22%)
  local copies, waits for them, and re-layouts  1.15 us (2%)
  other arithmetic  0.9 us (1%)
  between operations  0.87 us (1%)
    pallas_call x15, Pallas kernels, call(): pl.pallas_call(kernel, name=name, out_shape=[jax.ShapeDtypeStruct(s, d) f...  20.3 us
    all_to_all x1, starting transfers between devices, per_device(): every = lax.all_to_all(mine, 'phase', 0, 0, tiled=True)  8.43 us
    ppermute x5, starting transfers between devices, across(): return lax.ppermute(work, 'space', [(i, i ^ bits) for i in range(count)])  7.83 us
    ppermute x3, starting transfers between devices, per_device(): hi = lax.ppermute(down, 'space', backward)  7.76 us
    all_to_all x1, waiting for transfers between devices, per_device(): every = lax.all_to_all(mine, 'phase', 0, 0, tiled=True)  7.7 us
    all_to_all x1, starting transfers between devices, per_device(): blocks = lax.all_to_all(turned, 'phase', 0, 0, tiled=True)  4.79 us
    ppermute x5, waiting for transfers between devices, across(): return lax.ppermute(work, 'space', [(i, i ^ bits) for i in range(count)])  3.82 us
    ppermute x3, waiting for transfers between devices, per_device(): hi = lax.ppermute(down, 'space', backward)  3.61 us
  transfers between devices with their start and end apart: 13, of which 5 were waited for; matrix products, arithmetic and copies ran while one was open for 3% of the time, Pallas kernels for 17%

profile of v1, /device:TPU:1, one launch (start us, length us, event | category | flops | bytes accessed | tf_op | source)
XLA Modules:
  0.0 71.0 jit_solution(18070526198333195943)
XLA Ops:
  0.7 1.6 %pack.1 = (f32[6,8,1024]{2,1,0:T(8,128)S(1)}, f32[66,1024]{1,0:T(8,128)S(1)}, f32[66,1024]{1,0:T(8,128)S(1)}, f32[2,2,5,8,1024]{4,3,2,1,0:T(8,128)S(1)}, f32[2,2,5,8,1024]{4,3,2,1,0:T(8,128)S(1)}) custom-call(f32[2,2,5,8,1024]{4,3,2,1,0:T(8,128)} %x_hbm.1, f32[2,2,5,8,1024]{4,3,2,1,0:T(8,128)} %f_hbm.1, f32[4,8,1024]{2,1,0:T(8,128)} %cpl_hbm.1, ...), custom_call_target="tpu_custom_call" | custom-call | flops 1048576 | bytes 1048576 | tf_op jit(solution)/shard_map/pack/pallas_call | solution.py:24
  2.2 2.7 %collective-permute-start = (f32[66,1024]{1,0:T(8,128)S(1)}, f32[66,1024]{1,0:T(8,128)S(1)}, u32[]{:S(2)}, u32[]{:S(2)}) collective-permute-start(f32[66,1024]{1,0:T(8,128)S(1)} %get-tuple-element.52.up_ref), channel_id=1, source_target_pairs={{0,1},{1,2},{2,3},{3,4},{4,5},{5,6},{6,7},{7,8},{8,9},{9,10},{10,1... | collective-permute-start | bytes 811016 | tf_op jit(solution)/shard_map/ppermute | solution.py:544
  7.3 1.0 %tables.1 = (bf16[160,144]{1,0:T(8,128)(2,1)S(1)}, bf16[200,240]{1,0:T(8,128)(2,1)S(1)}, bf16[200,240]{1,0:T(8,128)(2,1)S(1)}, bf16[200,240]{1,0:T(8,128)(2,1)S(1)}) custom-call(f32[4,5,5]{2,1,0:T(8,128)S(1)} %copy.19.jac_ref, f32[8]{0:T(128)S(1)} %reshape.140.rot_ref), custom_call_target="tpu_custom_call" | custom-call | flops 1048576 | bytes 1048576 | tf_op jit(solution)/shard_map/tables/pallas_call | solution.py:24
  8.4 1.8 %pre.3 = (f32[2,2,5,8,1024]{4,3,2,1,0:T(8,128)S(1)}, f32[2,40,1024]{2,1,0:T(8,128)S(1)}, f32[2,5,8,1024]{3,2,1,0:T(8,128)S(1)}, f32[2,6,8,1024]{3,2,1,0:T(8,128)S(1)}) custom-call(f32[2,2,5,8,1024]{4,3,2,1,0:T(8,128)S(1)} %get-tuple-element.46.x_ref, f32[2,2,5,8,1024]{4,3,2,1,0:T(8,128)S(1)} %get-tuple-element.47.f_ref, ...), custom_call_target="tpu_custom_call" | custom-call | flops 41943040 | bytes 1048576 | tf_op jit(solution)/shard_map/pre/pallas_call | solution.py:24
  10.1 3.6 %collective-permute-done.1.hi_ref = f32[66,1024]{1,0:T(8,128)S(1)} collective-permute-done((f32[66,1024]{1,0:T(8,128)S(1)}, f32[66,1024]{1,0:T(8,128)S(1)}, u32[]{:S(2)}, u32[]{:S(2)}) %collective-permute-start.1) | collective-permute-done | bytes 270368 | tf_op jit(solution)/shard_map/ppermute | solution.py:545
  13.7 1.5 %post.3 = (f32[40,1024]{1,0:T(8,128)S(1)}, f32[40,1024]{1,0:T(8,128)S(1)}, f32[2,5,8,1024]{3,2,1,0:T(8,128)S(1)}, f32[2,6,8,1024]{3,2,1,0:T(8,128)S(1)}) custom-call(f32[8]{0:T(128)S(1)} %reshape.140.rot_ref, bf16[200,240]{1,0:T(8,128)(2,1)S(1)} %get-tuple-element.43.plain_ref, bf16[200,240]{1,0:T(8,128)(2,1)S(1)} %get-tuple-element.44.lo_turn_ref, ...), custom_call_target="tpu_custom_call" | custom-call | flops 20971520 | bytes 1048576 | tf_op jit(solution)/shard_map/post/pallas_call | solution.py:24
  15.4 3.0 %collective-permute-start.3 = (f32[40,1024]{1,0:T(8,128)S(1)}, f32[40,1024]{1,0:T(8,128)S(1)}, u32[]{:S(2)}, u32[]{:S(2)}) collective-permute-start(f32[40,1024]{1,0:T(8,128)S(1)} %get-tuple-element.56.refs_0_.down_ref), channel_id=1, source_target_pairs={{1,0},{2,1},{3,2},{4,3},{5,4},{6,5},{7,6},{8,7},{9,8},{10,9},{11,1... | collective-permute-start | bytes 491528 | tf_op jit(solution)/shard_map/ppermute | solution.py:545
  18.4 2.6 %onehot.1 = (bf16[16,256,512]{2,1,0:T(8,128)(2,1)S(1)}, f32[8,1024]{1,0:T(8,128)S(1)}) custom-call(s32[16,1,512]{2,1,0:T(1,128)S(1)} %bitcast.13, f32[16,1,512]{2,1,0:T(1,128)S(1)} %bitcast.18), custom_call_target="tpu_custom_call" | custom-call | flops 8388608 | bytes 1048576 | tf_op jit(solution)/shard_map/onehot/pallas_call | solution.py:24
  21.0 1.8 %pre.4 = (f32[2,2,5,8,1024]{4,3,2,1,0:T(8,128)S(1)}, f32[2,40,1024]{2,1,0:T(8,128)S(1)}) custom-call(f32[2,2,5,8,1024]{4,3,2,1,0:T(8,128)S(1)} %get-tuple-element.57.x_ref, f32[2,2,5,8,1024]{4,3,2,1,0:T(8,128)S(1)} %get-tuple-element.47.f_ref, f32[6,8,1024]{2,1,0:T(8,128)S(1)} %get-tuple-element.48.coef_ref, bf16[160,144]{1,0:T(8,128)(2,1)S(1)} %get-tuple-element.49.own_ref, ...), custom_call_target="tpu_custom_call" | custom-call | flops 41943040 | bytes 1048576 | tf_op jit(solution)/shard_map/pre/pallas_call | solution.py:24
  22.8 1.4 %post.4 = (f32[40,1024]{1,0:T(8,128)S(1)}, f32[40,1024]{1,0:T(8,128)S(1)}) custom-call(f32[8]{0:T(128)S(1)} %reshape.140.rot_ref, bf16[200,240]{1,0:T(8,128)(2,1)S(1)} %get-tuple-element.43.plain_ref, bf16[200,240]{1,0:T(8,128)(2,1)S(1)} %get-tuple-element.44.lo_turn_ref, bf16[200,240]{1,0:T(8,128)(2,1)S(1)} %get-tuple-element.45.hi_turn_ref, ...), custom_call_target="tpu_custom_call" | custom-call | flops 20971520 | bytes 1048576 | tf_op jit(solution)/shard_map/post/pallas_call | solution.py:24
  24.3 4.0 %collective-permute-start.5 = (f32[40,1024]{1,0:T(8,128)S(1)}, f32[40,1024]{1,0:T(8,128)S(1)}, u32[]{:S(2)}, u32[]{:S(2)}) collective-permute-start(f32[40,1024]{1,0:T(8,128)S(1)} %get-tuple-element.65.refs_0_.down_ref), channel_id=1, source_target_pairs={{1,0},{2,1},{3,2},{4,3},{5,4},{6,5},{7,6},{8,7},{9,8},{10,9},{11,1... | collective-permute-start | bytes 491528 | tf_op jit(solution)/shard_map/ppermute | solution.py:545
  28.4 1.8 %pre.5 = (f32[2,2,5,8,1024]{4,3,2,1,0:T(8,128)S(1)}, f32[2,40,1024]{2,1,0:T(8,128)S(1)}) custom-call(f32[2,2,5,8,1024]{4,3,2,1,0:T(8,128)S(1)} %get-tuple-element.66.x_ref, f32[2,2,5,8,1024]{4,3,2,1,0:T(8,128)S(1)} %get-tuple-element.47.f_ref, f32[6,8,1024]{2,1,0:T(8,128)S(1)} %get-tuple-element.48.coef_ref, bf16[160,144]{1,0:T(8,128)(2,1)S(1)} %get-tuple-element.49.own_ref, ...), custom_call_target="tpu_custom_call" | custom-call | flops 41943040 | bytes 1048576 | tf_op jit(solution)/shard_map/pre/pallas_call | solution.py:24
  30.2 1.3 %inner.1 = (f32[16,4,512]{2,1,0:T(4,128)S(1)}, f32[4,128]{1,0:T(4,128)S(1)}) custom-call(f32[5]{0:T(128)S(1)} %copy-done.2, f32[2,2,5,8,1024]{4,3,2,1,0:T(8,128)S(1)} %get-tuple-element.69.x_ref, s32[16,1,512]{2,1,0:T(1,128)S(1)} %bitcast.14, bf16[16,256,512]{2,1,0:T(8,128)(2,1)S(1)} %get-tuple-element.70.hot_ref, ...), custom_call_target="tpu_custom_call" | custom-call | flops 20971520 | bytes 1048576 | tf_op jit(solution)/shard_map/inner/pallas_call | solution.py:24
  31.5 1.5 %post.5 = (f32[40,1024]{1,0:T(8,128)S(1)}, f32[40,1024]{1,0:T(8,128)S(1)}, f32[2,8,1024]{2,1,0:T(8,128)S(1)}, f32[4,128]{1,0:T(4,128)S(1)}) custom-call(f32[8]{0:T(128)S(1)} %reshape.140.rot_ref, bf16[200,240]{1,0:T(8,128)(2,1)S(1)} %get-tuple-element.43.plain_ref, bf16[200,240]{1,0:T(8,128)(2,1)S(1)} %get-tuple-element.44.lo_turn_ref, ...), custom_call_target="tpu_custom_call" | custom-call | flops 20971520 | bytes 1048576 | tf_op jit(solution)/shard_map/post/pallas_call | solution.py:24
  33.1 1.4 %surface.1 = f32[16,4,640]{2,1,0:T(4,128)} custom-call(f32[2,8,1024]{2,1,0:T(8,128)S(1)} %get-tuple-element.72.press_ref, s32[16,1,512]{2,1,0:T(1,128)S(1)} %bitcast.15, bf16[16,256,512]{2,1,0:T(8,128)(2,1)S(1)} %get-tuple-element.70.hot_ref, f32[16,4,512]{2,1,0:T(4,128)S(1)} %get-tuple-element.73.inner_ref, f32[4,128]{1,0:T(4,128)S(1)} %get-tuple-element.74.work_ref), custom_call_target="tpu_custom_call" | custom-call | flops 268435456 | bytes 1048576 | tf_op jit(solution)/shard_map/surface/pallas_call | solution.py:24
  34.5 8.4 %all-to-all-start = ((f32[16,4,640]{2,1,0:T(4,128)}), f32[16,4,640]{2,1,0:T(4,128)S(1)}, u32[]{:S(2)}, u32[]{:S(2)}) async-start(f32[16,4,640]{2,1,0:T(4,128)} %surface.1), calls=%async_computation | async-start | bytes 327680 | tf_op jit(solution)/shard_map/all_to_all | solution.py:606
  43.2 1.0 %merge.1 = f32[2,2,5,8,1024]{4,3,2,1,0:T(8,128)} custom-call(f32[2,2,5,8,1024]{4,3,2,1,0:T(8,128)S(1)} %get-tuple-element.69.x_ref, f32[40,1024]{1,0:T(8,128)S(1)} %get-tuple-element.75.down_ref, f32[40,1024]{1,0:T(8,128)S(1)} %get-tuple-element.76.up_ref), custom_call_target="tpu_custom_call" | custom-call | flops 1048576 | bytes 1048576 | tf_op jit(solution)/shard_map/merge/pallas_call | solution.py:24
  44.2 7.7 %all-to-all-done.x_ref = f32[16,4,640]{2,1,0:T(4,128)S(1)} async-done(((f32[16,4,640]{2,1,0:T(4,128)}), f32[16,4,640]{2,1,0:T(4,128)S(1)}, u32[]{:S(2)}, u32[]{:S(2)}) %all-to-all-start) | async-done | bytes 163872 | tf_op jit(solution)/shard_map/all_to_all | solution.py:606
  52.0 3.7 %collective-permute-start.6 = (f32[4,2048]{1,0:T(4,128)S(1)}, f32[4,2048]{1,0:T(4,128)S(1)}, u32[]{:S(2)}, u32[]{:S(2)}) collective-permute-start(f32[4,2048]{1,0:T(4,128)S(1)} %work.1), channel_id=1, source_target_pairs={{0,8},{1,9},{2,10},{3,11},{4,12},{5,13},{6,14},{7,15},{8,0},{9,1},... | collective-permute-start | bytes 98312 | tf_op jit(solution)/shard_map/ppermute | solution.py:615
  56.6 4.8 %all-to-all-start.1 = ((f32[16,4,512]{2,1,0:T(4,128)}), f32[16,4,512]{2,1,0:T(4,128)S(1)}, u32[]{:S(2)}, u32[]{:S(2)}) async-start(f32[16,4,512]{2,1,0:T(4,128)} %phases.1), calls=%async_computation.1 | async-start | bytes 262144 | tf_op jit(solution)/shard_map/all_to_all | solution.py:629
  61.5 2.4 %collective-permute-done.7 = f32[4,128]{1,0:T(4,128)S(1)} collective-permute-done((f32[4,128]{1,0:T(4,128)S(1)}, f32[4,128]{1,0:T(4,128)S(1)}, u32[]{:S(2)}, u32[]{:S(2)}) %collective-permute-start.7) | collective-permute-done | bytes 2080 | tf_op jit(solution)/shard_map/ppermute | solution.py:615
  63.9 1.9 %collective-permute-start.10 = (f32[4,128]{1,0:T(4,128)S(1)}, f32[4,128]{1,0:T(4,128)S(1)}, u32[]{:S(2)}, u32[]{:S(2)}) collective-permute-start(f32[4,128]{1,0:T(4,128)S(1)} %add.46), channel_id=1, source_target_pairs={{0,3},{1,2},{2,1},{3,0},{4,7},{5,6},{6,5},{7,4},{8,11},{9,10},{10,... | collective-permute-start | bytes 6152 | tf_op jit(solution)/shard_map/ppermute | solution.py:615
  66.6 1.4 %collective-permute-start.9 = (f32[4,128]{1,0:T(4,128)S(1)}, f32[4,128]{1,0:T(4,128)S(1)}, u32[]{:S(2)}, u32[]{:S(2)}) collective-permute-start(f32[4,128]{1,0:T(4,128)S(1)} %add.46), channel_id=1, source_target_pairs={{0,2},{1,3},{2,0},{3,1},{4,6},{5,7},{6,4},{7,5},{8,10},{9,11},{10,... | collective-permute-start | bytes 6152 | tf_op jit(solution)/shard_map/ppermute | solution.py:615
  68.0 1.4 %collective-permute-done.9 = f32[4,128]{1,0:T(4,128)S(1)} collective-permute-done((f32[4,128]{1,0:T(4,128)S(1)}, f32[4,128]{1,0:T(4,128)S(1)}, u32[]{:S(2)}, u32[]{:S(2)}) %collective-permute-start.9) | collective-permute-done | bytes 2080 | tf_op jit(solution)/shard_map/ppermute | solution.py:615
  (40 shorter events, 6.5 us)
Async XLA Ops:
  0.6 17.7 %copy-start = (s32[8192]{0:T(1024)S(1)}, s32[8192]{0:T(1024)}, u32[]{:S(2)}) copy-start(s32[8192]{0:T(1024)} %param.17) | copy-start | bytes 98308
  0.6 17.7 %copy-start.1 = (f32[8192]{0:T(1024)S(1)}, f32[8192]{0:T(1024)}, u32[]{:S(2)}) copy-start(f32[8192]{0:T(1024)} %param.18) | copy-start | bytes 98308
  2.2 7.9 %collective-permute-start = (f32[66,1024]{1,0:T(8,128)S(1)}, f32[66,1024]{1,0:T(8,128)S(1)}, u32[]{:S(2)}, u32[]{:S(2)}) collective-permute-start(f32[66,1024]{1,0:T(8,128)S(1)} %get-tuple-element.52.up_ref), channel_id=1, source_target_pairs={{0,1},{1,2},{2,3},{3,4},{4,5},{5,6},{6,7},{7,8},{8,9},{9,10},{10,1... | collective-permute-start | bytes 811016 | tf_op jit(solution)/shard_map/ppermute | solution.py:544
  4.9 8.8 %collective-permute-start.1 = (f32[66,1024]{1,0:T(8,128)S(1)}, f32[66,1024]{1,0:T(8,128)S(1)}, u32[]{:S(2)}, u32[]{:S(2)}) collective-permute-start(f32[66,1024]{1,0:T(8,128)S(1)} %get-tuple-element.53.down_ref), channel_id=1, source_target_pairs={{1,0},{2,1},{3,2},{4,3},{5,4},{6,5},{7,6},{8,7},{9,8},{10,9},{11,1... | collective-permute-start | bytes 811016 | tf_op jit(solution)/shard_map/ppermute | solution.py:545
  8.4 20.0 %copy-start.3 = (s32[32]{0:T(128)S(1)}, s32[32]{0:T(128)}, u32[]{:S(2)}) copy-start(s32[32]{0:T(128)} %param.19) | copy-start | bytes 388
  13.7 16.5 %copy-start.2 = (f32[5]{0:T(128)S(1)}, f32[5]{0:T(128)}, u32[]{:S(2)}) copy-start(f32[5]{0:T(128)} %refs_4_.1) | copy-start | bytes 64
  15.3 7.5 %collective-permute-start.2 = (f32[40,1024]{1,0:T(8,128)S(1)}, f32[40,1024]{1,0:T(8,128)S(1)}, u32[]{:S(2)}, u32[]{:S(2)}) collective-permute-start(f32[40,1024]{1,0:T(8,128)S(1)} %get-tuple-element.55.refs_1_.up_ref), channel_id=1, source_target_pairs={{0,1},{1,2},{2,3},{3,4},{4,5},{5,6},{6,7},{7,8},{8,9},{9,10},{10,1... | collective-permute-start | bytes 491528 | tf_op jit(solution)/shard_map/ppermute | solution.py:544
  15.4 7.4 %collective-permute-start.3 = (f32[40,1024]{1,0:T(8,128)S(1)}, f32[40,1024]{1,0:T(8,128)S(1)}, u32[]{:S(2)}, u32[]{:S(2)}) collective-permute-start(f32[40,1024]{1,0:T(8,128)S(1)} %get-tuple-element.56.refs_0_.down_ref), channel_id=1, source_target_pairs={{1,0},{2,1},{3,2},{4,3},{5,4},{6,5},{7,6},{8,7},{9,8},{10,9},{11,1... | collective-permute-start | bytes 491528 | tf_op jit(solution)/shard_map/ppermute | solution.py:545
  24.2 7.3 %collective-permute-start.4 = (f32[40,1024]{1,0:T(8,128)S(1)}, f32[40,1024]{1,0:T(8,128)S(1)}, u32[]{:S(2)}, u32[]{:S(2)}) collective-permute-start(f32[40,1024]{1,0:T(8,128)S(1)} %get-tuple-element.64.refs_1_.up_ref), channel_id=1, source_target_pairs={{0,1},{1,2},{2,3},{3,4},{4,5},{5,6},{6,7},{7,8},{8,9},{9,10},{10,1... | collective-permute-start | bytes 491528 | tf_op jit(solution)/shard_map/ppermute | solution.py:544
  24.3 7.2 %collective-permute-start.5 = (f32[40,1024]{1,0:T(8,128)S(1)}, f32[40,1024]{1,0:T(8,128)S(1)}, u32[]{:S(2)}, u32[]{:S(2)}) collective-permute-start(f32[40,1024]{1,0:T(8,128)S(1)} %get-tuple-element.65.refs_0_.down_ref), channel_id=1, source_target_pairs={{1,0},{2,1},{3,2},{4,3},{5,4},{6,5},{7,6},{8,7},{9,8},{10,9},{11,1... | collective-permute-start | bytes 491528 | tf_op jit(solution)/shard_map/ppermute | solution.py:545
  34.5 17.4 %all-to-all-start = ((f32[16,4,640]{2,1,0:T(4,128)}), f32[16,4,640]{2,1,0:T(4,128)S(1)}, u32[]{:S(2)}, u32[]{:S(2)}) async-start(f32[16,4,640]{2,1,0:T(4,128)} %surface.1), calls=%async_computation | async-start | bytes 327680 | tf_op jit(solution)/shard_map/all_to_all | solution.py:606
  52.0 9.4 %collective-permute-start.6 = (f32[4,2048]{1,0:T(4,128)S(1)}, f32[4,2048]{1,0:T(4,128)S(1)}, u32[]{:S(2)}, u32[]{:S(2)}) collective-permute-start(f32[4,2048]{1,0:T(4,128)S(1)} %work.1), channel_id=1, source_target_pairs={{0,8},{1,9},{2,10},{3,11},{4,12},{5,13},{6,14},{7,15},{8,0},{9,1},... | collective-permute-start | bytes 98312 | tf_op jit(solution)/shard_map/ppermute | solution.py:615
  56.6 13.7 %all-to-all-start.1 = ((f32[16,4,512]{2,1,0:T(4,128)}), f32[16,4,512]{2,1,0:T(4,128)S(1)}, u32[]{:S(2)}, u32[]{:S(2)}) async-start(f32[16,4,512]{2,1,0:T(4,128)} %phases.1), calls=%async_computation.1 | async-start | bytes 262144 | tf_op jit(solution)/shard_map/all_to_all | solution.py:629
  61.4 2.5 %collective-permute-start.7 = (f32[4,128]{1,0:T(4,128)S(1)}, f32[4,128]{1,0:T(4,128)S(1)}, u32[]{:S(2)}, u32[]{:S(2)}) collective-permute-start(f32[4,128]{1,0:T(4,128)S(1)} %slice_add_fusion), channel_id=1, source_target_pairs={{0,4},{1,5},{2,6},{3,7},{4,0},{5,1},{6,2},{7,3},{8,12},{9,13},{10,... | collective-permute-start | bytes 6152 | tf_op jit(solution)/shard_map/ppermute | solution.py:615
  63.9 4.0 %collective-permute-start.10 = (f32[4,128]{1,0:T(4,128)S(1)}, f32[4,128]{1,0:T(4,128)S(1)}, u32[]{:S(2)}, u32[]{:S(2)}) collective-permute-start(f32[4,128]{1,0:T(4,128)S(1)} %add.46), channel_id=1, source_target_pairs={{0,3},{1,2},{2,1},{3,0},{4,7},{5,6},{6,5},{7,4},{8,11},{9,10},{10,... | collective-permute-start | bytes 6152 | tf_op jit(solution)/shard_map/ppermute | solution.py:615
  65.8 2.1 %collective-permute-start.8 = (f32[4,128]{1,0:T(4,128)S(1)}, f32[4,128]{1,0:T(4,128)S(1)}, u32[]{:S(2)}, u32[]{:S(2)}) collective-permute-start(f32[4,128]{1,0:T(4,128)S(1)} %add.46), channel_id=1, source_target_pairs={{0,1},{1,0},{2,3},{3,2},{4,5},{5,4},{6,7},{7,6},{8,9},{9,8},{10,11... | collective-permute-start | bytes 6152 | tf_op jit(solution)/shard_map/ppermute | solution.py:615
  66.6 2.8 %collective-permute-start.9 = (f32[4,128]{1,0:T(4,128)S(1)}, f32[4,128]{1,0:T(4,128)S(1)}, u32[]{:S(2)}, u32[]{:S(2)}) collective-permute-start(f32[4,128]{1,0:T(4,128)S(1)} %add.46), channel_id=1, source_target_pairs={{0,2},{1,3},{2,0},{3,1},{4,6},{5,7},{6,4},{7,5},{8,10},{9,11},{10,... | collective-permute-start | bytes 6152 | tf_op jit(solution)/shard_map/ppermute | solution.py:615

commit v2 on v1

--- a/solution.py
+++ b/solution.py
@@ -36,31 +36,33 @@
 
 
 def pack_kernel(
-    x_hbm, f_hbm, cpl_hbm, diag_hbm, inert_hbm, coef_ref, up_ref, down_ref, x_ref, f_ref, diag_ref, inert_ref, sems
+    x_hbm, f_hbm, cpl_hbm, diag_hbm, inert_hbm, coef_ref, up_ref, down_ref, diag_ref, inert_ref, xe_ref, fe_ref, sems
 ):
-    copies = [
+    edges = [
+        pltpu.make_async_copy(x_hbm.at[:, :, :, 6 * h : 6 * h + 2], xe_ref.at[h], sems.at[h])
+        for h in range(2)
+    ]
+    coefs = [
         pltpu.make_async_copy(src, dst, sems.at[i])
         for i, (src, dst) in enumerate(
-            [(x_hbm.at[p, c], x_ref.at[p, c]) for p in range(2) for c in range(2)]
-            + [
-                (diag_hbm, diag_ref),
-                (inert_hbm, inert_ref),
-                (cpl_hbm, coef_ref.at[0:4]),
-            ]
-            + [(f_hbm.at[p, c], f_ref.at[p, c]) for p in range(2) for c in range(2)]
+            [(diag_hbm, diag_ref), (inert_hbm, inert_ref), (cpl_hbm, coef_ref.at[0:4])], 2
         )
     ]
-    for copy in copies:
+    force = [
+        pltpu.make_async_copy(f_hbm.at[:, :, :, 7 * h : 7 * h + 1], fe_ref.at[h], sems.at[5 + h])
+        for h in range(2)
+    ]
+    for copy in edges + coefs + force:
         copy.start()
-    for i in range(4):
-        p, c = i // 2, i % 2
-        copies[i].wait()
-        for v in range(5):
-            for r in range(2):
-                at = 8 * v + 4 * p + 2 * r + c
-                up_ref[at : at + 1, :] = x_ref[p, c, v, 6 + r : 7 + r, :]
-                down_ref[at : at + 1, :] = x_ref[p, c, v, r : r + 1, :]
-    for copy in copies[4:7]:
+    for h, ref in enumerate((down_ref, up_ref)):
+        edges[h].wait()
+        for p in range(2):
+            for c in range(2):
+                for v in range(5):
+                    for r in range(2):
+                        at = 8 * v + 4 * p + 2 * r + c
+                        ref[at : at + 1, :] = xe_ref[h, p, c, v, r : r + 1, :]
+    for copy in coefs:
         copy.wait()
     diag = diag_ref[...]
     inert = inert_ref[...]
@@ -70,13 +72,13 @@
     for i in range(6):
         up_ref[60 + i : 61 + i, :] = coef_ref[i, 7:8, :]
         down_ref[60 + i : 61 + i, :] = coef_ref[i, 0:1, :]
-    for i in range(4):
-        p, c = i // 2, i % 2
-        copies[7 + i].wait()
-        for v in range(5):
-            at = 40 + 4 * v + 2 * p + c
-            up_ref[at : at + 1, :] = f_ref[p, c, v, 7:8, :]
-            down_ref[at : at + 1, :] = f_ref[p, c, v, 0:1, :]
+    for h, ref in enumerate((down_ref, up_ref)):
+        force[h].wait()
+        for p in range(2):
+            for c in range(2):
+                for v in range(5):
+                    at = 40 + 4 * v + 2 * p + c
+                    ref[at : at + 1, :] = fe_ref[h, p, c, v, :, :]
 
 
 def tables_kernel(jac_ref, rot_ref, own_ref, plain_ref, lo_ref, hi_ref):
@@ -136,40 +138,16 @@
         ref[...] = split(jnp.concatenate(tiles[i], axis=0))
 
 
-def hot_kernel(idx_ref, weight_ref, hot_ref, cell_ref, sum_ref):
+def hot_kernel(idx_ref, hot_ref):
     shape = hot_ref.shape[1:]
-    chunk = shape[1]
-    groups = cell_ref.shape[1] // WIDE
-    rows = 8 * groups
-    sum_ref[...] = jnp.zeros_like(sum_ref)
 
     def one(d, _):
-        idx = idx_ref[d]
-        low = jnp.broadcast_to(idx & (WIDE - 1), shape)
-        hot = jnp.where(lax.broadcasted_iota(jnp.int32, shape, 0) == low, 1.0, 0.0).astype(jnp.bfloat16)
-        hot_ref[d] = hot
-        top = jnp.broadcast_to(idx >> 8, (rows, chunk))
-        row = lax.broadcasted_iota(jnp.int32, (rows, chunk), 0)
-        weight = jnp.where(top == (row & 7) * groups + (row >> 3), jnp.broadcast_to(weight_ref[d], (rows, chunk)), 0.0)
-        parts = []
-        for _ in range(3):
-            part = weight.astype(jnp.bfloat16).astype(jnp.float32)
-            parts.append(part)
-            weight = weight - part
-        sum_ref[...] += lax.dot_general(
-            jnp.concatenate(parts, axis=0).astype(jnp.bfloat16),
-            hot,
-            (((1,), (1,)), ((), ())),
-            preferred_element_type=jnp.float32,
-        )
+        low = jnp.broadcast_to(idx_ref[d] & (WIDE - 1), shape)
+        hot = jnp.where(lax.broadcasted_iota(jnp.int32, shape, 0) == low, 1.0, 0.0)
+        hot_ref[d] = hot.astype(jnp.bfloat16)
         return 0
 
-    lax.fori_loop(0, hot_ref.shape[0], one, 0, unroll=4)
-    for g in range(groups):
-        total = sum_ref[8 * g : 8 * g + 8, :]
-        for i in range(1, 3):
-            total = total + sum_ref[rows * i + 8 * g : rows * i + 8 * g + 8, :]
-        cell_ref[:, g * WIDE : (g + 1) * WIDE] = total
+    lax.fori_loop(0, hot_ref.shape[0], one, 0)
 
 
 def multiply(table, b):
@@ -192,7 +170,16 @@
 
 def pre_kernel(first, x_ref, f_ref, coef_ref, own_ref, *refs):
     if first:
-        next_ref, mid_ref, ef_ref, ecoef_ref, b_ref, y_ref = refs
+        x_hbm, f_hbm = x_ref, f_ref
+        next_ref, mid_ref, ef_ref, ecoef_ref, f_ref, b_ref, y_ref, x_ref, sems = refs
+        copies = [
+            pltpu.make_async_copy(src.at[p, c], dst.at[p, c], sems.at[4 * p + 2 * i + c])
+            for p in range(2)
+            for i, (src, dst) in enumerate(((x_hbm, x_ref), (f_hbm, f_ref)))
+            for c in range(2)
+        ]
+        for copy in copies:
+            copy.start()
     else:
         edge_refs, (next_ref, mid_ref, b_ref, y_ref) = refs[:2], refs[2:]
     cells = x_ref.shape[-1]
@@ -206,18 +193,22 @@
                     jnp.broadcast_to(coef_ref[i, 6 * h + 1 : 6 * h + 2, :], (8, cells)),
                 )
                 ecoef_ref[h, i] = jnp.where(row & 1 == 0, tile, -tile) if i == 5 else tile
-            for n in range(20):
-                p, c, v = n // 10, n // 5 % 2, n % 5
-                for r in range(2):
-                    at = 4 * p + 2 * r + c
-                    ef_ref[h, v, at : at + 1, :] = f_ref[p, c, v, 6 * h + r : 6 * h + r + 1, :]
     for c in range(2):
         b_ref[c, 40:48, :] = jnp.zeros((8, cells), jnp.float32)
     coef = [coef_ref[i] for i in range(6)]
     for p in range(2):
+        if first:
+            for copy in copies[4 * p : 4 * p + 4]:
+                copy.wait()
         for c in range(2):
             b_ref[c, 0:40, :] = x_ref[p, c].reshape(40, cells)
-            if not first:
+            if first:
+                for h in range(2):
+                    for v in range(5):
+                        for r in range(2):
+                            at, row = 4 * p + 2 * r + c, 6 * h + r
+                            ef_ref[h, v, at : at + 1, :] = f_ref[p, c, v, row : row + 1, :]
+            else:
                 for h in range(2):
                     for v in range(5):
                         for r in range(2):
@@ -252,7 +243,7 @@
     if first:
         down_out, up_out, gf_ref, gcoef_ref = refs
     elif last:
-        gf_ref, gcoef_ref, cell_ref, part_work_ref, pw_ref, down_out, up_out, press_ref, work_ref = refs
+        gf_ref, gcoef_ref, pw_ref, down_out, up_out, press_ref = refs
     else:
         gf_ref, gcoef_ref, down_out, up_out = refs
     cells = lo_ref.shape[-1]
@@ -316,20 +307,9 @@
             for v in range(1, 5):
                 press = press + pw_ref[v] * new[8 * v : 8 * v + 8]
             press_ref[h] = press
-            weight = jnp.where(
-                (row >> 1) & 1 == 0,
-                jnp.broadcast_to(cell_ref[6 * h : 6 * h + 1, :], (8, cells)),
-                jnp.broadcast_to(cell_ref[6 * h + 1 : 6 * h + 2, :], (8, cells)),
-            )
-            work = weight * press if h == 0 else work + weight * press
-    if last:
-        work = jnp.broadcast_to(jnp.sum(work, axis=1, keepdims=True), (8, LANES))
-        both = work + pltpu.roll(work, 6, 0)
-        work_ref[0:2, :] = both[0:2] + part_work_ref[0:2, :]
-        work_ref[2:4, :] = both[4:6] + part_work_ref[2:4, :]
-
-
-def inner_kernel(pw_ref, x_ref, idx_ref, hot_ref, cell_ref, out_ref, work_ref, table_ref):
+
+
+def inner_kernel(pw_ref, x_ref, idx_ref, hot_ref, out_ref, table_ref):
     cells = x_ref.shape[-1]
     chunk = idx_ref.shape[-1]
     parts = idx_ref.shape[0]
@@ -344,8 +324,6 @@
             value = value + pw_ref[v] * x_ref[i // 2, i % 2, v]
         value = jnp.where(kept, value, 0.0)
         press.append(value)
-        work = jnp.sum(jnp.sum(value * cell_ref[...], axis=1, keepdims=True), axis=0, keepdims=True)
-        work_ref[i : i + 1, :] = jnp.broadcast_to(work, (1, LANES))
     for i in range(2):
         value = press[2 * i] + pltpu.roll(press[2 * i + 1], 4, 0)
         high = value.astype(jnp.bfloat16).astype(jnp.float32)
@@ -376,7 +354,7 @@
     lax.fori_loop(0, parts, one, 0, unroll=16)
 
 
-def surface_kernel(press_ref, idx_ref, hot_ref, inner_ref, work_ref, out_ref):
+def surface_kernel(press_ref, idx_ref, hot_ref, inner_ref, weight_ref, out_ref):
     cells = press_ref.shape[-1]
     chunk = idx_ref.shape[-1]
     parts = idx_ref.shape[0]
@@ -390,7 +368,7 @@
     row = lax.broadcasted_iota(jnp.int32, (8, chunk), 0)
     place = ((row >> 1) & 1) * groups
 
-    def one(d, _):
+    def one(d, work):
         both = jnp.dot(table, hot_ref[d], preferred_element_type=jnp.float32)
         found = both[:half] + both[half:]
         top = jnp.broadcast_to(idx_ref[d] >> 8, (8, chunk))
@@ -400,12 +378,14 @@
                 at = (h * groups + g) * 8
                 total = jnp.where(top == place + (6 * h * groups + g), found[at : at + 8], total)
         total = total + pltpu.roll(total, 6, 0)
-        out_ref[d, 0:2, 0:chunk] = inner_ref[d, 0:2, :] + total[0:2]
-        out_ref[d, 2:4, 0:chunk] = inner_ref[d, 2:4, :] + total[4:6]
-        out_ref[d, :, chunk : chunk + LANES] = work_ref[...]
-        return 0
-
-    lax.fori_loop(0, parts, one, 0, unroll=16)
+        values = inner_ref[d] + jnp.concatenate([total[0:2], total[4:6]], axis=0)
+        out_ref[d, :, 0:chunk] = values
+        return work + values * weight_ref[d]
+
+    work = lax.fori_loop(0, parts, one, jnp.zeros((4, chunk), jnp.float32), unroll=16)
+    work = jnp.broadcast_to(jnp.sum(work, axis=1, keepdims=True), (4, LANES))
+    for d in range(parts):
+        out_ref[d, :, chunk : chunk + LANES] = work
 
 
 def merge_kernel(x_ref, down_ref, up_ref, out_ref):
@@ -501,21 +481,23 @@
     chunk = entries // devices
     idx = surface_cells.reshape(devices, 1, chunk)
 
-    coef, up, down, state, forcing = call(
+    def in_hbm(a):
+        return pltpu.with_memory_space_constraint(a, pltpu.HBM)
+
+    state, forcing = in_hbm(previous), in_hbm(forcing)
+    coef, up, down = call(
         pack_kernel,
         "pack",
-        [((6, 8, cells), f32), ((66, cells), f32), ((66, cells), f32)]
-        + [(previous.shape, f32)] * 2,
+        [((6, 8, cells), f32), ((66, cells), f32), ((66, cells), f32)],
         [
             pltpu.VMEM((8, cells), f32),
             pltpu.VMEM((8, cells), f32),
-            pltpu.SemaphoreType.DMA((11,)),
+            pltpu.VMEM((2, 2, 2, 5, 2, cells), f32),
+            pltpu.VMEM((2, 2, 2, 5, 1, cells), f32),
+            pltpu.SemaphoreType.DMA((7,)),
         ],
         1 << 20,
-        [
-            pltpu.with_memory_space_constraint(a, pltpu.HBM)
-            for a in (previous, forcing, coupling, diagonal, inertia)
-        ],
+        [state, forcing] + [in_hbm(a) for a in (coupling, diagonal, inertia)],
         [HBM] * 5,
     )
     bf16 = jnp.bfloat16
@@ -528,14 +510,14 @@
         [jacobians, turn],
         [SMEM] * 2,
     )
-    hot, cell_weight = call(
+    (hot,) = call(
         hot_kernel,
         "onehot",
-        [((devices, WIDE, chunk), bf16), ((8, cells), f32)],
-        [pltpu.VMEM((96 * cells // 1024, WIDE), f32)],
+        [((devices, WIDE, chunk), bf16)],
+        [],
         8 << 20,
-        [idx, modal_weights.reshape(devices, 1, chunk)],
-        [VMEM] * 2,
+        [idx],
+        [VMEM],
     )
     steps = ITERS // WIDTH
     edge_shape = (2, 5, 8, cells)
@@ -548,36 +530,37 @@
             functools.partial(pre_kernel, first),
             "pre",
             [(previous.shape, f32), ((2, 40, cells), f32)]
-            + ([(edge_shape, f32), ((2, 6, 8, cells), f32)] if first else []),
-            [pltpu.VMEM((2, 48, cells), f32), pltpu.VMEM((2, 160, cells), f32)],
+            + ([(edge_shape, f32), ((2, 6, 8, cells), f32), (previous.shape, f32)] if first else []),
+            [pltpu.VMEM((2, 48, cells), f32), pltpu.VMEM((2, 160, cells), f32)]
+            + ([pltpu.VMEM(previous.shape, f32), pltpu.SemaphoreType.DMA((8,))] if first else []),
             40 << 20,
             operands,
-            [VMEM] * len(operands),
+            [HBM] * 2 + [VMEM] * 2 if first else [VMEM] * len(operands),
         )
         state, mid = got[:2]
         if first:
-            edges = got[2:]
+            edges, forcing = got[2:4], got[4]
             ghosts = ()
         if step == 1:
-            mid, hot, cell_weight = lax.optimization_barrier((mid, hot, cell_weight))
+            mid, hot = lax.optimization_barrier((mid, hot))
         outs = [((40, cells), f32)] * 2
         operands = [turn, *tables, *edges, lo, hi, up, down, mid, *ghosts]
         specs = [SMEM] + [VMEM] * (len(operands) - 1)
         if first:
             outs += [(edge_shape, f32), ((2, 6, 8, cells), f32)]
         if last:
-            inner, inner_work = call(
+            (inner,) = call(
                 inner_kernel,
                 "inner",
-                [((devices, 4, chunk), f32), ((4, LANES), f32)],
+                [((devices, 4, chunk), f32)],
                 [pltpu.VMEM((128, WIDE), f32)],
                 20 << 20,
-                [pressure_weights, state, idx, hot, cell_weight],
-                [SMEM] + [VMEM] * 4,
+                [pressure_weights, state, idx, hot],
+                [SMEM] + [VMEM] * 3,
             )
-            outs += [((2, 8, cells), f32), ((4, LANES), f32)]
-            operands += [cell_weight, inner_work, pressure_weights]
-            specs += [VMEM, VMEM, SMEM]
+            outs += [((2, 8, cells), f32)]
+            operands += [pressure_weights]
+            specs += [SMEM]
         down, up, *got = call(
             functools.partial(post_kernel, first, last),
             "post",
@@ -589,14 +572,14 @@
         )
         if first:
             ghosts = got
-    press, work = got
+    (press,) = got
     (mine,) = call(
         surface_kernel,
         "surface",
         [((devices, 4, chunk + LANES), f32)],
         [],
         1 << 28,
-        [press, idx, hot, inner, work],
+        [press, idx, hot, inner, modal_weights.reshape(devices, 1, chunk)],
         [VMEM] * 5,
     )
     (state,) = call(
@@ -614,9 +597,9 @@
     def across(bits):
         return lax.ppermute(work, "space", [(i, i ^ bits) for i in range(count)])
 
-    work = (work + across(8))[:, :LANES]
-    work = work + across(4)
-    work = (work + across(1)) + (across(2) + across(3))
+    work = (work + across(2))[:, :LANES]
+    work = (work + across(4)) + (across(8) + across(12))
+    work = work + across(1)
     (turned,) = call(
         phase_kernel,
         "phases",

time: 71.9 us -> 71.5 us (level)
    all_to_all x1, waiting for transfers between devices: 0.96 us -> 0.01 us  [per_device(): blocks = lax.all_to_all(turned, 'phase', 0, 0, tiled=True)]
    ppermute x5, waiting for transfers between devices: 3.82 us -> 4.76 us  [across(): return lax.ppermute(work, 'space', [(i, i ^ bits) for i in range(count)])]
    all_to_all x1, starting transfers between devices: 4.79 us -> 3.9 us  [per_device(): blocks = lax.all_to_all(turned, 'phase', 0, 0, tiled=True)]
    all_to_all x1, starting transfers between devices: 8.43 us -> 9.25 us  [per_device(): every = lax.all_to_all(mine, 'phase', 0, 0, tiled=True)]
  transfers between devices with their start and end apart: 13 -> 13, of which waited for: 5 -> 6; matrix products, arithmetic and copies ran while one was open for 3% -> 3% of each run, Pallas kernels for 17% -> 17%
where the time goes in v2:
time: 71.5 us; the launch traced here: 70.2 us
  starting transfers between devices  32.2 us (45%)
  Pallas kernels  19.7 us (28%)
  waiting for transfers between devices  15.4 us (22%)
  local copies, waits for them, and re-layouts  1.15 us (2%)
  other arithmetic  0.9 us (1%)
  between operations  0.87 us (1%)
    pallas_call x15, Pallas kernels, call(): pl.pallas_call(kernel, name=name, out_shape=[jax.ShapeDtypeStruct(s, d) f...  19.7 us
    all_to_all x1, starting transfers between devices, per_device(): every = lax.all_to_all(mine, 'phase', 0, 0, tiled=True)  9.25 us
    ppermute x5, starting transfers between devices, across(): return lax.ppermute(work, 'space', [(i, i ^ bits) for i in range(count)])  8.12 us
    ppermute x3, starting transfers between devices, per_device(): hi = lax.ppermute(down, 'space', backward)  8.05 us
    all_to_all x1, waiting for transfers between devices, per_device(): every = lax.all_to_all(mine, 'phase', 0, 0, tiled=True)  7.7 us
    ppermute x5, waiting for transfers between devices, across(): return lax.ppermute(work, 'space', [(i, i ^ bits) for i in range(count)])  4.76 us
    all_to_all x1, starting transfers between devices, per_device(): blocks = lax.all_to_all(turned, 'phase', 0, 0, tiled=True)  3.9 us
    ppermute x3, waiting for transfers between devices, per_device(): hi = lax.ppermute(down, 'space', backward)  2.92 us
  transfers between devices with their start and end apart: 13, of which 6 were waited for; matrix products, arithmetic and copies ran while one was open for 3% of the time, Pallas kernels for 17%

profile of v2, /device:TPU:1, one launch (start us, length us, event | category | flops | bytes accessed | tf_op | source)
XLA Modules:
  0.0 70.2 jit_solution(3333997207467266805)
XLA Ops:
  0.6 1.2 %pack.1 = (f32[6,8,1024]{2,1,0:T(8,128)S(1)}, f32[66,1024]{1,0:T(8,128)S(1)}, f32[66,1024]{1,0:T(8,128)S(1)}) custom-call(f32[2,2,5,8,1024]{4,3,2,1,0:T(8,128)} %x_ref.1, f32[2,2,5,8,1024]{4,3,2,1,0:T(8,128)} %f_ref.1, f32[4,8,1024]{2,1,0:T(8,128)} %cpl_hbm.1, f32[8,1024]{1,0:T(8,128)} %diag_hbm.1, f32[8,1024]{1,0:T(8,128)} %inert_hbm.1), custom_call_target="tpu_custom_call" | custom-call | flops 1048576 | bytes 1048576 | tf_op jit(solution)/shard_map/pack/pallas_call | solution.py:24
  1.9 2.7 %collective-permute-start = (f32[66,1024]{1,0:T(8,128)S(1)}, f32[66,1024]{1,0:T(8,128)S(1)}, u32[]{:S(2)}, u32[]{:S(2)}) collective-permute-start(f32[66,1024]{1,0:T(8,128)S(1)} %get-tuple-element.43.up_ref), channel_id=1, source_target_pairs={{0,1},{1,2},{2,3},{3,4},{4,5},{5,6},{6,7},{7,8},{8,9},{9,10},{10,1... | collective-permute-start | bytes 811016 | tf_op jit(solution)/shard_map/ppermute | solution.py:526
  7.0 1.0 %tables.1 = (bf16[160,144]{1,0:T(8,128)(2,1)S(1)}, bf16[200,240]{1,0:T(8,128)(2,1)S(1)}, bf16[200,240]{1,0:T(8,128)(2,1)S(1)}, bf16[200,240]{1,0:T(8,128)(2,1)S(1)}) custom-call(f32[4,5,5]{2,1,0:T(8,128)S(1)} %copy.19.jac_ref, f32[8]{0:T(128)S(1)} %reshape.140.rot_ref), custom_call_target="tpu_custom_call" | custom-call | flops 1048576 | bytes 1048576 | tf_op jit(solution)/shard_map/tables/pallas_call | solution.py:24
  8.0 3.2 %pre.3 = (f32[2,2,5,8,1024]{4,3,2,1,0:T(8,128)S(1)}, f32[2,40,1024]{2,1,0:T(8,128)S(1)}, f32[2,5,8,1024]{3,2,1,0:T(8,128)S(1)}, f32[2,6,8,1024]{3,2,1,0:T(8,128)S(1)}, f32[2,2,5,8,1024]{4,3,2,1,0:T(8,128)S(1)}) custom-call(f32[2,2,5,8,1024]{4,3,2,1,0:T(8,128)} %x_ref.1, f32[2,2,5,8,1024]{4,3,2,1,0:T(8,128)} %f_ref.1, ...), custom_call_target="tpu_custom_call" | custom-call | flops 41943040 | bytes 1048576 | tf_op jit(solution)/shard_map/pre/pallas_call | solution.py:24
  11.2 2.2 %collective-permute-done.1.hi_ref = f32[66,1024]{1,0:T(8,128)S(1)} collective-permute-done((f32[66,1024]{1,0:T(8,128)S(1)}, f32[66,1024]{1,0:T(8,128)S(1)}, u32[]{:S(2)}, u32[]{:S(2)}) %collective-permute-start.1) | collective-permute-done | bytes 270368 | tf_op jit(solution)/shard_map/ppermute | solution.py:527
  13.4 1.5 %post.3 = (f32[40,1024]{1,0:T(8,128)S(1)}, f32[40,1024]{1,0:T(8,128)S(1)}, f32[2,5,8,1024]{3,2,1,0:T(8,128)S(1)}, f32[2,6,8,1024]{3,2,1,0:T(8,128)S(1)}) custom-call(f32[8]{0:T(128)S(1)} %reshape.140.rot_ref, bf16[200,240]{1,0:T(8,128)(2,1)S(1)} %get-tuple-element.36.plain_ref, bf16[200,240]{1,0:T(8,128)(2,1)S(1)} %get-tuple-element.37.lo_turn_ref, ...), custom_call_target="tpu_custom_call" | custom-call | flops 20971520 | bytes 1048576 | tf_op jit(solution)/shard_map/post/pallas_call | solution.py:24
  15.1 3.0 %collective-permute-start.3 = (f32[40,1024]{1,0:T(8,128)S(1)}, f32[40,1024]{1,0:T(8,128)S(1)}, u32[]{:S(2)}, u32[]{:S(2)}) collective-permute-start(f32[40,1024]{1,0:T(8,128)S(1)} %get-tuple-element.47.refs_0_.down_ref), channel_id=1, source_target_pairs={{1,0},{2,1},{3,2},{4,3},{5,4},{6,5},{7,6},{8,7},{9,8},{10,9},{11,1... | collective-permute-start | bytes 491528 | tf_op jit(solution)/shard_map/ppermute | solution.py:527
  18.9 1.8 %pre.4 = (f32[2,2,5,8,1024]{4,3,2,1,0:T(8,128)S(1)}, f32[2,40,1024]{2,1,0:T(8,128)S(1)}) custom-call(f32[2,2,5,8,1024]{4,3,2,1,0:T(8,128)S(1)} %get-tuple-element.48.x_ref, f32[2,2,5,8,1024]{4,3,2,1,0:T(8,128)S(1)} %get-tuple-element.49.f_ref, f32[6,8,1024]{2,1,0:T(8,128)S(1)} %get-tuple-element.39.coef_ref, bf16[160,144]{1,0:T(8,128)(2,1)S(1)} %get-tuple-element.40.own_ref, ...), custom_call_target="tpu_custom_call" | custom-call | flops 41943040 | bytes 1048576 | tf_op jit(solution)/shard_map/pre/pallas_call | solution.py:24
  21.4 1.5 %post.4 = (f32[40,1024]{1,0:T(8,128)S(1)}, f32[40,1024]{1,0:T(8,128)S(1)}) custom-call(f32[8]{0:T(128)S(1)} %reshape.140.rot_ref, bf16[200,240]{1,0:T(8,128)(2,1)S(1)} %get-tuple-element.36.plain_ref, bf16[200,240]{1,0:T(8,128)(2,1)S(1)} %get-tuple-element.37.lo_turn_ref, bf16[200,240]{1,0:T(8,128)(2,1)S(1)} %get-tuple-element.38.hi_turn_ref, ...), custom_call_target="tpu_custom_call" | custom-call | flops 20971520 | bytes 1048576 | tf_op jit(solution)/shard_map/post/pallas_call | solution.py:24
  23.0 4.3 %collective-permute-start.5 = (f32[40,1024]{1,0:T(8,128)S(1)}, f32[40,1024]{1,0:T(8,128)S(1)}, u32[]{:S(2)}, u32[]{:S(2)}) collective-permute-start(f32[40,1024]{1,0:T(8,128)S(1)} %get-tuple-element.55.refs_0_.down_ref), channel_id=1, source_target_pairs={{1,0},{2,1},{3,2},{4,3},{5,4},{6,5},{7,6},{8,7},{9,8},{10,9},{11,1... | collective-permute-start | bytes 491528 | tf_op jit(solution)/shard_map/ppermute | solution.py:527
  27.4 1.8 %pre.5 = (f32[2,2,5,8,1024]{4,3,2,1,0:T(8,128)S(1)}, f32[2,40,1024]{2,1,0:T(8,128)S(1)}) custom-call(f32[2,2,5,8,1024]{4,3,2,1,0:T(8,128)S(1)} %get-tuple-element.56.x_ref, f32[2,2,5,8,1024]{4,3,2,1,0:T(8,128)S(1)} %get-tuple-element.49.f_ref, f32[6,8,1024]{2,1,0:T(8,128)S(1)} %get-tuple-element.39.coef_ref, bf16[160,144]{1,0:T(8,128)(2,1)S(1)} %get-tuple-element.40.own_ref, ...), custom_call_target="tpu_custom_call" | custom-call | flops 41943040 | bytes 1048576 | tf_op jit(solution)/shard_map/pre/pallas_call | solution.py:24
  29.2 1.3 %inner.1.inner_ref = f32[16,4,512]{2,1,0:T(4,128)S(1)} custom-call(f32[5]{0:T(128)S(1)} %copy-done.2, f32[2,2,5,8,1024]{4,3,2,1,0:T(8,128)S(1)} %get-tuple-element.60.x_ref, s32[16,1,512]{2,1,0:T(1,128)S(1)} %bitcast.14, bf16[16,256,512]{2,1,0:T(8,128)(2,1)S(1)} %onehot.1.hot_ref), custom_call_target="tpu_custom_call" | custom-call | flops 20971520 | bytes 1048576 | tf_op jit(solution)/shard_map/inner/pallas_call | solution.py:24
  30.5 1.5 %post.5 = (f32[40,1024]{1,0:T(8,128)S(1)}, f32[40,1024]{1,0:T(8,128)S(1)}, f32[2,8,1024]{2,1,0:T(8,128)S(1)}) custom-call(f32[8]{0:T(128)S(1)} %reshape.140.rot_ref, bf16[200,240]{1,0:T(8,128)(2,1)S(1)} %get-tuple-element.36.plain_ref, bf16[200,240]{1,0:T(8,128)(2,1)S(1)} %get-tuple-element.37.lo_turn_ref, ...), custom_call_target="tpu_custom_call" | custom-call | flops 20971520 | bytes 1048576 | tf_op jit(solution)/shard_map/post/pallas_call | solution.py:24
  32.0 1.5 %surface.1 = f32[16,4,640]{2,1,0:T(4,128)} custom-call(f32[2,8,1024]{2,1,0:T(8,128)S(1)} %get-tuple-element.58.press_ref, s32[16,1,512]{2,1,0:T(1,128)S(1)} %bitcast.15, bf16[16,256,512]{2,1,0:T(8,128)(2,1)S(1)} %onehot.1.hot_ref, f32[16,4,512]{2,1,0:T(4,128)S(1)} %inner.1.inner_ref, f32[16,1,512]{2,1,0:T(1,128)S(1)} %bitcast.18), custom_call_target="tpu_custom_call" | custom-call | flops 268435456 | bytes 1048576 | tf_op jit(solution)/shard_map/surface/pallas_call | solution.py:24
  33.5 9.2 %all-to-all-start = ((f32[16,4,640]{2,1,0:T(4,128)}), f32[16,4,640]{2,1,0:T(4,128)S(1)}, u32[]{:S(2)}, u32[]{:S(2)}) async-start(f32[16,4,640]{2,1,0:T(4,128)} %surface.1), calls=%async_computation | async-start | bytes 327680 | tf_op jit(solution)/shard_map/all_to_all | solution.py:589
  43.0 1.0 %merge.1 = f32[2,2,5,8,1024]{4,3,2,1,0:T(8,128)} custom-call(f32[2,2,5,8,1024]{4,3,2,1,0:T(8,128)S(1)} %get-tuple-element.60.x_ref, f32[40,1024]{1,0:T(8,128)S(1)} %get-tuple-element.61.down_ref, f32[40,1024]{1,0:T(8,128)S(1)} %get-tuple-element.62.up_ref), custom_call_target="tpu_custom_call" | custom-call | flops 1048576 | bytes 1048576 | tf_op jit(solution)/shard_map/merge/pallas_call | solution.py:24
  44.0 7.7 %all-to-all-done.x_ref = f32[16,4,640]{2,1,0:T(4,128)S(1)} async-done(((f32[16,4,640]{2,1,0:T(4,128)}), f32[16,4,640]{2,1,0:T(4,128)S(1)}, u32[]{:S(2)}, u32[]{:S(2)}) %all-to-all-start) | async-done | bytes 163872 | tf_op jit(solution)/shard_map/all_to_all | solution.py:589
  51.8 1.9 %collective-permute-start.6 = (f32[4,2048]{1,0:T(4,128)S(1)}, f32[4,2048]{1,0:T(4,128)S(1)}, u32[]{:S(2)}, u32[]{:S(2)}) collective-permute-start(f32[4,2048]{1,0:T(4,128)S(1)} %work.1), channel_id=1, source_target_pairs={{0,2},{1,3},{2,0},{3,1},{4,6},{5,7},{6,4},{7,5},{8,10},{9,11},{10,... | collective-permute-start | bytes 98312 | tf_op jit(solution)/shard_map/ppermute | solution.py:598
  54.6 3.9 %all-to-all-start.1 = ((f32[16,4,512]{2,1,0:T(4,128)}), f32[16,4,512]{2,1,0:T(4,128)S(1)}, u32[]{:S(2)}, u32[]{:S(2)}) async-start(f32[16,4,512]{2,1,0:T(4,128)} %phases.1), calls=%async_computation.1 | async-start | bytes 262144 | tf_op jit(solution)/shard_map/all_to_all | solution.py:612
  58.5 1.4 %collective-permute-start.7 = (f32[4,128]{1,0:T(4,128)S(1)}, f32[4,128]{1,0:T(4,128)S(1)}, u32[]{:S(2)}, u32[]{:S(2)}) collective-permute-start(f32[4,128]{1,0:T(4,128)S(1)} %slice_add_fusion), channel_id=1, source_target_pairs={{0,4},{1,5},{2,6},{3,7},{4,0},{5,1},{6,2},{7,3},{8,12},{9,13},{10,... | collective-permute-start | bytes 6152 | tf_op jit(solution)/shard_map/ppermute | solution.py:598
  59.9 4.0 %collective-permute-start.8 = (f32[4,128]{1,0:T(4,128)S(1)}, f32[4,128]{1,0:T(4,128)S(1)}, u32[]{:S(2)}, u32[]{:S(2)}) collective-permute-start(f32[4,128]{1,0:T(4,128)S(1)} %slice_add_fusion), channel_id=1, source_target_pairs={{0,8},{1,9},{2,10},{3,11},{4,12},{5,13},{6,14},{7,15},{8,0},{9,1},... | collective-permute-start | bytes 6152 | tf_op jit(solution)/shard_map/ppermute | solution.py:598
  63.9 1.0 %collective-permute-done.8 = f32[4,128]{1,0:T(4,128)S(1)} collective-permute-done((f32[4,128]{1,0:T(4,128)S(1)}, f32[4,128]{1,0:T(4,128)S(1)}, u32[]{:S(2)}, u32[]{:S(2)}) %collective-permute-start.8) | collective-permute-done | bytes 2080 | tf_op jit(solution)/shard_map/ppermute | solution.py:598
  64.9 2.9 %collective-permute-done.9 = f32[4,128]{1,0:T(4,128)S(1)} collective-permute-done((f32[4,128]{1,0:T(4,128)S(1)}, f32[4,128]{1,0:T(4,128)S(1)}, u32[]{:S(2)}, u32[]{:S(2)}) %collective-permute-start.9) | collective-permute-done | bytes 2080 | tf_op jit(solution)/shard_map/ppermute | solution.py:598
  67.8 0.9 %collective-permute-start.10 = (f32[4,128]{1,0:T(4,128)S(1)}, f32[4,128]{1,0:T(4,128)S(1)}, u32[]{:S(2)}, u32[]{:S(2)}) collective-permute-start(f32[4,128]{1,0:T(4,128)S(1)} %add_add_fusion), channel_id=1, source_target_pairs={{0,1},{1,0},{2,3},{3,2},{4,5},{5,4},{6,7},{7,6},{8,9},{9,8},{10,11... | collective-permute-start | bytes 6152 | tf_op jit(solution)/shard_map/ppermute | solution.py:598
  (40 shorter events, 7.0 us)
Async XLA Ops:
  0.6 17.4 %copy-start = (s32[8192]{0:T(1024)S(1)}, s32[8192]{0:T(1024)}, u32[]{:S(2)}) copy-start(s32[8192]{0:T(1024)} %param.17) | copy-start | bytes 98308
  1.9 9.3 %collective-permute-start = (f32[66,1024]{1,0:T(8,128)S(1)}, f32[66,1024]{1,0:T(8,128)S(1)}, u32[]{:S(2)}, u32[]{:S(2)}) collective-permute-start(f32[66,1024]{1,0:T(8,128)S(1)} %get-tuple-element.43.up_ref), channel_id=1, source_target_pairs={{0,1},{1,2},{2,3},{3,4},{4,5},{5,6},{6,7},{7,8},{8,9},{9,10},{10,1... | collective-permute-start | bytes 811016 | tf_op jit(solution)/shard_map/ppermute | solution.py:526
  4.6 8.8 %collective-permute-start.1 = (f32[66,1024]{1,0:T(8,128)S(1)}, f32[66,1024]{1,0:T(8,128)S(1)}, u32[]{:S(2)}, u32[]{:S(2)}) collective-permute-start(f32[66,1024]{1,0:T(8,128)S(1)} %get-tuple-element.44.down_ref), channel_id=1, source_target_pairs={{1,0},{2,1},{3,2},{4,3},{5,4},{6,5},{7,6},{8,7},{9,8},{10,9},{11,1... | collective-permute-start | bytes 811016 | tf_op jit(solution)/shard_map/ppermute | solution.py:527
  15.0 5.7 %collective-permute-start.2 = (f32[40,1024]{1,0:T(8,128)S(1)}, f32[40,1024]{1,0:T(8,128)S(1)}, u32[]{:S(2)}, u32[]{:S(2)}) collective-permute-start(f32[40,1024]{1,0:T(8,128)S(1)} %get-tuple-element.46.refs_1_.up_ref), channel_id=1, source_target_pairs={{0,1},{1,2},{2,3},{3,4},{4,5},{5,6},{6,7},{7,8},{8,9},{9,10},{10,1... | collective-permute-start | bytes 491528 | tf_op jit(solution)/shard_map/ppermute | solution.py:526
  15.1 6.4 %collective-permute-start.3 = (f32[40,1024]{1,0:T(8,128)S(1)}, f32[40,1024]{1,0:T(8,128)S(1)}, u32[]{:S(2)}, u32[]{:S(2)}) collective-permute-start(f32[40,1024]{1,0:T(8,128)S(1)} %get-tuple-element.47.refs_0_.down_ref), channel_id=1, source_target_pairs={{1,0},{2,1},{3,2},{4,3},{5,4},{6,5},{7,6},{8,7},{9,8},{10,9},{11,1... | collective-permute-start | bytes 491528 | tf_op jit(solution)/shard_map/ppermute | solution.py:527
  18.1 9.2 %copy-start.3 = (s32[32]{0:T(128)S(1)}, s32[32]{0:T(128)}, u32[]{:S(2)}) copy-start(s32[32]{0:T(128)} %param.19) | copy-start | bytes 388
  18.9 10.3 %copy-start.2 = (f32[5]{0:T(128)S(1)}, f32[5]{0:T(128)}, u32[]{:S(2)}) copy-start(f32[5]{0:T(128)} %pw_ref.1) | copy-start | bytes 64
  22.9 7.6 %collective-permute-start.4 = (f32[40,1024]{1,0:T(8,128)S(1)}, f32[40,1024]{1,0:T(8,128)S(1)}, u32[]{:S(2)}, u32[]{:S(2)}) collective-permute-start(f32[40,1024]{1,0:T(8,128)S(1)} %get-tuple-element.54.refs_1_.up_ref), channel_id=1, source_target_pairs={{0,1},{1,2},{2,3},{3,4},{4,5},{5,6},{6,7},{7,8},{8,9},{9,10},{10,1... | collective-permute-start | bytes 491528 | tf_op jit(solution)/shard_map/ppermute | solution.py:526
  23.0 7.5 %collective-permute-start.5 = (f32[40,1024]{1,0:T(8,128)S(1)}, f32[40,1024]{1,0:T(8,128)S(1)}, u32[]{:S(2)}, u32[]{:S(2)}) collective-permute-start(f32[40,1024]{1,0:T(8,128)S(1)} %get-tuple-element.55.refs_0_.down_ref), channel_id=1, source_target_pairs={{1,0},{2,1},{3,2},{4,3},{5,4},{6,5},{7,6},{8,7},{9,8},{10,9},{11,1... | collective-permute-start | bytes 491528 | tf_op jit(solution)/shard_map/ppermute | solution.py:527
  29.1 2.9 %copy-start.1 = (f32[8192]{0:T(1024)S(1)}, f32[8192]{0:T(1024)}, u32[]{:S(2)}) copy-start(f32[8192]{0:T(1024)} %param.18) | copy-start | bytes 98308
  33.5 18.2 %all-to-all-start = ((f32[16,4,640]{2,1,0:T(4,128)}), f32[16,4,640]{2,1,0:T(4,128)S(1)}, u32[]{:S(2)}, u32[]{:S(2)}) async-start(f32[16,4,640]{2,1,0:T(4,128)} %surface.1), calls=%async_computation | async-start | bytes 327680 | tf_op jit(solution)/shard_map/all_to_all | solution.py:589
  51.8 6.6 %collective-permute-start.6 = (f32[4,2048]{1,0:T(4,128)S(1)}, f32[4,2048]{1,0:T(4,128)S(1)}, u32[]{:S(2)}, u32[]{:S(2)}) collective-permute-start(f32[4,2048]{1,0:T(4,128)S(1)} %work.1), channel_id=1, source_target_pairs={{0,2},{1,3},{2,0},{3,1},{4,6},{5,7},{6,4},{7,5},{8,10},{9,11},{10,... | collective-permute-start | bytes 98312 | tf_op jit(solution)/shard_map/ppermute | solution.py:598
  54.6 15.0 %all-to-all-start.1 = ((f32[16,4,512]{2,1,0:T(4,128)}), f32[16,4,512]{2,1,0:T(4,128)S(1)}, u32[]{:S(2)}, u32[]{:S(2)}) async-start(f32[16,4,512]{2,1,0:T(4,128)} %phases.1), calls=%async_computation.1 | async-start | bytes 262144 | tf_op jit(solution)/shard_map/all_to_all | solution.py:612
  58.5 5.4 %collective-permute-start.7 = (f32[4,128]{1,0:T(4,128)S(1)}, f32[4,128]{1,0:T(4,128)S(1)}, u32[]{:S(2)}, u32[]{:S(2)}) collective-permute-start(f32[4,128]{1,0:T(4,128)S(1)} %slice_add_fusion), channel_id=1, source_target_pairs={{0,4},{1,5},{2,6},{3,7},{4,0},{5,1},{6,2},{7,3},{8,12},{9,13},{10,... | collective-permute-start | bytes 6152 | tf_op jit(solution)/shard_map/ppermute | solution.py:598
  59.9 5.0 %collective-permute-start.8 = (f32[4,128]{1,0:T(4,128)S(1)}, f32[4,128]{1,0:T(4,128)S(1)}, u32[]{:S(2)}, u32[]{:S(2)}) collective-permute-start(f32[4,128]{1,0:T(4,128)S(1)} %slice_add_fusion), channel_id=1, source_target_pairs={{0,8},{1,9},{2,10},{3,11},{4,12},{5,13},{6,14},{7,15},{8,0},{9,1},... | collective-permute-start | bytes 6152 | tf_op jit(solution)/shard_map/ppermute | solution.py:598
  63.9 3.9 %collective-permute-start.9 = (f32[4,128]{1,0:T(4,128)S(1)}, f32[4,128]{1,0:T(4,128)S(1)}, u32[]{:S(2)}, u32[]{:S(2)}) collective-permute-start(f32[4,128]{1,0:T(4,128)S(1)} %slice_add_fusion), channel_id=1, source_target_pairs={{0,12},{1,13},{2,14},{3,15},{4,8},{5,9},{6,10},{7,11},{8,4},{9,5},... | collective-permute-start | bytes 6152 | tf_op jit(solution)/shard_map/ppermute | solution.py:598
  67.8 1.7 %collective-permute-start.10 = (f32[4,128]{1,0:T(4,128)S(1)}, f32[4,128]{1,0:T(4,128)S(1)}, u32[]{:S(2)}, u32[]{:S(2)}) collective-permute-start(f32[4,128]{1,0:T(4,128)S(1)} %add_add_fusion), channel_id=1, source_target_pairs={{0,1},{1,0},{2,3},{3,2},{4,5},{5,4},{6,7},{7,6},{8,9},{9,8},{10,11... | collective-permute-start | bytes 6152 | tf_op jit(solution)/shard_map/ppermute | solution.py:598

commit v3 on v2

--- a/solution.py
+++ b/solution.py
@@ -28,7 +28,7 @@
         in_specs=in_specs,
         out_specs=out_specs or [VMEM] * len(out_shapes),
         scratch_shapes=scratch,
-        compiler_params=pltpu.CompilerParams(vmem_limit_bytes=40 * 1024 * 1024),
+        compiler_params=pltpu.CompilerParams(vmem_limit_bytes=20 * 1024 * 1024),
         cost_estimate=pl.CostEstimate(
             flops=flops, bytes_accessed=1 << 20, transcendentals=0
         ),
@@ -239,9 +239,9 @@
                         next_ref[p, c, v] = new
 
 
-def post_kernel(first, last, rot_ref, plain_ref, lo_turn_ref, hi_turn_ref, ef_ref, ecoef_ref, lo_ref, hi_ref, up_ref, down_ref, mid_ref, *refs):
+def post_kernel(first, last, plain_ref, lo_turn_ref, hi_turn_ref, ef_ref, ecoef_ref, lo_ref, hi_ref, up_ref, down_ref, mid_ref, *refs):
     if first:
-        down_out, up_out, gf_ref, gcoef_ref = refs
+        rot_ref, down_out, up_out, gf_ref, gcoef_ref = refs
     elif last:
         gf_ref, gcoef_ref, pw_ref, down_out, up_out, press_ref = refs
     else:
@@ -262,7 +262,8 @@
             ghost, base = (lo_ref, 0) if h == 0 else (hi_ref, 2)
             for v in range(5):
                 for p in range(2):
-                    cos, sin = rot_ref[4 * p + base], rot_ref[4 * p + base + 1]
+                    i = 4 * p + base
+                    cos, sin = rot_ref[i : i + 1, :], rot_ref[i + 1 : i + 2, :]
                     at = 40 + 4 * v + 2 * p
                     re = ghost[at : at + 1, :]
                     im = ghost[at + 1 : at + 2, :]
@@ -303,9 +304,9 @@
         )
         (up_out if h else down_out)[...] = new
         if last:
-            press = pw_ref[0] * new[0:8]
+            press = pw_ref[0:1, :] * new[0:8]
             for v in range(1, 5):
-                press = press + pw_ref[v] * new[8 * v : 8 * v + 8]
+                press = press + pw_ref[v : v + 1, :] * new[8 * v : 8 * v + 8]
             press_ref[h] = press
 
 
@@ -544,9 +545,9 @@
         if step == 1:
             mid, hot = lax.optimization_barrier((mid, hot))
         outs = [((40, cells), f32)] * 2
-        operands = [turn, *tables, *edges, lo, hi, up, down, mid, *ghosts]
-        specs = [SMEM] + [VMEM] * (len(operands) - 1)
+        operands = [*tables, *edges, lo, hi, up, down, mid, *ghosts]
         if first:
+            operands += [jnp.broadcast_to(turn[:, None], (8, cells))]
             outs += [(edge_shape, f32), ((2, 6, 8, cells), f32)]
         if last:
             (inner,) = call(
@@ -559,8 +560,7 @@
                 [SMEM] + [VMEM] * 3,
             )
             outs += [((2, 8, cells), f32)]
-            operands += [pressure_weights]
-            specs += [SMEM]
+            operands += [jnp.broadcast_to(pressure_weights[:, None], (5, cells))]
         down, up, *got = call(
             functools.partial(post_kernel, first, last),
             "post",
@@ -568,7 +568,7 @@
             [],
             20 << 20,
             operands,
-            specs,
+            [VMEM] * len(operands),
         )
         if first:
             ghosts = got

time: 71.5 us -> 70.1 us (0.980)
  Pallas kernels: 19.7 us -> 18.3 us
    pallas_call x15, Pallas kernels: 19.7 us -> 18.3 us  [call(): pl.pallas_call(kernel, name=name, out_shape=[jax.ShapeDtypeStruct(s, d) f...]
where the time goes in v3:
time: 70.1 us; the launch traced here: 68.8 us
  starting transfers between devices  32.1 us (46%)
  Pallas kernels  18.3 us (26%)
  waiting for transfers between devices  15.3 us (22%)
  local copies, waits for them, and re-layouts  1.29 us (2%)
  other arithmetic  0.9 us (1%)
  between operations  0.87 us (1%)
    pallas_call x15, Pallas kernels, call(): pl.pallas_call(kernel, name=name, out_shape=[jax.ShapeDtypeStruct(s, d) f...  18.3 us
    all_to_all x1, starting transfers between devices, per_device(): every = lax.all_to_all(mine, 'phase', 0, 0, tiled=True)  8.63 us
    ppermute x3, starting transfers between devices, per_device(): hi = lax.ppermute(down, 'space', backward)  8.63 us
    ppermute x5, starting transfers between devices, across(): return lax.ppermute(work, 'space', [(i, i ^ bits) for i in range(count)])  8.1 us
    all_to_all x1, waiting for transfers between devices, per_device(): every = lax.all_to_all(mine, 'phase', 0, 0, tiled=True)  7.7 us
    ppermute x5, waiting for transfers between devices, across(): return lax.ppermute(work, 'space', [(i, i ^ bits) for i in range(count)])  4.76 us
    all_to_all x1, starting transfers between devices, per_device(): blocks = lax.all_to_all(turned, 'phase', 0, 0, tiled=True)  3.91 us
    ppermute x3, waiting for transfers between devices, per_device(): hi = lax.ppermute(down, 'space', backward)  2.88 us
  transfers between devices with their start and end apart: 13, of which 6 were waited for; matrix products, arithmetic and copies ran while one was open for 3% of the time, Pallas kernels for 17%

profile of v3, /device:TPU:1, one launch (start us, length us, event | category | flops | bytes accessed | tf_op | source)
XLA Modules:
  0.0 68.8 jit_solution(3566001836192128478)
XLA Ops:
  0.6 1.2 %pack.1 = (f32[6,8,1024]{2,1,0:T(8,128)S(1)}, f32[66,1024]{1,0:T(8,128)S(1)}, f32[66,1024]{1,0:T(8,128)S(1)}) custom-call(f32[2,2,5,8,1024]{4,3,2,1,0:T(8,128)} %x_ref.1, f32[2,2,5,8,1024]{4,3,2,1,0:T(8,128)} %f_ref.1, f32[4,8,1024]{2,1,0:T(8,128)} %cpl_hbm.1, f32[8,1024]{1,0:T(8,128)} %diag_hbm.1, f32[8,1024]{1,0:T(8,128)} %inert_hbm.1), custom_call_target="tpu_custom_call" | custom-call | flops 1048576 | bytes 1048576 | tf_op jit(solution)/shard_map/pack/pallas_call | solution.py:24
  1.9 2.7 %collective-permute-start = (f32[66,1024]{1,0:T(8,128)S(1)}, f32[66,1024]{1,0:T(8,128)S(1)}, u32[]{:S(2)}, u32[]{:S(2)}) collective-permute-start(f32[66,1024]{1,0:T(8,128)S(1)} %get-tuple-element.43.up_ref), channel_id=1, source_target_pairs={{0,1},{1,2},{2,3},{3,4},{4,5},{5,6},{6,7},{7,8},{8,9},{9,10},{10,1... | collective-permute-start | bytes 811016 | tf_op jit(solution)/shard_map/ppermute | solution.py:527
  7.0 1.0 %tables.1 = (bf16[160,144]{1,0:T(8,128)(2,1)S(1)}, bf16[200,240]{1,0:T(8,128)(2,1)S(1)}, bf16[200,240]{1,0:T(8,128)(2,1)S(1)}, bf16[200,240]{1,0:T(8,128)(2,1)S(1)}) custom-call(f32[4,5,5]{2,1,0:T(8,128)S(1)} %copy.19.jac_ref, f32[8]{0:T(128)S(1)} %reshape.142.rot_ref), custom_call_target="tpu_custom_call" | custom-call | flops 1048576 | bytes 1048576 | tf_op jit(solution)/shard_map/tables/pallas_call | solution.py:24
  8.0 3.2 %pre.3 = (f32[2,2,5,8,1024]{4,3,2,1,0:T(8,128)S(1)}, f32[2,40,1024]{2,1,0:T(8,128)S(1)}, f32[2,5,8,1024]{3,2,1,0:T(8,128)S(1)}, f32[2,6,8,1024]{3,2,1,0:T(8,128)S(1)}, f32[2,2,5,8,1024]{4,3,2,1,0:T(8,128)S(1)}) custom-call(f32[2,2,5,8,1024]{4,3,2,1,0:T(8,128)} %x_ref.1, f32[2,2,5,8,1024]{4,3,2,1,0:T(8,128)} %f_ref.1, ...), custom_call_target="tpu_custom_call" | custom-call | flops 41943040 | bytes 1048576 | tf_op jit(solution)/shard_map/pre/pallas_call | solution.py:24
  11.2 2.2 %collective-permute-done.1.hi_ref = f32[66,1024]{1,0:T(8,128)S(1)} collective-permute-done((f32[66,1024]{1,0:T(8,128)S(1)}, f32[66,1024]{1,0:T(8,128)S(1)}, u32[]{:S(2)}, u32[]{:S(2)}) %collective-permute-start.1) | collective-permute-done | bytes 270368 | tf_op jit(solution)/shard_map/ppermute | solution.py:528
  13.5 1.0 %post.3 = (f32[40,1024]{1,0:T(8,128)S(1)}, f32[40,1024]{1,0:T(8,128)S(1)}, f32[2,5,8,1024]{3,2,1,0:T(8,128)S(1)}, f32[2,6,8,1024]{3,2,1,0:T(8,128)S(1)}) custom-call(bf16[200,240]{1,0:T(8,128)(2,1)S(1)} %get-tuple-element.36.plain_ref, bf16[200,240]{1,0:T(8,128)(2,1)S(1)} %get-tuple-element.37.lo_turn_ref, ...), custom_call_target="tpu_custom_call" | custom-call | flops 20971520 | bytes 1048576 | tf_op jit(solution)/shard_map/post/pallas_call | solution.py:24
  14.6 3.0 %collective-permute-start.3 = (f32[40,1024]{1,0:T(8,128)S(1)}, f32[40,1024]{1,0:T(8,128)S(1)}, u32[]{:S(2)}, u32[]{:S(2)}) collective-permute-start(f32[40,1024]{1,0:T(8,128)S(1)} %get-tuple-element.47.refs_0_.down_ref), channel_id=1, source_target_pairs={{1,0},{2,1},{3,2},{4,3},{5,4},{6,5},{7,6},{8,7},{9,8},{10,9},{11,1... | collective-permute-start | bytes 491528 | tf_op jit(solution)/shard_map/ppermute | solution.py:528
  18.4 1.8 %pre.4 = (f32[2,2,5,8,1024]{4,3,2,1,0:T(8,128)S(1)}, f32[2,40,1024]{2,1,0:T(8,128)S(1)}) custom-call(f32[2,2,5,8,1024]{4,3,2,1,0:T(8,128)S(1)} %get-tuple-element.48.x_ref, f32[2,2,5,8,1024]{4,3,2,1,0:T(8,128)S(1)} %get-tuple-element.49.f_ref, f32[6,8,1024]{2,1,0:T(8,128)S(1)} %get-tuple-element.39.coef_ref, bf16[160,144]{1,0:T(8,128)(2,1)S(1)} %get-tuple-element.40.own_ref, ...), custom_call_target="tpu_custom_call" | custom-call | flops 41943040 | bytes 1048576 | tf_op jit(solution)/shard_map/pre/pallas_call | solution.py:24
  21.0 0.9 %post.4 = (f32[40,1024]{1,0:T(8,128)S(1)}, f32[40,1024]{1,0:T(8,128)S(1)}) custom-call(bf16[200,240]{1,0:T(8,128)(2,1)S(1)} %get-tuple-element.36.plain_ref, bf16[200,240]{1,0:T(8,128)(2,1)S(1)} %get-tuple-element.37.lo_turn_ref, bf16[200,240]{1,0:T(8,128)(2,1)S(1)} %get-tuple-element.38.hi_turn_ref, f32[2,5,8,1024]{3,2,1,0:T(8,128)S(1)} %get-tuple-element.41.ef_ref, ...), custom_call_target="tpu_custom_call" | custom-call | flops 20971520 | bytes 1048576 | tf_op jit(solution)/shard_map/post/pallas_call | solution.py:24
  22.0 4.9 %collective-permute-start.5 = (f32[40,1024]{1,0:T(8,128)S(1)}, f32[40,1024]{1,0:T(8,128)S(1)}, u32[]{:S(2)}, u32[]{:S(2)}) collective-permute-start(f32[40,1024]{1,0:T(8,128)S(1)} %get-tuple-element.55.refs_0_.down_ref), channel_id=1, source_target_pairs={{1,0},{2,1},{3,2},{4,3},{5,4},{6,5},{7,6},{8,7},{9,8},{10,9},{11,1... | collective-permute-start | bytes 491528 | tf_op jit(solution)/shard_map/ppermute | solution.py:528
  27.0 1.8 %pre.5 = (f32[2,2,5,8,1024]{4,3,2,1,0:T(8,128)S(1)}, f32[2,40,1024]{2,1,0:T(8,128)S(1)}) custom-call(f32[2,2,5,8,1024]{4,3,2,1,0:T(8,128)S(1)} %get-tuple-element.56.x_ref, f32[2,2,5,8,1024]{4,3,2,1,0:T(8,128)S(1)} %get-tuple-element.49.f_ref, f32[6,8,1024]{2,1,0:T(8,128)S(1)} %get-tuple-element.39.coef_ref, bf16[160,144]{1,0:T(8,128)(2,1)S(1)} %get-tuple-element.40.own_ref, ...), custom_call_target="tpu_custom_call" | custom-call | flops 41943040 | bytes 1048576 | tf_op jit(solution)/shard_map/pre/pallas_call | solution.py:24
  28.8 1.3 %inner.1.inner_ref = f32[16,4,512]{2,1,0:T(4,128)S(1)} custom-call(f32[5]{0:T(128)S(1)} %copy-done.2, f32[2,2,5,8,1024]{4,3,2,1,0:T(8,128)S(1)} %get-tuple-element.60.x_ref, s32[16,1,512]{2,1,0:T(1,128)S(1)} %bitcast.14, bf16[16,256,512]{2,1,0:T(8,128)(2,1)S(1)} %onehot.1.hot_ref), custom_call_target="tpu_custom_call" | custom-call | flops 20971520 | bytes 1048576 | tf_op jit(solution)/shard_map/inner/pallas_call | solution.py:24
  30.2 1.0 %post.5 = (f32[40,1024]{1,0:T(8,128)S(1)}, f32[40,1024]{1,0:T(8,128)S(1)}, f32[2,8,1024]{2,1,0:T(8,128)S(1)}) custom-call(bf16[200,240]{1,0:T(8,128)(2,1)S(1)} %get-tuple-element.36.plain_ref, bf16[200,240]{1,0:T(8,128)(2,1)S(1)} %get-tuple-element.37.lo_turn_ref, bf16[200,240]{1,0:T(8,128)(2,1)S(1)} %get-tuple-element.38.hi_turn_ref, ...), custom_call_target="tpu_custom_call" | custom-call | flops 20971520 | bytes 1048576 | tf_op jit(solution)/shard_map/post/pallas_call | solution.py:24
  31.2 1.5 %surface.1 = f32[16,4,640]{2,1,0:T(4,128)} custom-call(f32[2,8,1024]{2,1,0:T(8,128)S(1)} %get-tuple-element.58.press_ref, s32[16,1,512]{2,1,0:T(1,128)S(1)} %bitcast.15, bf16[16,256,512]{2,1,0:T(8,128)(2,1)S(1)} %onehot.1.hot_ref, f32[16,4,512]{2,1,0:T(4,128)S(1)} %inner.1.inner_ref, f32[16,1,512]{2,1,0:T(1,128)S(1)} %bitcast.18), custom_call_target="tpu_custom_call" | custom-call | flops 268435456 | bytes 1048576 | tf_op jit(solution)/shard_map/surface/pallas_call | solution.py:24
  32.7 8.6 %all-to-all-start = ((f32[16,4,640]{2,1,0:T(4,128)}), f32[16,4,640]{2,1,0:T(4,128)S(1)}, u32[]{:S(2)}, u32[]{:S(2)}) async-start(f32[16,4,640]{2,1,0:T(4,128)} %surface.1), calls=%async_computation | async-start | bytes 327680 | tf_op jit(solution)/shard_map/all_to_all | solution.py:589
  41.6 1.0 %merge.1 = f32[2,2,5,8,1024]{4,3,2,1,0:T(8,128)} custom-call(f32[2,2,5,8,1024]{4,3,2,1,0:T(8,128)S(1)} %get-tuple-element.60.x_ref, f32[40,1024]{1,0:T(8,128)S(1)} %get-tuple-element.61.down_ref, f32[40,1024]{1,0:T(8,128)S(1)} %get-tuple-element.62.up_ref), custom_call_target="tpu_custom_call" | custom-call | flops 1048576 | bytes 1048576 | tf_op jit(solution)/shard_map/merge/pallas_call | solution.py:24
  42.6 7.7 %all-to-all-done.x_ref = f32[16,4,640]{2,1,0:T(4,128)S(1)} async-done(((f32[16,4,640]{2,1,0:T(4,128)}), f32[16,4,640]{2,1,0:T(4,128)S(1)}, u32[]{:S(2)}, u32[]{:S(2)}) %all-to-all-start) | async-done | bytes 163872 | tf_op jit(solution)/shard_map/all_to_all | solution.py:589
  50.4 1.8 %collective-permute-start.6 = (f32[4,2048]{1,0:T(4,128)S(1)}, f32[4,2048]{1,0:T(4,128)S(1)}, u32[]{:S(2)}, u32[]{:S(2)}) collective-permute-start(f32[4,2048]{1,0:T(4,128)S(1)} %work.1), channel_id=1, source_target_pairs={{0,2},{1,3},{2,0},{3,1},{4,6},{5,7},{6,4},{7,5},{8,10},{9,11},{10,... | collective-permute-start | bytes 98312 | tf_op jit(solution)/shard_map/ppermute | solution.py:598
  53.1 3.9 %all-to-all-start.1 = ((f32[16,4,512]{2,1,0:T(4,128)}), f32[16,4,512]{2,1,0:T(4,128)S(1)}, u32[]{:S(2)}, u32[]{:S(2)}) async-start(f32[16,4,512]{2,1,0:T(4,128)} %phases.1), calls=%async_computation.1 | async-start | bytes 262144 | tf_op jit(solution)/shard_map/all_to_all | solution.py:612
  57.1 1.4 %collective-permute-start.7 = (f32[4,128]{1,0:T(4,128)S(1)}, f32[4,128]{1,0:T(4,128)S(1)}, u32[]{:S(2)}, u32[]{:S(2)}) collective-permute-start(f32[4,128]{1,0:T(4,128)S(1)} %slice_add_fusion), channel_id=1, source_target_pairs={{0,4},{1,5},{2,6},{3,7},{4,0},{5,1},{6,2},{7,3},{8,12},{9,13},{10,... | collective-permute-start | bytes 6152 | tf_op jit(solution)/shard_map/ppermute | solution.py:598
  58.5 4.0 %collective-permute-start.8 = (f32[4,128]{1,0:T(4,128)S(1)}, f32[4,128]{1,0:T(4,128)S(1)}, u32[]{:S(2)}, u32[]{:S(2)}) collective-permute-start(f32[4,128]{1,0:T(4,128)S(1)} %slice_add_fusion), channel_id=1, source_target_pairs={{0,8},{1,9},{2,10},{3,11},{4,12},{5,13},{6,14},{7,15},{8,0},{9,1},... | collective-permute-start | bytes 6152 | tf_op jit(solution)/shard_map/ppermute | solution.py:598
  62.5 1.0 %collective-permute-done.8 = f32[4,128]{1,0:T(4,128)S(1)} collective-permute-done((f32[4,128]{1,0:T(4,128)S(1)}, f32[4,128]{1,0:T(4,128)S(1)}, u32[]{:S(2)}, u32[]{:S(2)}) %collective-permute-start.8) | collective-permute-done | bytes 2080 | tf_op jit(solution)/shard_map/ppermute | solution.py:598
  63.5 2.9 %collective-permute-done.9 = f32[4,128]{1,0:T(4,128)S(1)} collective-permute-done((f32[4,128]{1,0:T(4,128)S(1)}, f32[4,128]{1,0:T(4,128)S(1)}, u32[]{:S(2)}, u32[]{:S(2)}) %collective-permute-start.9) | collective-permute-done | bytes 2080 | tf_op jit(solution)/shard_map/ppermute | solution.py:598
  66.4 0.9 %collective-permute-start.10 = (f32[4,128]{1,0:T(4,128)S(1)}, f32[4,128]{1,0:T(4,128)S(1)}, u32[]{:S(2)}, u32[]{:S(2)}) collective-permute-start(f32[4,128]{1,0:T(4,128)S(1)} %add_add_fusion), channel_id=1, source_target_pairs={{0,1},{1,0},{2,3},{3,2},{4,5},{5,4},{6,7},{7,6},{8,9},{9,8},{10,11... | collective-permute-start | bytes 6152 | tf_op jit(solution)/shard_map/ppermute | solution.py:598
  (42 shorter events, 7.2 us)
Async XLA Ops:
  0.6 17.0 %copy-start = (s32[8192]{0:T(1024)S(1)}, s32[8192]{0:T(1024)}, u32[]{:S(2)}) copy-start(s32[8192]{0:T(1024)} %param.17) | copy-start | bytes 98308
  1.9 9.3 %collective-permute-start = (f32[66,1024]{1,0:T(8,128)S(1)}, f32[66,1024]{1,0:T(8,128)S(1)}, u32[]{:S(2)}, u32[]{:S(2)}) collective-permute-start(f32[66,1024]{1,0:T(8,128)S(1)} %get-tuple-element.43.up_ref), channel_id=1, source_target_pairs={{0,1},{1,2},{2,3},{3,4},{4,5},{5,6},{6,7},{7,8},{8,9},{9,10},{10,1... | collective-permute-start | bytes 811016 | tf_op jit(solution)/shard_map/ppermute | solution.py:527
  4.6 8.8 %collective-permute-start.1 = (f32[66,1024]{1,0:T(8,128)S(1)}, f32[66,1024]{1,0:T(8,128)S(1)}, u32[]{:S(2)}, u32[]{:S(2)}) collective-permute-start(f32[66,1024]{1,0:T(8,128)S(1)} %get-tuple-element.44.down_ref), channel_id=1, source_target_pairs={{1,0},{2,1},{3,2},{4,3},{5,4},{6,5},{7,6},{8,7},{9,8},{10,9},{11,1... | collective-permute-start | bytes 811016 | tf_op jit(solution)/shard_map/ppermute | solution.py:528
  14.5 5.7 %collective-permute-start.2 = (f32[40,1024]{1,0:T(8,128)S(1)}, f32[40,1024]{1,0:T(8,128)S(1)}, u32[]{:S(2)}, u32[]{:S(2)}) collective-permute-start(f32[40,1024]{1,0:T(8,128)S(1)} %get-tuple-element.46.refs_1_.up_ref), channel_id=1, source_target_pairs={{0,1},{1,2},{2,3},{3,4},{4,5},{5,6},{6,7},{7,8},{8,9},{9,10},{10,1... | collective-permute-start | bytes 491528 | tf_op jit(solution)/shard_map/ppermute | solution.py:527
  14.6 6.4 %collective-permute-start.3 = (f32[40,1024]{1,0:T(8,128)S(1)}, f32[40,1024]{1,0:T(8,128)S(1)}, u32[]{:S(2)}, u32[]{:S(2)}) collective-permute-start(f32[40,1024]{1,0:T(8,128)S(1)} %get-tuple-element.47.refs_0_.down_ref), channel_id=1, source_target_pairs={{1,0},{2,1},{3,2},{4,3},{5,4},{6,5},{7,6},{8,7},{9,8},{10,9},{11,1... | collective-permute-start | bytes 491528 | tf_op jit(solution)/shard_map/ppermute | solution.py:528
  17.6 9.3 %copy-start.3 = (s32[32]{0:T(128)S(1)}, s32[32]{0:T(128)}, u32[]{:S(2)}) copy-start(s32[32]{0:T(128)} %param.19) | copy-start | bytes 388
  18.4 10.4 %copy-start.2 = (f32[5]{0:T(128)S(1)}, f32[5]{0:T(128)}, u32[]{:S(2)}) copy-start(f32[5]{0:T(128)} %pw_ref.1) | copy-start | bytes 64
  21.9 8.2 %collective-permute-start.4 = (f32[40,1024]{1,0:T(8,128)S(1)}, f32[40,1024]{1,0:T(8,128)S(1)}, u32[]{:S(2)}, u32[]{:S(2)}) collective-permute-start(f32[40,1024]{1,0:T(8,128)S(1)} %get-tuple-element.54.refs_1_.up_ref), channel_id=1, source_target_pairs={{0,1},{1,2},{2,3},{3,4},{4,5},{5,6},{6,7},{7,8},{8,9},{9,10},{10,1... | collective-permute-start | bytes 491528 | tf_op jit(solution)/shard_map/ppermute | solution.py:527
  22.0 8.2 %collective-permute-start.5 = (f32[40,1024]{1,0:T(8,128)S(1)}, f32[40,1024]{1,0:T(8,128)S(1)}, u32[]{:S(2)}, u32[]{:S(2)}) collective-permute-start(f32[40,1024]{1,0:T(8,128)S(1)} %get-tuple-element.55.refs_0_.down_ref), channel_id=1, source_target_pairs={{1,0},{2,1},{3,2},{4,3},{5,4},{6,5},{7,6},{8,7},{9,8},{10,9},{11,1... | collective-permute-start | bytes 491528 | tf_op jit(solution)/shard_map/ppermute | solution.py:528
  28.8 2.4 %copy-start.1 = (f32[8192]{0:T(1024)S(1)}, f32[8192]{0:T(1024)}, u32[]{:S(2)}) copy-start(f32[8192]{0:T(1024)} %param.18) | copy-start | bytes 98308
  32.7 17.6 %all-to-all-start = ((f32[16,4,640]{2,1,0:T(4,128)}), f32[16,4,640]{2,1,0:T(4,128)S(1)}, u32[]{:S(2)}, u32[]{:S(2)}) async-start(f32[16,4,640]{2,1,0:T(4,128)} %surface.1), calls=%async_computation | async-start | bytes 327680 | tf_op jit(solution)/shard_map/all_to_all | solution.py:589
  50.4 6.6 %collective-permute-start.6 = (f32[4,2048]{1,0:T(4,128)S(1)}, f32[4,2048]{1,0:T(4,128)S(1)}, u32[]{:S(2)}, u32[]{:S(2)}) collective-permute-start(f32[4,2048]{1,0:T(4,128)S(1)} %work.1), channel_id=1, source_target_pairs={{0,2},{1,3},{2,0},{3,1},{4,6},{5,7},{6,4},{7,5},{8,10},{9,11},{10,... | collective-permute-start | bytes 98312 | tf_op jit(solution)/shard_map/ppermute | solution.py:598
  53.1 15.0 %all-to-all-start.1 = ((f32[16,4,512]{2,1,0:T(4,128)}), f32[16,4,512]{2,1,0:T(4,128)S(1)}, u32[]{:S(2)}, u32[]{:S(2)}) async-start(f32[16,4,512]{2,1,0:T(4,128)} %phases.1), calls=%async_computation.1 | async-start | bytes 262144 | tf_op jit(solution)/shard_map/all_to_all | solution.py:612
  57.1 5.4 %collective-permute-start.7 = (f32[4,128]{1,0:T(4,128)S(1)}, f32[4,128]{1,0:T(4,128)S(1)}, u32[]{:S(2)}, u32[]{:S(2)}) collective-permute-start(f32[4,128]{1,0:T(4,128)S(1)} %slice_add_fusion), channel_id=1, source_target_pairs={{0,4},{1,5},{2,6},{3,7},{4,0},{5,1},{6,2},{7,3},{8,12},{9,13},{10,... | collective-permute-start | bytes 6152 | tf_op jit(solution)/shard_map/ppermute | solution.py:598
  58.5 5.0 %collective-permute-start.8 = (f32[4,128]{1,0:T(4,128)S(1)}, f32[4,128]{1,0:T(4,128)S(1)}, u32[]{:S(2)}, u32[]{:S(2)}) collective-permute-start(f32[4,128]{1,0:T(4,128)S(1)} %slice_add_fusion), channel_id=1, source_target_pairs={{0,8},{1,9},{2,10},{3,11},{4,12},{5,13},{6,14},{7,15},{8,0},{9,1},... | collective-permute-start | bytes 6152 | tf_op jit(solution)/shard_map/ppermute | solution.py:598
  62.5 3.9 %collective-permute-start.9 = (f32[4,128]{1,0:T(4,128)S(1)}, f32[4,128]{1,0:T(4,128)S(1)}, u32[]{:S(2)}, u32[]{:S(2)}) collective-permute-start(f32[4,128]{1,0:T(4,128)S(1)} %slice_add_fusion), channel_id=1, source_target_pairs={{0,12},{1,13},{2,14},{3,15},{4,8},{5,9},{6,10},{7,11},{8,4},{9,5},... | collective-permute-start | bytes 6152 | tf_op jit(solution)/shard_map/ppermute | solution.py:598
  66.4 1.7 %collective-permute-start.10 = (f32[4,128]{1,0:T(4,128)S(1)}, f32[4,128]{1,0:T(4,128)S(1)}, u32[]{:S(2)}, u32[]{:S(2)}) collective-permute-start(f32[4,128]{1,0:T(4,128)S(1)} %add_add_fusion), channel_id=1, source_target_pairs={{0,1},{1,0},{2,3},{3,2},{4,5},{5,4},{6,7},{7,6},{8,9},{9,8},{10,11... | collective-permute-start | bytes 6152 | tf_op jit(solution)/shard_map/ppermute | solution.py:598

commit v4 on v3

--- a/solution.py
+++ b/solution.py
@@ -243,7 +243,8 @@
     if first:
         rot_ref, down_out, up_out, gf_ref, gcoef_ref = refs
     elif last:
-        gf_ref, gcoef_ref, pw_ref, down_out, up_out, press_ref = refs
+        gf_ref, gcoef_ref, pw_ref, idx_ref, hot_ref, inner_ref, weight_ref, down_out, up_out, surface_ref = refs
+        presses = []
     else:
         gf_ref, gcoef_ref, down_out, up_out = refs
     cells = lo_ref.shape[-1]
@@ -307,7 +308,9 @@
             press = pw_ref[0:1, :] * new[0:8]
             for v in range(1, 5):
                 press = press + pw_ref[v : v + 1, :] * new[8 * v : 8 * v + 8]
-            press_ref[h] = press
+            presses.append(press)
+    if last:
+        surface(presses, idx_ref, hot_ref, inner_ref, weight_ref, surface_ref)
 
 
 def inner_kernel(pw_ref, x_ref, idx_ref, hot_ref, out_ref, table_ref):
@@ -320,9 +323,9 @@
     kept = (row >= 2) & (row < 6)
     press = []
     for i in range(4):
-        value = pw_ref[0] * x_ref[i // 2, i % 2, 0]
+        value = pw_ref[0:1, :] * x_ref[i // 2, i % 2, 0]
         for v in range(1, 5):
-            value = value + pw_ref[v] * x_ref[i // 2, i % 2, v]
+            value = value + pw_ref[v : v + 1, :] * x_ref[i // 2, i % 2, v]
         value = jnp.where(kept, value, 0.0)
         press.append(value)
     for i in range(2):
@@ -355,13 +358,13 @@
     lax.fori_loop(0, parts, one, 0, unroll=16)
 
 
-def surface_kernel(press_ref, idx_ref, hot_ref, inner_ref, weight_ref, out_ref):
-    cells = press_ref.shape[-1]
+def surface(presses, idx_ref, hot_ref, inner_ref, weight_ref, out_ref):
+    cells = presses[0].shape[-1]
     chunk = idx_ref.shape[-1]
     parts = idx_ref.shape[0]
     groups = cells // WIDE
     half = 16 * groups
-    tiles = [press_ref[h, :, g * WIDE : (g + 1) * WIDE] for h in range(2) for g in range(groups)]
+    tiles = [x[:, g * WIDE : (g + 1) * WIDE] for x in presses for g in range(groups)]
     value = jnp.concatenate(tiles, axis=0)
     high = value.astype(jnp.bfloat16)
     low = (value - high.astype(jnp.float32)).astype(jnp.bfloat16)
@@ -380,13 +383,16 @@
                 total = jnp.where(top == place + (6 * h * groups + g), found[at : at + 8], total)
         total = total + pltpu.roll(total, 6, 0)
         values = inner_ref[d] + jnp.concatenate([total[0:2], total[4:6]], axis=0)
-        out_ref[d, :, 0:chunk] = values
+        for p in range(2):
+            out_ref[d, :, p * chunk : (p + 1) * chunk] = values[2 * p : 2 * p + 2]
         return work + values * weight_ref[d]
 
     work = lax.fori_loop(0, parts, one, jnp.zeros((4, chunk), jnp.float32), unroll=16)
     work = jnp.broadcast_to(jnp.sum(work, axis=1, keepdims=True), (4, LANES))
+    lane = lax.broadcasted_iota(jnp.int32, (2, LANES), 1)
+    work = jnp.where(lane < LANES // 2, work[0:2], work[2:4])
     for d in range(parts):
-        out_ref[d, :, chunk : chunk + LANES] = work
+        out_ref[d, :, 2 * chunk : 2 * chunk + LANES] = work
 
 
 def merge_kernel(x_ref, down_ref, up_ref, out_ref):
@@ -399,33 +405,35 @@
                 out_ref[p, c, v, to : to + 1, :] = ref[at : at + 1, :]
 
 
-def work_kernel(table_ref, x_ref, work_ref):
-    chunk = x_ref.shape[-1] - LANES
-    rows = jnp.concatenate([x_ref[d, :, chunk:] for d in range(x_ref.shape[0])], axis=0)
-    work = jnp.dot(
-        table_ref[...], rows, precision=HIGHEST, preferred_element_type=jnp.float32
-    )
+def phase_kernel(table_ref, work_table_ref, x_ref, out_ref, work_ref):
+    parts = x_ref.shape[0]
+    chunk = out_ref.shape[-1]
+    rows = jnp.concatenate([x_ref[d, :, 2 * chunk :] for d in range(parts)], axis=0)
+    work = [
+        jnp.dot(work_table_ref[p], rows, precision=HIGHEST, preferred_element_type=jnp.float32)
+        for p in range(2)
+    ]
+    half = LANES // 2
+    work = jnp.broadcast_to(work[0][:, 0:1] + work[1][:, half : half + 1], (4, LANES))
     for i in range(work_ref.shape[1] // LANES):
         work_ref[:, i * LANES : (i + 1) * LANES] = work
-
-
-def phase_kernel(table_ref, x_ref, out_ref):
-    parts = x_ref.shape[0]
-    chunk = out_ref.shape[-1]
     table = table_ref[...]
     high = table.astype(jnp.bfloat16).astype(jnp.float32)
     table = jnp.concatenate([high, high, table - high], axis=1).astype(jnp.bfloat16)
-    rows = jnp.concatenate([x_ref[d, :, 0:chunk] for d in range(parts)], axis=0)
+    rows = jnp.concatenate(
+        [x_ref[d, :, p * chunk : (p + 1) * chunk] for d in range(parts) for p in range(2)], axis=0
+    )
     y = multiply(table, rows)
     for d in range(parts):
-        out_ref[d] = y[4 * d : 4 * d + 4]
+        for m in range(2):
+            out_ref[d, m] = y[4 * d + 2 * m : 4 * d + 2 * m + 2]
 
 
 def place_kernel(x_ref, work_ref, out_ref, modal_ref):
     chunk = x_ref.shape[-1]
     for d in range(x_ref.shape[0]):
         for m in range(2):
-            out_ref[m, :, d * chunk : (d + 1) * chunk] = x_ref[d, 2 * m : 2 * m + 2, :]
+            out_ref[m, :, d * chunk : (d + 1) * chunk] = x_ref[d, m]
     lane = lax.broadcasted_iota(jnp.int32, (1, 2), 1)
     for m in range(2):
         re = jnp.broadcast_to(work_ref[2 * m : 2 * m + 1, 0:1], (1, 2))
@@ -520,6 +528,7 @@
         [idx],
         [VMEM],
     )
+    pressure_rows = jnp.broadcast_to(pressure_weights[:, None], (5, cells))
     steps = ITERS // WIDTH
     edge_shape = (2, 5, 8, cells)
     for step in range(steps):
@@ -556,11 +565,17 @@
                 [((devices, 4, chunk), f32)],
                 [pltpu.VMEM((128, WIDE), f32)],
                 20 << 20,
-                [pressure_weights, state, idx, hot],
-                [SMEM] + [VMEM] * 3,
+                [pressure_rows, state, idx, hot],
+                [VMEM] * 4,
             )
-            outs += [((2, 8, cells), f32)]
-            operands += [jnp.broadcast_to(pressure_weights[:, None], (5, cells))]
+            outs += [((devices, 2, 2 * chunk + LANES), f32)]
+            operands += [
+                pressure_rows,
+                idx,
+                hot,
+                inner,
+                modal_weights.reshape(devices, 1, chunk),
+            ]
         down, up, *got = call(
             functools.partial(post_kernel, first, last),
             "post",
@@ -572,16 +587,7 @@
         )
         if first:
             ghosts = got
-    (press,) = got
-    (mine,) = call(
-        surface_kernel,
-        "surface",
-        [((devices, 4, chunk + LANES), f32)],
-        [],
-        1 << 28,
-        [press, idx, hot, inner, modal_weights.reshape(devices, 1, chunk)],
-        [VMEM] * 5,
-    )
+    (mine,) = got
     (state,) = call(
         merge_kernel, "merge", [(previous.shape, f32)], [], 1 << 20, [state, down, up], [VMEM] * 3
     )
@@ -589,10 +595,16 @@
     every = lax.all_to_all(mine, "phase", 0, 0, tiled=True)
     every, state = lax.optimization_barrier((every, state))
     own_table = lax.dynamic_slice_in_dim(table, lax.axis_index("phase") * 4, 4)
-    (work,) = call(
-        work_kernel, "work", [((4, 2048), f32)], [], 1 << 16, [own_table, every], [VMEM] * 2
-    )
-    work, ready = lax.optimization_barrier((work, every))
+    work_table = own_table.reshape(4, devices, 2, 2).transpose(2, 0, 1, 3).reshape(2, 4, -1)
+    turned, work = call(
+        phase_kernel,
+        "phases",
+        [((devices, 2, 2, chunk), f32), ((4, 2048), f32)],
+        [],
+        1 << 24,
+        [table, work_table, every],
+        [VMEM] * 3,
+    )
 
     def across(bits):
         return lax.ppermute(work, "space", [(i, i ^ bits) for i in range(count)])
@@ -600,15 +612,6 @@
     work = (work + across(2))[:, :LANES]
     work = (work + across(4)) + (across(8) + across(12))
     work = work + across(1)
-    (turned,) = call(
-        phase_kernel,
-        "phases",
-        [((devices, 4, chunk), f32)],
-        [],
-        1 << 24,
-        [table, ready],
-        [VMEM] * 2,
-    )
     blocks = lax.all_to_all(turned, "phase", 0, 0, tiled=True)
     influence, modal_work = call(
         place_kernel,

time: 70.1 us -> 69.8 us (level)
    pallas_call x15 -> x13, Pallas kernels: 18.3 us -> 17.6 us  [call(): pl.pallas_call(kernel, name=name, out_shape=[jax.ShapeDtypeStruct(s, d) f...]
  transfers between devices with their start and end apart: 13 -> 13, of which waited for: 6 -> 6; matrix products, arithmetic and copies ran while one was open for 3% -> 3% of each run, Pallas kernels for 17% -> 15%
where the time goes in v4:
time: 69.8 us; the launch traced here: 68.8 us
  starting transfers between devices  32.8 us (47%)
  Pallas kernels  17.6 us (25%)
  waiting for transfers between devices  15.1 us (22%)
  local copies, waits for them, and re-layouts  1.49 us (2%)
  other arithmetic  0.9 us (1%)
  between operations  0.87 us (1%)
    pallas_call x13, Pallas kernels, call(): pl.pallas_call(kernel, name=name, out_shape=[jax.ShapeDtypeStruct(s, d) f...  17.6 us
    all_to_all x1, starting transfers between devices, per_device(): every = lax.all_to_all(mine, 'phase', 0, 0, tiled=True)  9.12 us
    ppermute x3, starting transfers between devices, per_device(): hi = lax.ppermute(down, 'space', backward)  8.62 us
    ppermute x5, starting transfers between devices, across(): return lax.ppermute(work, 'space', [(i, i ^ bits) for i in range(count)])  8.48 us
    all_to_all x1, waiting for transfers between devices, per_device(): every = lax.all_to_all(mine, 'phase', 0, 0, tiled=True)  7.49 us
    ppermute x5, waiting for transfers between devices, across(): return lax.ppermute(work, 'space', [(i, i ^ bits) for i in range(count)])  4.76 us
    all_to_all x1, starting transfers between devices, per_device(): blocks = lax.all_to_all(turned, 'phase', 0, 0, tiled=True)  3.74 us
    ppermute x3, starting transfers between devices, per_device(): lo = lax.ppermute(up, 'space', forward)  2.84 us
  transfers between devices with their start and end apart: 13, of which 6 were waited for; matrix products, arithmetic and copies ran while one was open for 3% of the time, Pallas kernels for 15%

profile of v4, /device:TPU:1, one launch (start us, length us, event | category | flops | bytes accessed | tf_op | source)
XLA Modules:
  0.0 68.8 jit_solution(15623003268150028018)
XLA Ops:
  0.6 1.2 %pack.1 = (f32[6,8,1024]{2,1,0:T(8,128)S(1)}, f32[66,1024]{1,0:T(8,128)S(1)}, f32[66,1024]{1,0:T(8,128)S(1)}) custom-call(f32[2,2,5,8,1024]{4,3,2,1,0:T(8,128)} %x_ref.1, f32[2,2,5,8,1024]{4,3,2,1,0:T(8,128)} %f_ref.1, f32[4,8,1024]{2,1,0:T(8,128)} %cpl_hbm.1, f32[8,1024]{1,0:T(8,128)} %diag_hbm.1, f32[8,1024]{1,0:T(8,128)} %inert_hbm.1), custom_call_target="tpu_custom_call" | custom-call | flops 1048576 | bytes 1048576 | tf_op jit(solution)/shard_map/pack/pallas_call | solution.py:24
  1.9 2.7 %collective-permute-start = (f32[66,1024]{1,0:T(8,128)S(1)}, f32[66,1024]{1,0:T(8,128)S(1)}, u32[]{:S(2)}, u32[]{:S(2)}) collective-permute-start(f32[66,1024]{1,0:T(8,128)S(1)} %get-tuple-element.43.up_ref), channel_id=1, source_target_pairs={{0,1},{1,2},{2,3},{3,4},{4,5},{5,6},{6,7},{7,8},{8,9},{9,10},{10,1... | collective-permute-start | bytes 811016 | tf_op jit(solution)/shard_map/ppermute | solution.py:536
  7.0 1.0 %tables.1 = (bf16[160,144]{1,0:T(8,128)(2,1)S(1)}, bf16[200,240]{1,0:T(8,128)(2,1)S(1)}, bf16[200,240]{1,0:T(8,128)(2,1)S(1)}, bf16[200,240]{1,0:T(8,128)(2,1)S(1)}) custom-call(f32[4,5,5]{2,1,0:T(8,128)S(1)} %copy.22.jac_ref, f32[8]{0:T(128)S(1)} %reshape.148.rot_ref), custom_call_target="tpu_custom_call" | custom-call | flops 1048576 | bytes 1048576 | tf_op jit(solution)/shard_map/tables/pallas_call | solution.py:24
  8.0 3.2 %pre.3 = (f32[2,2,5,8,1024]{4,3,2,1,0:T(8,128)S(1)}, f32[2,40,1024]{2,1,0:T(8,128)S(1)}, f32[2,5,8,1024]{3,2,1,0:T(8,128)S(1)}, f32[2,6,8,1024]{3,2,1,0:T(8,128)S(1)}, f32[2,2,5,8,1024]{4,3,2,1,0:T(8,128)S(1)}) custom-call(f32[2,2,5,8,1024]{4,3,2,1,0:T(8,128)} %x_ref.1, f32[2,2,5,8,1024]{4,3,2,1,0:T(8,128)} %f_ref.1, ...), custom_call_target="tpu_custom_call" | custom-call | flops 41943040 | bytes 1048576 | tf_op jit(solution)/shard_map/pre/pallas_call | solution.py:24
  11.2 2.2 %collective-permute-done.1.hi_ref = f32[66,1024]{1,0:T(8,128)S(1)} collective-permute-done((f32[66,1024]{1,0:T(8,128)S(1)}, f32[66,1024]{1,0:T(8,128)S(1)}, u32[]{:S(2)}, u32[]{:S(2)}) %collective-permute-start.1) | collective-permute-done | bytes 270368 | tf_op jit(solution)/shard_map/ppermute | solution.py:537
  13.5 1.0 %post.3 = (f32[40,1024]{1,0:T(8,128)S(1)}, f32[40,1024]{1,0:T(8,128)S(1)}, f32[2,5,8,1024]{3,2,1,0:T(8,128)S(1)}, f32[2,6,8,1024]{3,2,1,0:T(8,128)S(1)}) custom-call(bf16[200,240]{1,0:T(8,128)(2,1)S(1)} %get-tuple-element.36.plain_ref, bf16[200,240]{1,0:T(8,128)(2,1)S(1)} %get-tuple-element.37.lo_turn_ref, ...), custom_call_target="tpu_custom_call" | custom-call | flops 20971520 | bytes 1048576 | tf_op jit(solution)/shard_map/post/pallas_call | solution.py:24
  14.6 3.0 %collective-permute-start.3 = (f32[40,1024]{1,0:T(8,128)S(1)}, f32[40,1024]{1,0:T(8,128)S(1)}, u32[]{:S(2)}, u32[]{:S(2)}) collective-permute-start(f32[40,1024]{1,0:T(8,128)S(1)} %get-tuple-element.47.refs_0_.down_ref), channel_id=1, source_target_pairs={{1,0},{2,1},{3,2},{4,3},{5,4},{6,5},{7,6},{8,7},{9,8},{10,9},{11,1... | collective-permute-start | bytes 491528 | tf_op jit(solution)/shard_map/ppermute | solution.py:537
  18.4 1.8 %pre.4 = (f32[2,2,5,8,1024]{4,3,2,1,0:T(8,128)S(1)}, f32[2,40,1024]{2,1,0:T(8,128)S(1)}) custom-call(f32[2,2,5,8,1024]{4,3,2,1,0:T(8,128)S(1)} %get-tuple-element.48.x_ref, f32[2,2,5,8,1024]{4,3,2,1,0:T(8,128)S(1)} %get-tuple-element.49.f_ref, f32[6,8,1024]{2,1,0:T(8,128)S(1)} %get-tuple-element.39.coef_ref, bf16[160,144]{1,0:T(8,128)(2,1)S(1)} %get-tuple-element.40.own_ref, ...), custom_call_target="tpu_custom_call" | custom-call | flops 41943040 | bytes 1048576 | tf_op jit(solution)/shard_map/pre/pallas_call | solution.py:24
  20.9 0.9 %post.4 = (f32[40,1024]{1,0:T(8,128)S(1)}, f32[40,1024]{1,0:T(8,128)S(1)}) custom-call(bf16[200,240]{1,0:T(8,128)(2,1)S(1)} %get-tuple-element.36.plain_ref, bf16[200,240]{1,0:T(8,128)(2,1)S(1)} %get-tuple-element.37.lo_turn_ref, bf16[200,240]{1,0:T(8,128)(2,1)S(1)} %get-tuple-element.38.hi_turn_ref, f32[2,5,8,1024]{3,2,1,0:T(8,128)S(1)} %get-tuple-element.41.ef_ref, ...), custom_call_target="tpu_custom_call" | custom-call | flops 20971520 | bytes 1048576 | tf_op jit(solution)/shard_map/post/pallas_call | solution.py:24
  22.0 4.9 %collective-permute-start.5 = (f32[40,1024]{1,0:T(8,128)S(1)}, f32[40,1024]{1,0:T(8,128)S(1)}, u32[]{:S(2)}, u32[]{:S(2)}) collective-permute-start(f32[40,1024]{1,0:T(8,128)S(1)} %get-tuple-element.55.refs_0_.down_ref), channel_id=1, source_target_pairs={{1,0},{2,1},{3,2},{4,3},{5,4},{6,5},{7,6},{8,7},{9,8},{10,9},{11,1... | collective-permute-start | bytes 491528 | tf_op jit(solution)/shard_map/ppermute | solution.py:537
  27.0 1.8 %pre.5 = (f32[2,2,5,8,1024]{4,3,2,1,0:T(8,128)S(1)}, f32[2,40,1024]{2,1,0:T(8,128)S(1)}) custom-call(f32[2,2,5,8,1024]{4,3,2,1,0:T(8,128)S(1)} %get-tuple-element.56.x_ref, f32[2,2,5,8,1024]{4,3,2,1,0:T(8,128)S(1)} %get-tuple-element.49.f_ref, f32[6,8,1024]{2,1,0:T(8,128)S(1)} %get-tuple-element.39.coef_ref, bf16[160,144]{1,0:T(8,128)(2,1)S(1)} %get-tuple-element.40.own_ref, ...), custom_call_target="tpu_custom_call" | custom-call | flops 41943040 | bytes 1048576 | tf_op jit(solution)/shard_map/pre/pallas_call | solution.py:24
  29.7 2.4 %post.5 = (f32[40,1024]{1,0:T(8,128)S(1)}, f32[40,1024]{1,0:T(8,128)S(1)}, f32[16,2,1152]{2,1,0:T(2,128)}) custom-call(bf16[200,240]{1,0:T(8,128)(2,1)S(1)} %get-tuple-element.36.plain_ref, bf16[200,240]{1,0:T(8,128)(2,1)S(1)} %get-tuple-element.37.lo_turn_ref, bf16[200,240]{1,0:T(8,128)(2,1)S(1)} %get-tuple-element.38.hi_turn_ref, ...), custom_call_target="tpu_custom_call" | custom-call | flops 20971520 | bytes 1048576 | tf_op jit(solution)/shard_map/post/pallas_call | solution.py:24
  32.1 9.1 %all-to-all-start = ((f32[16,2,1152]{2,1,0:T(2,128)}), f32[16,2,1152]{2,1,0:T(2,128)S(1)}, u32[]{:S(2)}, u32[]{:S(2)}) async-start(f32[16,2,1152]{2,1,0:T(2,128)} %get-tuple-element.60), calls=%async_computation | async-start | bytes 294912 | tf_op jit(solution)/shard_map/all_to_all | solution.py:595
  41.7 1.0 %merge.1 = f32[2,2,5,8,1024]{4,3,2,1,0:T(8,128)} custom-call(f32[2,2,5,8,1024]{4,3,2,1,0:T(8,128)S(1)} %get-tuple-element.59.x_ref, f32[40,1024]{1,0:T(8,128)S(1)} %get-tuple-element.61.down_ref, f32[40,1024]{1,0:T(8,128)S(1)} %get-tuple-element.62.up_ref), custom_call_target="tpu_custom_call" | custom-call | flops 1048576 | bytes 1048576 | tf_op jit(solution)/shard_map/merge/pallas_call | solution.py:24
  42.7 7.5 %all-to-all-done.x_ref = f32[16,2,1152]{2,1,0:T(2,128)S(1)} async-done(((f32[16,2,1152]{2,1,0:T(2,128)}), f32[16,2,1152]{2,1,0:T(2,128)S(1)}, u32[]{:S(2)}, u32[]{:S(2)}) %all-to-all-start) | async-done | bytes 147488 | tf_op jit(solution)/shard_map/all_to_all | solution.py:595
  50.2 0.9 %phases.1 = (f32[16,2,2,512]{3,2,1,0:T(2,128)}, f32[4,2048]{1,0:T(4,128)S(1)}) custom-call(f32[64,64]{1,0:T(8,128)S(1)} %bitcast.21, f32[2,4,32]{2,1,0:T(4,128)S(1)} %copy.28.work_table_ref, f32[16,2,1152]{2,1,0:T(2,128)S(1)} %all-to-all-done.x_ref), custom_call_target="tpu_custom_call" | custom-call | flops 16777216 | bytes 1048576 | tf_op jit(solution)/shard_map/phases/pallas_call | solution.py:24
  51.1 1.8 %collective-permute-start.6 = (f32[4,2048]{1,0:T(4,128)S(1)}, f32[4,2048]{1,0:T(4,128)S(1)}, u32[]{:S(2)}, u32[]{:S(2)}) collective-permute-start(f32[4,2048]{1,0:T(4,128)S(1)} %get-tuple-element.66), channel_id=1, source_target_pairs={{0,2},{1,3},{2,0},{3,1},{4,6},{5,7},{6,4},{7,5},{8,10},{9,11},{10,... | collective-permute-start | bytes 98312 | tf_op jit(solution)/shard_map/ppermute | solution.py:610
  52.9 3.7 %all-to-all-start.1 = ((f32[16,2,2,512]{3,2,1,0:T(2,128)}), f32[16,2,2,512]{3,2,1,0:T(2,128)S(1)}, u32[]{:S(2)}, u32[]{:S(2)}) async-start(f32[16,2,2,512]{3,2,1,0:T(2,128)} %get-tuple-element.65), calls=%async_computation.1 | async-start | bytes 262144 | tf_op jit(solution)/shard_map/all_to_all | solution.py:615
  56.7 1.4 %collective-permute-start.7 = (f32[4,128]{1,0:T(4,128)S(1)}, f32[4,128]{1,0:T(4,128)S(1)}, u32[]{:S(2)}, u32[]{:S(2)}) collective-permute-start(f32[4,128]{1,0:T(4,128)S(1)} %slice_add_fusion), channel_id=1, source_target_pairs={{0,4},{1,5},{2,6},{3,7},{4,0},{5,1},{6,2},{7,3},{8,12},{9,13},{10,... | collective-permute-start | bytes 6152 | tf_op jit(solution)/shard_map/ppermute | solution.py:610
  58.0 4.0 %collective-permute-start.8 = (f32[4,128]{1,0:T(4,128)S(1)}, f32[4,128]{1,0:T(4,128)S(1)}, u32[]{:S(2)}, u32[]{:S(2)}) collective-permute-start(f32[4,128]{1,0:T(4,128)S(1)} %slice_add_fusion), channel_id=1, source_target_pairs={{0,8},{1,9},{2,10},{3,11},{4,12},{5,13},{6,14},{7,15},{8,0},{9,1},... | collective-permute-start | bytes 6152 | tf_op jit(solution)/shard_map/ppermute | solution.py:610
  62.0 1.0 %collective-permute-done.8 = f32[4,128]{1,0:T(4,128)S(1)} collective-permute-done((f32[4,128]{1,0:T(4,128)S(1)}, f32[4,128]{1,0:T(4,128)S(1)}, u32[]{:S(2)}, u32[]{:S(2)}) %collective-permute-start.8) | collective-permute-done | bytes 2080 | tf_op jit(solution)/shard_map/ppermute | solution.py:610
  63.0 2.9 %collective-permute-done.9 = f32[4,128]{1,0:T(4,128)S(1)} collective-permute-done((f32[4,128]{1,0:T(4,128)S(1)}, f32[4,128]{1,0:T(4,128)S(1)}, u32[]{:S(2)}, u32[]{:S(2)}) %collective-permute-start.9) | collective-permute-done | bytes 2080 | tf_op jit(solution)/shard_map/ppermute | solution.py:610
  66.0 1.3 %collective-permute-start.10 = (f32[4,128]{1,0:T(4,128)S(1)}, f32[4,128]{1,0:T(4,128)S(1)}, u32[]{:S(2)}, u32[]{:S(2)}) collective-permute-start(f32[4,128]{1,0:T(4,128)S(1)} %add_add_fusion), channel_id=1, source_target_pairs={{0,1},{1,0},{2,3},{3,2},{4,5},{5,4},{6,7},{7,6},{8,9},{9,8},{10,11... | collective-permute-start | bytes 6152 | tf_op jit(solution)/shard_map/ppermute | solution.py:610
  67.3 0.8 %collective-permute-done.10 = f32[4,128]{1,0:T(4,128)S(1)} collective-permute-done((f32[4,128]{1,0:T(4,128)S(1)}, f32[4,128]{1,0:T(4,128)S(1)}, u32[]{:S(2)}, u32[]{:S(2)}) %collective-permute-start.10) | collective-permute-done | bytes 2080 | tf_op jit(solution)/shard_map/ppermute | solution.py:610
  (43 shorter events, 6.3 us)
Async XLA Ops:
  0.6 17.0 %copy-start = (s32[8192]{0:T(1024)S(1)}, s32[8192]{0:T(1024)}, u32[]{:S(2)}) copy-start(s32[8192]{0:T(1024)} %param.17) | copy-start | bytes 98308
  1.9 9.3 %collective-permute-start = (f32[66,1024]{1,0:T(8,128)S(1)}, f32[66,1024]{1,0:T(8,128)S(1)}, u32[]{:S(2)}, u32[]{:S(2)}) collective-permute-start(f32[66,1024]{1,0:T(8,128)S(1)} %get-tuple-element.43.up_ref), channel_id=1, source_target_pairs={{0,1},{1,2},{2,3},{3,4},{4,5},{5,6},{6,7},{7,8},{8,9},{9,10},{10,1... | collective-permute-start | bytes 811016 | tf_op jit(solution)/shard_map/ppermute | solution.py:536
  4.6 8.8 %collective-permute-start.1 = (f32[66,1024]{1,0:T(8,128)S(1)}, f32[66,1024]{1,0:T(8,128)S(1)}, u32[]{:S(2)}, u32[]{:S(2)}) collective-permute-start(f32[66,1024]{1,0:T(8,128)S(1)} %get-tuple-element.44.down_ref), channel_id=1, source_target_pairs={{1,0},{2,1},{3,2},{4,3},{5,4},{6,5},{7,6},{8,7},{9,8},{10,9},{11,1... | collective-permute-start | bytes 811016 | tf_op jit(solution)/shard_map/ppermute | solution.py:537
  14.5 5.8 %collective-permute-start.2 = (f32[40,1024]{1,0:T(8,128)S(1)}, f32[40,1024]{1,0:T(8,128)S(1)}, u32[]{:S(2)}, u32[]{:S(2)}) collective-permute-start(f32[40,1024]{1,0:T(8,128)S(1)} %get-tuple-element.46.refs_1_.up_ref), channel_id=1, source_target_pairs={{0,1},{1,2},{2,3},{3,4},{4,5},{5,6},{6,7},{7,8},{8,9},{9,10},{10,1... | collective-permute-start | bytes 491528 | tf_op jit(solution)/shard_map/ppermute | solution.py:536
  14.6 6.4 %collective-permute-start.3 = (f32[40,1024]{1,0:T(8,128)S(1)}, f32[40,1024]{1,0:T(8,128)S(1)}, u32[]{:S(2)}, u32[]{:S(2)}) collective-permute-start(f32[40,1024]{1,0:T(8,128)S(1)} %get-tuple-element.47.refs_0_.down_ref), channel_id=1, source_target_pairs={{1,0},{2,1},{3,2},{4,3},{5,4},{6,5},{7,6},{8,7},{9,8},{10,9},{11,1... | collective-permute-start | bytes 491528 | tf_op jit(solution)/shard_map/ppermute | solution.py:537
  17.6 9.3 %copy-start.2 = (s32[32]{0:T(128)S(1)}, s32[32]{0:T(128)}, u32[]{:S(2)}) copy-start(s32[32]{0:T(128)} %param.19) | copy-start | bytes 388
  18.4 10.4 %copy-start.3 = (f32[5]{0:T(128)S(1)}, f32[5]{0:T(128)}, u32[]{:S(2)}) copy-start(f32[5]{0:T(128)} %param.16) | copy-start | bytes 64
  21.9 7.8 %copy-start.1 = (f32[8192]{0:T(1024)S(1)}, f32[8192]{0:T(1024)}, u32[]{:S(2)}) copy-start(f32[8192]{0:T(1024)} %param.18) | copy-start | bytes 98308
  21.9 7.8 %collective-permute-start.4 = (f32[40,1024]{1,0:T(8,128)S(1)}, f32[40,1024]{1,0:T(8,128)S(1)}, u32[]{:S(2)}, u32[]{:S(2)}) collective-permute-start(f32[40,1024]{1,0:T(8,128)S(1)} %get-tuple-element.54.refs_1_.up_ref), channel_id=1, source_target_pairs={{0,1},{1,2},{2,3},{3,4},{4,5},{5,6},{6,7},{7,8},{8,9},{9,10},{10,1... | collective-permute-start | bytes 491528 | tf_op jit(solution)/shard_map/ppermute | solution.py:536
  22.0 7.7 %collective-permute-start.5 = (f32[40,1024]{1,0:T(8,128)S(1)}, f32[40,1024]{1,0:T(8,128)S(1)}, u32[]{:S(2)}, u32[]{:S(2)}) collective-permute-start(f32[40,1024]{1,0:T(8,128)S(1)} %get-tuple-element.55.refs_0_.down_ref), channel_id=1, source_target_pairs={{1,0},{2,1},{3,2},{4,3},{5,4},{6,5},{7,6},{8,7},{9,8},{10,9},{11,1... | collective-permute-start | bytes 491528 | tf_op jit(solution)/shard_map/ppermute | solution.py:537
  32.1 18.1 %all-to-all-start = ((f32[16,2,1152]{2,1,0:T(2,128)}), f32[16,2,1152]{2,1,0:T(2,128)S(1)}, u32[]{:S(2)}, u32[]{:S(2)}) async-start(f32[16,2,1152]{2,1,0:T(2,128)} %get-tuple-element.60), calls=%async_computation | async-start | bytes 294912 | tf_op jit(solution)/shard_map/all_to_all | solution.py:595
  51.1 5.6 %collective-permute-start.6 = (f32[4,2048]{1,0:T(4,128)S(1)}, f32[4,2048]{1,0:T(4,128)S(1)}, u32[]{:S(2)}, u32[]{:S(2)}) collective-permute-start(f32[4,2048]{1,0:T(4,128)S(1)} %get-tuple-element.66), channel_id=1, source_target_pairs={{0,2},{1,3},{2,0},{3,1},{4,6},{5,7},{6,4},{7,5},{8,10},{9,11},{10,... | collective-permute-start | bytes 98312 | tf_op jit(solution)/shard_map/ppermute | solution.py:610
  52.9 15.2 %all-to-all-start.1 = ((f32[16,2,2,512]{3,2,1,0:T(2,128)}), f32[16,2,2,512]{3,2,1,0:T(2,128)S(1)}, u32[]{:S(2)}, u32[]{:S(2)}) async-start(f32[16,2,2,512]{3,2,1,0:T(2,128)} %get-tuple-element.65), calls=%async_computation.1 | async-start | bytes 262144 | tf_op jit(solution)/shard_map/all_to_all | solution.py:615
  56.7 5.4 %collective-permute-start.7 = (f32[4,128]{1,0:T(4,128)S(1)}, f32[4,128]{1,0:T(4,128)S(1)}, u32[]{:S(2)}, u32[]{:S(2)}) collective-permute-start(f32[4,128]{1,0:T(4,128)S(1)} %slice_add_fusion), channel_id=1, source_target_pairs={{0,4},{1,5},{2,6},{3,7},{4,0},{5,1},{6,2},{7,3},{8,12},{9,13},{10,... | collective-permute-start | bytes 6152 | tf_op jit(solution)/shard_map/ppermute | solution.py:610
  58.0 5.0 %collective-permute-start.8 = (f32[4,128]{1,0:T(4,128)S(1)}, f32[4,128]{1,0:T(4,128)S(1)}, u32[]{:S(2)}, u32[]{:S(2)}) collective-permute-start(f32[4,128]{1,0:T(4,128)S(1)} %slice_add_fusion), channel_id=1, source_target_pairs={{0,8},{1,9},{2,10},{3,11},{4,12},{5,13},{6,14},{7,15},{8,0},{9,1},... | collective-permute-start | bytes 6152 | tf_op jit(solution)/shard_map/ppermute | solution.py:610
  62.0 3.9 %collective-permute-start.9 = (f32[4,128]{1,0:T(4,128)S(1)}, f32[4,128]{1,0:T(4,128)S(1)}, u32[]{:S(2)}, u32[]{:S(2)}) collective-permute-start(f32[4,128]{1,0:T(4,128)S(1)} %slice_add_fusion), channel_id=1, source_target_pairs={{0,12},{1,13},{2,14},{3,15},{4,8},{5,9},{6,10},{7,11},{8,4},{9,5},... | collective-permute-start | bytes 6152 | tf_op jit(solution)/shard_map/ppermute | solution.py:610
  66.0 2.1 %collective-permute-start.10 = (f32[4,128]{1,0:T(4,128)S(1)}, f32[4,128]{1,0:T(4,128)S(1)}, u32[]{:S(2)}, u32[]{:S(2)}) collective-permute-start(f32[4,128]{1,0:T(4,128)S(1)} %add_add_fusion), channel_id=1, source_target_pairs={{0,1},{1,0},{2,3},{3,2},{4,5},{5,4},{6,7},{7,6},{8,9},{9,8},{10,11... | collective-permute-start | bytes 6152 | tf_op jit(solution)/shard_map/ppermute | solution.py:610

commit v5 on v4

--- a/solution.py
+++ b/solution.py
@@ -470,8 +470,9 @@
     devices = lax.axis_size("phase")
     count = lax.axis_size("space")
     here = lax.axis_index("space")
-    forward = [(i, (i + 1) % count) for i in range(count)]
-    backward = [((i + 1) % count, i) for i in range(count)]
+    even = here % 2 == 0
+    inner_pairs = [(i, i ^ 1) for i in range(count)]
+    outer = [(i, (i - 1 + 2 * (i % 2)) % count) for i in range(count)]
 
     local_index = lax.dynamic_slice_in_dim(phase_index, lax.axis_index("phase") * 2, 2)
     angles = 2.0 * math.pi / blades * local_index.astype(f32)
@@ -533,8 +534,10 @@
     edge_shape = (2, 5, 8, cells)
     for step in range(steps):
         first, last = step == 0, step == steps - 1
-        lo = lax.ppermute(up, "space", forward)
-        hi = lax.ppermute(down, "space", backward)
+        apart = lax.ppermute(jnp.where(even, down, up), "space", outer)
+        inside = lax.ppermute(jnp.where(even, up, down), "space", inner_pairs)
+        lo = jnp.where(even, apart, inside)
+        hi = jnp.where(even, inside, apart)
         operands = [state, forcing, coef, own] + ([] if first else [down, up])
         got = call(
             functools.partial(pre_kernel, first),

time: 69.8 us -> 69.1 us (0.990)
  waiting for transfers between devices: 15.1 us -> 12.9 us
  starting transfers between devices: 32.8 us -> 34.8 us
    ppermute x6, waiting for transfers between devices: 2.85 us -> 0.63 us  [the longest x3 0.62 us: per_device(): apart = lax.ppermute(jnp.where(even, down, up), 'space', outer)]
    all_to_all x1, starting transfers between devices: 9.12 us -> 10.5 us  [per_device(): every = lax.all_to_all(mine, 'phase', 0, 0, tiled=True)]
    all_to_all x1, starting transfers between devices: 3.74 us -> 4.87 us  [per_device(): blocks = lax.all_to_all(turned, 'phase', 0, 0, tiled=True)]
    ppermute x5, starting transfers between devices: 8.48 us -> 7.75 us  [across(): return lax.ppermute(work, 'space', [(i, i ^ bits) for i in range(count)])]
  transfers between devices with their start and end apart: 13 -> 13, of which waited for: 6 -> 5; matrix products, arithmetic and copies ran while one was open for 3% -> 3% of each run, Pallas kernels for 15% -> 15%
where the time goes in v5:
time: 69.1 us; the launch traced here: 68.7 us
  starting transfers between devices  34.8 us (50%)
  Pallas kernels  17.5 us (25%)
  waiting for transfers between devices  12.9 us (19%)
  local copies, waits for them, and re-layouts  1.49 us (2%)
  other arithmetic  1.1 us (2%)
  between operations  0.93 us (1%)
    pallas_call x13, Pallas kernels, call(): pl.pallas_call(kernel, name=name, out_shape=[jax.ShapeDtypeStruct(s, d) f...  17.5 us
    all_to_all x1, starting transfers between devices, per_device(): every = lax.all_to_all(mine, 'phase', 0, 0, tiled=True)  10.5 us
    ppermute x3, starting transfers between devices, per_device(): inside = lax.ppermute(jnp.where(even, up, down), 'space', inner_pairs)  8.89 us
    ppermute x5, starting transfers between devices, across(): return lax.ppermute(work, 'space', [(i, i ^ bits) for i in range(count)])  7.75 us
    all_to_all x1, waiting for transfers between devices, per_device(): every = lax.all_to_all(mine, 'phase', 0, 0, tiled=True)  7.49 us
    all_to_all x1, starting transfers between devices, per_device(): blocks = lax.all_to_all(turned, 'phase', 0, 0, tiled=True)  4.87 us
    ppermute x5, waiting for transfers between devices, across(): return lax.ppermute(work, 'space', [(i, i ^ bits) for i in range(count)])  4.76 us
    ppermute x3, starting transfers between devices, per_device(): apart = lax.ppermute(jnp.where(even, down, up), 'space', outer)  2.87 us
  transfers between devices with their start and end apart: 13, of which 5 were waited for; matrix products, arithmetic and copies ran while one was open for 3% of the time, Pallas kernels for 15%

profile of v5, /device:TPU:1, one launch (start us, length us, event | category | flops | bytes accessed | tf_op | source)
XLA Modules:
  0.0 68.7 jit_solution(2973767346752408896)
XLA Ops:
  0.7 1.2 %pack.1 = (f32[6,8,1024]{2,1,0:T(8,128)S(1)}, f32[66,1024]{1,0:T(8,128)S(1)}, f32[66,1024]{1,0:T(8,128)S(1)}) custom-call(f32[2,2,5,8,1024]{4,3,2,1,0:T(8,128)} %x_ref.1, f32[2,2,5,8,1024]{4,3,2,1,0:T(8,128)} %f_ref.1, f32[4,8,1024]{2,1,0:T(8,128)} %cpl_hbm.1, f32[8,1024]{1,0:T(8,128)} %diag_hbm.1, f32[8,1024]{1,0:T(8,128)} %inert_hbm.1), custom_call_target="tpu_custom_call" | custom-call | flops 1048576 | bytes 1048576 | tf_op jit(solution)/shard_map/pack/pallas_call | solution.py:24
  2.0 2.7 %collective-permute-start = (f32[66,1024]{1,0:T(8,128)S(1)}, f32[66,1024]{1,0:T(8,128)S(1)}, u32[]{:S(2)}, u32[]{:S(2)}) collective-permute-start(f32[66,1024]{1,0:T(8,128)S(1)} %get-tuple-element.72), channel_id=1, source_target_pairs={{0,15},{1,2},{2,1},{3,4},{4,3},{5,6},{6,5},{7,8},{8,7},{9,10},{10,... | collective-permute-start | bytes 811016 | tf_op jit(solution)/shard_map/ppermute | solution.py:537
  4.7 2.3 %collective-permute-start.1 = (f32[66,1024]{1,0:T(8,128)S(1)}, f32[66,1024]{1,0:T(8,128)S(1)}, u32[]{:S(2)}, u32[]{:S(2)}) collective-permute-start(f32[66,1024]{1,0:T(8,128)S(1)} %get-tuple-element.71), channel_id=1, source_target_pairs={{0,1},{1,0},{2,3},{3,2},{4,5},{5,4},{6,7},{7,6},{8,9},{9,8},{10,11... | collective-permute-start | bytes 811016 | tf_op jit(solution)/shard_map/ppermute | solution.py:538
  8.6 1.0 %tables.1 = (bf16[160,144]{1,0:T(8,128)(2,1)S(1)}, bf16[200,240]{1,0:T(8,128)(2,1)S(1)}, bf16[200,240]{1,0:T(8,128)(2,1)S(1)}, bf16[200,240]{1,0:T(8,128)(2,1)S(1)}) custom-call(f32[4,5,5]{2,1,0:T(8,128)S(1)} %copy.22.jac_ref, f32[8]{0:T(128)S(1)} %reshape.148.rot_ref), custom_call_target="tpu_custom_call" | custom-call | flops 1048576 | bytes 1048576 | tf_op jit(solution)/shard_map/tables/pallas_call | solution.py:24
  9.7 3.2 %pre.3 = (f32[2,2,5,8,1024]{4,3,2,1,0:T(8,128)S(1)}, f32[2,40,1024]{2,1,0:T(8,128)S(1)}, f32[2,5,8,1024]{3,2,1,0:T(8,128)S(1)}, f32[2,6,8,1024]{3,2,1,0:T(8,128)S(1)}, f32[2,2,5,8,1024]{4,3,2,1,0:T(8,128)S(1)}) custom-call(f32[2,2,5,8,1024]{4,3,2,1,0:T(8,128)} %x_ref.1, f32[2,2,5,8,1024]{4,3,2,1,0:T(8,128)} %f_ref.1, ...), custom_call_target="tpu_custom_call" | custom-call | flops 41943040 | bytes 1048576 | tf_op jit(solution)/shard_map/pre/pallas_call | solution.py:24
  13.0 1.0 %post.3 = (f32[40,1024]{1,0:T(8,128)S(1)}, f32[40,1024]{1,0:T(8,128)S(1)}, f32[2,5,8,1024]{3,2,1,0:T(8,128)S(1)}, f32[2,6,8,1024]{3,2,1,0:T(8,128)S(1)}) custom-call(bf16[200,240]{1,0:T(8,128)(2,1)S(1)} %get-tuple-element.36.plain_ref, bf16[200,240]{1,0:T(8,128)(2,1)S(1)} %get-tuple-element.37.lo_turn_ref, ...), custom_call_target="tpu_custom_call" | custom-call | flops 20971520 | bytes 1048576 | tf_op jit(solution)/shard_map/post/pallas_call | solution.py:24
  14.2 3.0 %collective-permute-start.3 = (f32[40,1024]{1,0:T(8,128)S(1)}, f32[40,1024]{1,0:T(8,128)S(1)}, u32[]{:S(2)}, u32[]{:S(2)}) collective-permute-start(f32[40,1024]{1,0:T(8,128)S(1)} %get-tuple-element.79), channel_id=1, source_target_pairs={{0,1},{1,0},{2,3},{3,2},{4,5},{5,4},{6,7},{7,6},{8,9},{9,8},{10,11... | collective-permute-start | bytes 491528 | tf_op jit(solution)/shard_map/ppermute | solution.py:538
  17.2 0.8 %onehot.1.hot_ref.refs_4_ = bf16[16,256,512]{2,1,0:T(8,128)(2,1)S(1)} custom-call(s32[16,1,512]{2,1,0:T(1,128)S(1)} %bitcast.17), custom_call_target="tpu_custom_call" | custom-call | flops 8388608 | bytes 1048576 | tf_op jit(solution)/shard_map/onehot/pallas_call | solution.py:24
  18.0 1.8 %pre.4 = (f32[2,2,5,8,1024]{4,3,2,1,0:T(8,128)S(1)}, f32[2,40,1024]{2,1,0:T(8,128)S(1)}) custom-call(f32[2,2,5,8,1024]{4,3,2,1,0:T(8,128)S(1)} %get-tuple-element.48.x_ref, f32[2,2,5,8,1024]{4,3,2,1,0:T(8,128)S(1)} %get-tuple-element.49.f_ref, f32[6,8,1024]{2,1,0:T(8,128)S(1)} %get-tuple-element.39.coef_ref, bf16[160,144]{1,0:T(8,128)(2,1)S(1)} %get-tuple-element.40.own_ref, ...), custom_call_target="tpu_custom_call" | custom-call | flops 41943040 | bytes 1048576 | tf_op jit(solution)/shard_map/pre/pallas_call | solution.py:24
  20.4 0.9 %post.4 = (f32[40,1024]{1,0:T(8,128)S(1)}, f32[40,1024]{1,0:T(8,128)S(1)}) custom-call(bf16[200,240]{1,0:T(8,128)(2,1)S(1)} %get-tuple-element.36.plain_ref, bf16[200,240]{1,0:T(8,128)(2,1)S(1)} %get-tuple-element.37.lo_turn_ref, bf16[200,240]{1,0:T(8,128)(2,1)S(1)} %get-tuple-element.38.hi_turn_ref, f32[2,5,8,1024]{3,2,1,0:T(8,128)S(1)} %get-tuple-element.41.ef_ref, ...), custom_call_target="tpu_custom_call" | custom-call | flops 20971520 | bytes 1048576 | tf_op jit(solution)/shard_map/post/pallas_call | solution.py:24
  21.5 3.6 %collective-permute-start.5 = (f32[40,1024]{1,0:T(8,128)S(1)}, f32[40,1024]{1,0:T(8,128)S(1)}, u32[]{:S(2)}, u32[]{:S(2)}) collective-permute-start(f32[40,1024]{1,0:T(8,128)S(1)} %get-tuple-element.75), channel_id=1, source_target_pairs={{0,1},{1,0},{2,3},{3,2},{4,5},{5,4},{6,7},{7,6},{8,9},{9,8},{10,11... | collective-permute-start | bytes 491528 | tf_op jit(solution)/shard_map/ppermute | solution.py:538
  25.2 1.8 %pre.5 = (f32[2,2,5,8,1024]{4,3,2,1,0:T(8,128)S(1)}, f32[2,40,1024]{2,1,0:T(8,128)S(1)}) custom-call(f32[2,2,5,8,1024]{4,3,2,1,0:T(8,128)S(1)} %get-tuple-element.56.x_ref, f32[2,2,5,8,1024]{4,3,2,1,0:T(8,128)S(1)} %get-tuple-element.49.f_ref, f32[6,8,1024]{2,1,0:T(8,128)S(1)} %get-tuple-element.39.coef_ref, bf16[160,144]{1,0:T(8,128)(2,1)S(1)} %get-tuple-element.40.own_ref, ...), custom_call_target="tpu_custom_call" | custom-call | flops 41943040 | bytes 1048576 | tf_op jit(solution)/shard_map/pre/pallas_call | solution.py:24
  27.9 2.4 %post.5 = (f32[40,1024]{1,0:T(8,128)S(1)}, f32[40,1024]{1,0:T(8,128)S(1)}, f32[16,2,1152]{2,1,0:T(2,128)}) custom-call(bf16[200,240]{1,0:T(8,128)(2,1)S(1)} %get-tuple-element.36.plain_ref, bf16[200,240]{1,0:T(8,128)(2,1)S(1)} %get-tuple-element.37.lo_turn_ref, bf16[200,240]{1,0:T(8,128)(2,1)S(1)} %get-tuple-element.38.hi_turn_ref, ...), custom_call_target="tpu_custom_call" | custom-call | flops 20971520 | bytes 1048576 | tf_op jit(solution)/shard_map/post/pallas_call | solution.py:24
  30.3 10.5 %all-to-all-start = ((f32[16,2,1152]{2,1,0:T(2,128)}), f32[16,2,1152]{2,1,0:T(2,128)S(1)}, u32[]{:S(2)}, u32[]{:S(2)}) async-start(f32[16,2,1152]{2,1,0:T(2,128)} %get-tuple-element.60), calls=%async_computation | async-start | bytes 294912 | tf_op jit(solution)/shard_map/all_to_all | solution.py:598
  41.3 1.0 %merge.1 = f32[2,2,5,8,1024]{4,3,2,1,0:T(8,128)} custom-call(f32[2,2,5,8,1024]{4,3,2,1,0:T(8,128)S(1)} %get-tuple-element.59.x_ref, f32[40,1024]{1,0:T(8,128)S(1)} %get-tuple-element.61.down_ref, f32[40,1024]{1,0:T(8,128)S(1)} %get-tuple-element.62.up_ref), custom_call_target="tpu_custom_call" | custom-call | flops 1048576 | bytes 1048576 | tf_op jit(solution)/shard_map/merge/pallas_call | solution.py:24
  42.2 7.5 %all-to-all-done.x_ref = f32[16,2,1152]{2,1,0:T(2,128)S(1)} async-done(((f32[16,2,1152]{2,1,0:T(2,128)}), f32[16,2,1152]{2,1,0:T(2,128)S(1)}, u32[]{:S(2)}, u32[]{:S(2)}) %all-to-all-start) | async-done | bytes 147488 | tf_op jit(solution)/shard_map/all_to_all | solution.py:598
  49.7 0.9 %phases.1 = (f32[16,2,2,512]{3,2,1,0:T(2,128)}, f32[4,2048]{1,0:T(4,128)S(1)}) custom-call(f32[64,64]{1,0:T(8,128)S(1)} %bitcast.21, f32[2,4,32]{2,1,0:T(4,128)S(1)} %copy.28.work_table_ref, f32[16,2,1152]{2,1,0:T(2,128)S(1)} %all-to-all-done.x_ref), custom_call_target="tpu_custom_call" | custom-call | flops 16777216 | bytes 1048576 | tf_op jit(solution)/shard_map/phases/pallas_call | solution.py:24
  50.6 0.9 %collective-permute-start.6 = (f32[4,2048]{1,0:T(4,128)S(1)}, f32[4,2048]{1,0:T(4,128)S(1)}, u32[]{:S(2)}, u32[]{:S(2)}) collective-permute-start(f32[4,2048]{1,0:T(4,128)S(1)} %get-tuple-element.66), channel_id=1, source_target_pairs={{0,2},{1,3},{2,0},{3,1},{4,6},{5,7},{6,4},{7,5},{8,10},{9,11},{10,... | collective-permute-start | bytes 98312 | tf_op jit(solution)/shard_map/ppermute | solution.py:613
  51.5 4.9 %all-to-all-start.1 = ((f32[16,2,2,512]{3,2,1,0:T(2,128)}), f32[16,2,2,512]{3,2,1,0:T(2,128)S(1)}, u32[]{:S(2)}, u32[]{:S(2)}) async-start(f32[16,2,2,512]{3,2,1,0:T(2,128)} %get-tuple-element.65), calls=%async_computation.1 | async-start | bytes 262144 | tf_op jit(solution)/shard_map/all_to_all | solution.py:618
  56.8 3.9 %collective-permute-start.8 = (f32[4,128]{1,0:T(4,128)S(1)}, f32[4,128]{1,0:T(4,128)S(1)}, u32[]{:S(2)}, u32[]{:S(2)}) collective-permute-start(f32[4,128]{1,0:T(4,128)S(1)} %slice_add_fusion), channel_id=1, source_target_pairs={{0,8},{1,9},{2,10},{3,11},{4,12},{5,13},{6,14},{7,15},{8,0},{9,1},... | collective-permute-start | bytes 6152 | tf_op jit(solution)/shard_map/ppermute | solution.py:613
  60.7 1.0 %collective-permute-done.8 = f32[4,128]{1,0:T(4,128)S(1)} collective-permute-done((f32[4,128]{1,0:T(4,128)S(1)}, f32[4,128]{1,0:T(4,128)S(1)}, u32[]{:S(2)}, u32[]{:S(2)}) %collective-permute-start.8) | collective-permute-done | bytes 2080 | tf_op jit(solution)/shard_map/ppermute | solution.py:613
  61.7 2.9 %collective-permute-done.9 = f32[4,128]{1,0:T(4,128)S(1)} collective-permute-done((f32[4,128]{1,0:T(4,128)S(1)}, f32[4,128]{1,0:T(4,128)S(1)}, u32[]{:S(2)}, u32[]{:S(2)}) %collective-permute-start.9) | collective-permute-done | bytes 2080 | tf_op jit(solution)/shard_map/ppermute | solution.py:613
  64.6 2.6 %collective-permute-start.10 = (f32[4,128]{1,0:T(4,128)S(1)}, f32[4,128]{1,0:T(4,128)S(1)}, u32[]{:S(2)}, u32[]{:S(2)}) collective-permute-start(f32[4,128]{1,0:T(4,128)S(1)} %add_add_fusion), channel_id=1, source_target_pairs={{0,1},{1,0},{2,3},{3,2},{4,5},{5,4},{6,7},{7,6},{8,9},{9,8},{10,11... | collective-permute-start | bytes 6152 | tf_op jit(solution)/shard_map/ppermute | solution.py:613
  67.2 0.8 %collective-permute-done.10 = f32[4,128]{1,0:T(4,128)S(1)} collective-permute-done((f32[4,128]{1,0:T(4,128)S(1)}, f32[4,128]{1,0:T(4,128)S(1)}, u32[]{:S(2)}, u32[]{:S(2)}) %collective-permute-start.10) | collective-permute-done | bytes 2080 | tf_op jit(solution)/shard_map/ppermute | solution.py:613
  (49 shorter events, 5.3 us)
Async XLA Ops:
  0.6 16.5 %copy-start = (s32[8192]{0:T(1024)S(1)}, s32[8192]{0:T(1024)}, u32[]{:S(2)}) copy-start(s32[8192]{0:T(1024)} %param.17) | copy-start | bytes 98308
  2.0 10.9 %collective-permute-start = (f32[66,1024]{1,0:T(8,128)S(1)}, f32[66,1024]{1,0:T(8,128)S(1)}, u32[]{:S(2)}, u32[]{:S(2)}) collective-permute-start(f32[66,1024]{1,0:T(8,128)S(1)} %get-tuple-element.72), channel_id=1, source_target_pairs={{0,15},{1,2},{2,1},{3,4},{4,3},{5,6},{6,5},{7,8},{8,7},{9,10},{10,... | collective-permute-start | bytes 811016 | tf_op jit(solution)/shard_map/ppermute | solution.py:537
  4.7 8.2 %collective-permute-start.1 = (f32[66,1024]{1,0:T(8,128)S(1)}, f32[66,1024]{1,0:T(8,128)S(1)}, u32[]{:S(2)}, u32[]{:S(2)}) collective-permute-start(f32[66,1024]{1,0:T(8,128)S(1)} %get-tuple-element.71), channel_id=1, source_target_pairs={{0,1},{1,0},{2,3},{3,2},{4,5},{5,4},{6,7},{7,6},{8,9},{9,8},{10,11... | collective-permute-start | bytes 811016 | tf_op jit(solution)/shard_map/ppermute | solution.py:538
  14.1 6.3 %collective-permute-start.2 = (f32[40,1024]{1,0:T(8,128)S(1)}, f32[40,1024]{1,0:T(8,128)S(1)}, u32[]{:S(2)}, u32[]{:S(2)}) collective-permute-start(f32[40,1024]{1,0:T(8,128)S(1)} %get-tuple-element.80), channel_id=1, source_target_pairs={{0,15},{1,2},{2,1},{3,4},{4,3},{5,6},{6,5},{7,8},{8,7},{9,10},{10,... | collective-permute-start | bytes 491528 | tf_op jit(solution)/shard_map/ppermute | solution.py:537
  14.2 6.2 %collective-permute-start.3 = (f32[40,1024]{1,0:T(8,128)S(1)}, f32[40,1024]{1,0:T(8,128)S(1)}, u32[]{:S(2)}, u32[]{:S(2)}) collective-permute-start(f32[40,1024]{1,0:T(8,128)S(1)} %get-tuple-element.79), channel_id=1, source_target_pairs={{0,1},{1,0},{2,3},{3,2},{4,5},{5,4},{6,7},{7,6},{8,9},{9,8},{10,11... | collective-permute-start | bytes 491528 | tf_op jit(solution)/shard_map/ppermute | solution.py:538
  17.2 8.0 %copy-start.2 = (s32[32]{0:T(128)S(1)}, s32[32]{0:T(128)}, u32[]{:S(2)}) copy-start(s32[32]{0:T(128)} %param.19) | copy-start | bytes 388
  18.0 9.0 %copy-start.3 = (f32[5]{0:T(128)S(1)}, f32[5]{0:T(128)}, u32[]{:S(2)}) copy-start(f32[5]{0:T(128)} %param.16) | copy-start | bytes 64
  21.4 6.6 %copy-start.1 = (f32[8192]{0:T(1024)S(1)}, f32[8192]{0:T(1024)}, u32[]{:S(2)}) copy-start(f32[8192]{0:T(1024)} %param.18) | copy-start | bytes 98308
  21.4 6.5 %collective-permute-start.4 = (f32[40,1024]{1,0:T(8,128)S(1)}, f32[40,1024]{1,0:T(8,128)S(1)}, u32[]{:S(2)}, u32[]{:S(2)}) collective-permute-start(f32[40,1024]{1,0:T(8,128)S(1)} %get-tuple-element.76), channel_id=1, source_target_pairs={{0,15},{1,2},{2,1},{3,4},{4,3},{5,6},{6,5},{7,8},{8,7},{9,10},{10,... | collective-permute-start | bytes 491528 | tf_op jit(solution)/shard_map/ppermute | solution.py:537
  21.5 6.4 %collective-permute-start.5 = (f32[40,1024]{1,0:T(8,128)S(1)}, f32[40,1024]{1,0:T(8,128)S(1)}, u32[]{:S(2)}, u32[]{:S(2)}) collective-permute-start(f32[40,1024]{1,0:T(8,128)S(1)} %get-tuple-element.75), channel_id=1, source_target_pairs={{0,1},{1,0},{2,3},{3,2},{4,5},{5,4},{6,7},{7,6},{8,9},{9,8},{10,11... | collective-permute-start | bytes 491528 | tf_op jit(solution)/shard_map/ppermute | solution.py:538
  30.3 19.4 %all-to-all-start = ((f32[16,2,1152]{2,1,0:T(2,128)}), f32[16,2,1152]{2,1,0:T(2,128)S(1)}, u32[]{:S(2)}, u32[]{:S(2)}) async-start(f32[16,2,1152]{2,1,0:T(2,128)} %get-tuple-element.60), calls=%async_computation | async-start | bytes 294912 | tf_op jit(solution)/shard_map/all_to_all | solution.py:598
  50.6 5.7 %collective-permute-start.6 = (f32[4,2048]{1,0:T(4,128)S(1)}, f32[4,2048]{1,0:T(4,128)S(1)}, u32[]{:S(2)}, u32[]{:S(2)}) collective-permute-start(f32[4,2048]{1,0:T(4,128)S(1)} %get-tuple-element.66), channel_id=1, source_target_pairs={{0,2},{1,3},{2,0},{3,1},{4,6},{5,7},{6,4},{7,5},{8,10},{9,11},{10,... | collective-permute-start | bytes 98312 | tf_op jit(solution)/shard_map/ppermute | solution.py:613
  51.5 16.6 %all-to-all-start.1 = ((f32[16,2,2,512]{3,2,1,0:T(2,128)}), f32[16,2,2,512]{3,2,1,0:T(2,128)S(1)}, u32[]{:S(2)}, u32[]{:S(2)}) async-start(f32[16,2,2,512]{3,2,1,0:T(2,128)} %get-tuple-element.65), calls=%async_computation.1 | async-start | bytes 262144 | tf_op jit(solution)/shard_map/all_to_all | solution.py:618
  56.4 4.3 %collective-permute-start.7 = (f32[4,128]{1,0:T(4,128)S(1)}, f32[4,128]{1,0:T(4,128)S(1)}, u32[]{:S(2)}, u32[]{:S(2)}) collective-permute-start(f32[4,128]{1,0:T(4,128)S(1)} %slice_add_fusion), channel_id=1, source_target_pairs={{0,4},{1,5},{2,6},{3,7},{4,0},{5,1},{6,2},{7,3},{8,12},{9,13},{10,... | collective-permute-start | bytes 6152 | tf_op jit(solution)/shard_map/ppermute | solution.py:613
  56.8 4.9 %collective-permute-start.8 = (f32[4,128]{1,0:T(4,128)S(1)}, f32[4,128]{1,0:T(4,128)S(1)}, u32[]{:S(2)}, u32[]{:S(2)}) collective-permute-start(f32[4,128]{1,0:T(4,128)S(1)} %slice_add_fusion), channel_id=1, source_target_pairs={{0,8},{1,9},{2,10},{3,11},{4,12},{5,13},{6,14},{7,15},{8,0},{9,1},... | collective-permute-start | bytes 6152 | tf_op jit(solution)/shard_map/ppermute | solution.py:613
  60.7 3.9 %collective-permute-start.9 = (f32[4,128]{1,0:T(4,128)S(1)}, f32[4,128]{1,0:T(4,128)S(1)}, u32[]{:S(2)}, u32[]{:S(2)}) collective-permute-start(f32[4,128]{1,0:T(4,128)S(1)} %slice_add_fusion), channel_id=1, source_target_pairs={{0,12},{1,13},{2,14},{3,15},{4,8},{5,9},{6,10},{7,11},{8,4},{9,5},... | collective-permute-start | bytes 6152 | tf_op jit(solution)/shard_map/ppermute | solution.py:613
  64.6 3.4 %collective-permute-start.10 = (f32[4,128]{1,0:T(4,128)S(1)}, f32[4,128]{1,0:T(4,128)S(1)}, u32[]{:S(2)}, u32[]{:S(2)}) collective-permute-start(f32[4,128]{1,0:T(4,128)S(1)} %add_add_fusion), channel_id=1, source_target_pairs={{0,1},{1,0},{2,3},{3,2},{4,5},{5,4},{6,7},{7,6},{8,9},{9,8},{10,11... | collective-permute-start | bytes 6152 | tf_op jit(solution)/shard_map/ppermute | solution.py:613

commit v6 on v5

--- a/solution.py
+++ b/solution.py
@@ -134,8 +134,9 @@
             value = jnp.where(here, value, 0.0)
             for i in range(3):
                 tiles[i].append(value * factors[i])
+    spare = jnp.zeros((8, 80), jnp.float32)
     for i, ref in enumerate((plain_ref, lo_ref, hi_ref)):
-        ref[...] = split(jnp.concatenate(tiles[i], axis=0))
+        ref[...] = split(jnp.concatenate(tiles[i] + [spare], axis=0))
 
 
 def hot_kernel(idx_ref, hot_ref):
@@ -514,7 +515,7 @@
     own, *tables = call(
         tables_kernel,
         "tables",
-        [((160, 144), bf16)] + [((200, 240), bf16)] * 3,
+        [((160, 144), bf16)] + [((208, 240), bf16)] * 3,
         [],
         1 << 20,
         [jacobians, turn],

time: 69.1 us -> 69.1 us (level)
  no operation moved by 1% of the time
where the time goes in v6:
time: 69.1 us; the launch traced here: 68.7 us
  starting transfers between devices  34.9 us (51%)
  Pallas kernels  17.4 us (25%)
  waiting for transfers between devices  12.9 us (19%)
  local copies, waits for them, and re-layouts  1.49 us (2%)
  other arithmetic  1.1 us (2%)
  between operations  0.93 us (1%)
    pallas_call x13, Pallas kernels, call(): pl.pallas_call(kernel, name=name, out_shape=[jax.ShapeDtypeStruct(s, d) f...  17.4 us
    all_to_all x1, starting transfers between devices, per_device(): every = lax.all_to_all(mine, 'phase', 0, 0, tiled=True)  10.5 us
    ppermute x3, starting transfers between devices, per_device(): inside = lax.ppermute(jnp.where(even, up, down), 'space', inner_pairs)  8.91 us
    ppermute x5, starting transfers between devices, across(): return lax.ppermute(work, 'space', [(i, i ^ bits) for i in range(count)])  7.79 us
    all_to_all x1, waiting for transfers between devices, per_device(): every = lax.all_to_all(mine, 'phase', 0, 0, tiled=True)  7.49 us
    all_to_all x1, starting transfers between devices, per_device(): blocks = lax.all_to_all(turned, 'phase', 0, 0, tiled=True)  4.86 us
    ppermute x5, waiting for transfers between devices, across(): return lax.ppermute(work, 'space', [(i, i ^ bits) for i in range(count)])  4.76 us
    ppermute x3, starting transfers between devices, per_device(): apart = lax.ppermute(jnp.where(even, down, up), 'space', outer)  2.87 us
  transfers between devices with their start and end apart: 13, of which 5 were waited for; matrix products, arithmetic and copies ran while one was open for 3% of the time, Pallas kernels for 15%

profile of v6, /device:TPU:1, one launch (start us, length us, event | category | flops | bytes accessed | tf_op | source)
XLA Modules:
  0.0 68.7 jit_solution(6646277505835991287)
XLA Ops:
  0.7 1.2 %pack.1 = (f32[6,8,1024]{2,1,0:T(8,128)S(1)}, f32[66,1024]{1,0:T(8,128)S(1)}, f32[66,1024]{1,0:T(8,128)S(1)}) custom-call(f32[2,2,5,8,1024]{4,3,2,1,0:T(8,128)} %x_ref.1, f32[2,2,5,8,1024]{4,3,2,1,0:T(8,128)} %f_ref.1, f32[4,8,1024]{2,1,0:T(8,128)} %cpl_hbm.1, f32[8,1024]{1,0:T(8,128)} %diag_hbm.1, f32[8,1024]{1,0:T(8,128)} %inert_hbm.1), custom_call_target="tpu_custom_call" | custom-call | flops 1048576 | bytes 1048576 | tf_op jit(solution)/shard_map/pack/pallas_call | solution.py:24
  2.0 2.7 %collective-permute-start = (f32[66,1024]{1,0:T(8,128)S(1)}, f32[66,1024]{1,0:T(8,128)S(1)}, u32[]{:S(2)}, u32[]{:S(2)}) collective-permute-start(f32[66,1024]{1,0:T(8,128)S(1)} %get-tuple-element.72), channel_id=1, source_target_pairs={{0,15},{1,2},{2,1},{3,4},{4,3},{5,6},{6,5},{7,8},{8,7},{9,10},{10,... | collective-permute-start | bytes 811016 | tf_op jit(solution)/shard_map/ppermute | solution.py:538
  4.7 2.3 %collective-permute-start.1 = (f32[66,1024]{1,0:T(8,128)S(1)}, f32[66,1024]{1,0:T(8,128)S(1)}, u32[]{:S(2)}, u32[]{:S(2)}) collective-permute-start(f32[66,1024]{1,0:T(8,128)S(1)} %get-tuple-element.71), channel_id=1, source_target_pairs={{0,1},{1,0},{2,3},{3,2},{4,5},{5,4},{6,7},{7,6},{8,9},{9,8},{10,11... | collective-permute-start | bytes 811016 | tf_op jit(solution)/shard_map/ppermute | solution.py:539
  8.6 1.0 %tables.1 = (bf16[160,144]{1,0:T(8,128)(2,1)S(1)}, bf16[208,240]{1,0:T(8,128)(2,1)S(1)}, bf16[208,240]{1,0:T(8,128)(2,1)S(1)}, bf16[208,240]{1,0:T(8,128)(2,1)S(1)}) custom-call(f32[4,5,5]{2,1,0:T(8,128)S(1)} %copy.22.jac_ref, f32[8]{0:T(128)S(1)} %reshape.148.rot_ref), custom_call_target="tpu_custom_call" | custom-call | flops 1048576 | bytes 1048576 | tf_op jit(solution)/shard_map/tables/pallas_call | solution.py:24
  9.7 3.2 %pre.3 = (f32[2,2,5,8,1024]{4,3,2,1,0:T(8,128)S(1)}, f32[2,40,1024]{2,1,0:T(8,128)S(1)}, f32[2,5,8,1024]{3,2,1,0:T(8,128)S(1)}, f32[2,6,8,1024]{3,2,1,0:T(8,128)S(1)}, f32[2,2,5,8,1024]{4,3,2,1,0:T(8,128)S(1)}) custom-call(f32[2,2,5,8,1024]{4,3,2,1,0:T(8,128)} %x_ref.1, f32[2,2,5,8,1024]{4,3,2,1,0:T(8,128)} %f_ref.1, ...), custom_call_target="tpu_custom_call" | custom-call | flops 41943040 | bytes 1048576 | tf_op jit(solution)/shard_map/pre/pallas_call | solution.py:24
  13.0 1.0 %post.3 = (f32[40,1024]{1,0:T(8,128)S(1)}, f32[40,1024]{1,0:T(8,128)S(1)}, f32[2,5,8,1024]{3,2,1,0:T(8,128)S(1)}, f32[2,6,8,1024]{3,2,1,0:T(8,128)S(1)}) custom-call(bf16[208,240]{1,0:T(8,128)(2,1)S(1)} %get-tuple-element.36.plain_ref, bf16[208,240]{1,0:T(8,128)(2,1)S(1)} %get-tuple-element.37.lo_turn_ref, ...), custom_call_target="tpu_custom_call" | custom-call | flops 20971520 | bytes 1048576 | tf_op jit(solution)/shard_map/post/pallas_call | solution.py:24
  14.2 3.0 %collective-permute-start.3 = (f32[40,1024]{1,0:T(8,128)S(1)}, f32[40,1024]{1,0:T(8,128)S(1)}, u32[]{:S(2)}, u32[]{:S(2)}) collective-permute-start(f32[40,1024]{1,0:T(8,128)S(1)} %get-tuple-element.79), channel_id=1, source_target_pairs={{0,1},{1,0},{2,3},{3,2},{4,5},{5,4},{6,7},{7,6},{8,9},{9,8},{10,11... | collective-permute-start | bytes 491528 | tf_op jit(solution)/shard_map/ppermute | solution.py:539
  17.2 0.8 %onehot.1.hot_ref.refs_4_ = bf16[16,256,512]{2,1,0:T(8,128)(2,1)S(1)} custom-call(s32[16,1,512]{2,1,0:T(1,128)S(1)} %bitcast.17), custom_call_target="tpu_custom_call" | custom-call | flops 8388608 | bytes 1048576 | tf_op jit(solution)/shard_map/onehot/pallas_call | solution.py:24
  18.0 1.8 %pre.4 = (f32[2,2,5,8,1024]{4,3,2,1,0:T(8,128)S(1)}, f32[2,40,1024]{2,1,0:T(8,128)S(1)}) custom-call(f32[2,2,5,8,1024]{4,3,2,1,0:T(8,128)S(1)} %get-tuple-element.48.x_ref, f32[2,2,5,8,1024]{4,3,2,1,0:T(8,128)S(1)} %get-tuple-element.49.f_ref, f32[6,8,1024]{2,1,0:T(8,128)S(1)} %get-tuple-element.39.coef_ref, bf16[160,144]{1,0:T(8,128)(2,1)S(1)} %get-tuple-element.40.own_ref, ...), custom_call_target="tpu_custom_call" | custom-call | flops 41943040 | bytes 1048576 | tf_op jit(solution)/shard_map/pre/pallas_call | solution.py:24
  20.4 0.9 %post.4 = (f32[40,1024]{1,0:T(8,128)S(1)}, f32[40,1024]{1,0:T(8,128)S(1)}) custom-call(bf16[208,240]{1,0:T(8,128)(2,1)S(1)} %get-tuple-element.36.plain_ref, bf16[208,240]{1,0:T(8,128)(2,1)S(1)} %get-tuple-element.37.lo_turn_ref, bf16[208,240]{1,0:T(8,128)(2,1)S(1)} %get-tuple-element.38.hi_turn_ref, f32[2,5,8,1024]{3,2,1,0:T(8,128)S(1)} %get-tuple-element.41.ef_ref, ...), custom_call_target="tpu_custom_call" | custom-call | flops 20971520 | bytes 1048576 | tf_op jit(solution)/shard_map/post/pallas_call | solution.py:24
  21.5 3.6 %collective-permute-start.5 = (f32[40,1024]{1,0:T(8,128)S(1)}, f32[40,1024]{1,0:T(8,128)S(1)}, u32[]{:S(2)}, u32[]{:S(2)}) collective-permute-start(f32[40,1024]{1,0:T(8,128)S(1)} %get-tuple-element.75), channel_id=1, source_target_pairs={{0,1},{1,0},{2,3},{3,2},{4,5},{5,4},{6,7},{7,6},{8,9},{9,8},{10,11... | collective-permute-start | bytes 491528 | tf_op jit(solution)/shard_map/ppermute | solution.py:539
  25.2 1.8 %pre.5 = (f32[2,2,5,8,1024]{4,3,2,1,0:T(8,128)S(1)}, f32[2,40,1024]{2,1,0:T(8,128)S(1)}) custom-call(f32[2,2,5,8,1024]{4,3,2,1,0:T(8,128)S(1)} %get-tuple-element.56.x_ref, f32[2,2,5,8,1024]{4,3,2,1,0:T(8,128)S(1)} %get-tuple-element.49.f_ref, f32[6,8,1024]{2,1,0:T(8,128)S(1)} %get-tuple-element.39.coef_ref, bf16[160,144]{1,0:T(8,128)(2,1)S(1)} %get-tuple-element.40.own_ref, ...), custom_call_target="tpu_custom_call" | custom-call | flops 41943040 | bytes 1048576 | tf_op jit(solution)/shard_map/pre/pallas_call | solution.py:24
  27.9 2.4 %post.5 = (f32[40,1024]{1,0:T(8,128)S(1)}, f32[40,1024]{1,0:T(8,128)S(1)}, f32[16,2,1152]{2,1,0:T(2,128)}) custom-call(bf16[208,240]{1,0:T(8,128)(2,1)S(1)} %get-tuple-element.36.plain_ref, bf16[208,240]{1,0:T(8,128)(2,1)S(1)} %get-tuple-element.37.lo_turn_ref, bf16[208,240]{1,0:T(8,128)(2,1)S(1)} %get-tuple-element.38.hi_turn_ref, ...), custom_call_target="tpu_custom_call" | custom-call | flops 20971520 | bytes 1048576 | tf_op jit(solution)/shard_map/post/pallas_call | solution.py:24
  30.3 10.5 %all-to-all-start = ((f32[16,2,1152]{2,1,0:T(2,128)}), f32[16,2,1152]{2,1,0:T(2,128)S(1)}, u32[]{:S(2)}, u32[]{:S(2)}) async-start(f32[16,2,1152]{2,1,0:T(2,128)} %get-tuple-element.60), calls=%async_computation | async-start | bytes 294912 | tf_op jit(solution)/shard_map/all_to_all | solution.py:599
  41.2 1.0 %merge.1 = f32[2,2,5,8,1024]{4,3,2,1,0:T(8,128)} custom-call(f32[2,2,5,8,1024]{4,3,2,1,0:T(8,128)S(1)} %get-tuple-element.59.x_ref, f32[40,1024]{1,0:T(8,128)S(1)} %get-tuple-element.61.down_ref, f32[40,1024]{1,0:T(8,128)S(1)} %get-tuple-element.62.up_ref), custom_call_target="tpu_custom_call" | custom-call | flops 1048576 | bytes 1048576 | tf_op jit(solution)/shard_map/merge/pallas_call | solution.py:24
  42.2 7.5 %all-to-all-done.x_ref = f32[16,2,1152]{2,1,0:T(2,128)S(1)} async-done(((f32[16,2,1152]{2,1,0:T(2,128)}), f32[16,2,1152]{2,1,0:T(2,128)S(1)}, u32[]{:S(2)}, u32[]{:S(2)}) %all-to-all-start) | async-done | bytes 147488 | tf_op jit(solution)/shard_map/all_to_all | solution.py:599
  49.7 0.9 %phases.1 = (f32[16,2,2,512]{3,2,1,0:T(2,128)}, f32[4,2048]{1,0:T(4,128)S(1)}) custom-call(f32[64,64]{1,0:T(8,128)S(1)} %bitcast.21, f32[2,4,32]{2,1,0:T(4,128)S(1)} %copy.28.work_table_ref, f32[16,2,1152]{2,1,0:T(2,128)S(1)} %all-to-all-done.x_ref), custom_call_target="tpu_custom_call" | custom-call | flops 16777216 | bytes 1048576 | tf_op jit(solution)/shard_map/phases/pallas_call | solution.py:24
  50.6 0.9 %collective-permute-start.6 = (f32[4,2048]{1,0:T(4,128)S(1)}, f32[4,2048]{1,0:T(4,128)S(1)}, u32[]{:S(2)}, u32[]{:S(2)}) collective-permute-start(f32[4,2048]{1,0:T(4,128)S(1)} %get-tuple-element.66), channel_id=1, source_target_pairs={{0,2},{1,3},{2,0},{3,1},{4,6},{5,7},{6,4},{7,5},{8,10},{9,11},{10,... | collective-permute-start | bytes 98312 | tf_op jit(solution)/shard_map/ppermute | solution.py:614
  51.5 4.9 %all-to-all-start.1 = ((f32[16,2,2,512]{3,2,1,0:T(2,128)}), f32[16,2,2,512]{3,2,1,0:T(2,128)S(1)}, u32[]{:S(2)}, u32[]{:S(2)}) async-start(f32[16,2,2,512]{3,2,1,0:T(2,128)} %get-tuple-element.65), calls=%async_computation.1 | async-start | bytes 262144 | tf_op jit(solution)/shard_map/all_to_all | solution.py:619
  56.8 3.9 %collective-permute-start.8 = (f32[4,128]{1,0:T(4,128)S(1)}, f32[4,128]{1,0:T(4,128)S(1)}, u32[]{:S(2)}, u32[]{:S(2)}) collective-permute-start(f32[4,128]{1,0:T(4,128)S(1)} %slice_add_fusion), channel_id=1, source_target_pairs={{0,8},{1,9},{2,10},{3,11},{4,12},{5,13},{6,14},{7,15},{8,0},{9,1},... | collective-permute-start | bytes 6152 | tf_op jit(solution)/shard_map/ppermute | solution.py:614
  60.7 1.0 %collective-permute-done.8 = f32[4,128]{1,0:T(4,128)S(1)} collective-permute-done((f32[4,128]{1,0:T(4,128)S(1)}, f32[4,128]{1,0:T(4,128)S(1)}, u32[]{:S(2)}, u32[]{:S(2)}) %collective-permute-start.8) | collective-permute-done | bytes 2080 | tf_op jit(solution)/shard_map/ppermute | solution.py:614
  61.7 2.9 %collective-permute-done.9 = f32[4,128]{1,0:T(4,128)S(1)} collective-permute-done((f32[4,128]{1,0:T(4,128)S(1)}, f32[4,128]{1,0:T(4,128)S(1)}, u32[]{:S(2)}, u32[]{:S(2)}) %collective-permute-start.9) | collective-permute-done | bytes 2080 | tf_op jit(solution)/shard_map/ppermute | solution.py:614
  64.7 2.6 %collective-permute-start.10 = (f32[4,128]{1,0:T(4,128)S(1)}, f32[4,128]{1,0:T(4,128)S(1)}, u32[]{:S(2)}, u32[]{:S(2)}) collective-permute-start(f32[4,128]{1,0:T(4,128)S(1)} %add_add_fusion), channel_id=1, source_target_pairs={{0,1},{1,0},{2,3},{3,2},{4,5},{5,4},{6,7},{7,6},{8,9},{9,8},{10,11... | collective-permute-start | bytes 6152 | tf_op jit(solution)/shard_map/ppermute | solution.py:614
  67.2 0.8 %collective-permute-done.10 = f32[4,128]{1,0:T(4,128)S(1)} collective-permute-done((f32[4,128]{1,0:T(4,128)S(1)}, f32[4,128]{1,0:T(4,128)S(1)}, u32[]{:S(2)}, u32[]{:S(2)}) %collective-permute-start.10) | collective-permute-done | bytes 2080 | tf_op jit(solution)/shard_map/ppermute | solution.py:614
  (49 shorter events, 5.3 us)
Async XLA Ops:
  0.6 16.5 %copy-start = (s32[8192]{0:T(1024)S(1)}, s32[8192]{0:T(1024)}, u32[]{:S(2)}) copy-start(s32[8192]{0:T(1024)} %param.17) | copy-start | bytes 98308
  2.0 10.9 %collective-permute-start = (f32[66,1024]{1,0:T(8,128)S(1)}, f32[66,1024]{1,0:T(8,128)S(1)}, u32[]{:S(2)}, u32[]{:S(2)}) collective-permute-start(f32[66,1024]{1,0:T(8,128)S(1)} %get-tuple-element.72), channel_id=1, source_target_pairs={{0,15},{1,2},{2,1},{3,4},{4,3},{5,6},{6,5},{7,8},{8,7},{9,10},{10,... | collective-permute-start | bytes 811016 | tf_op jit(solution)/shard_map/ppermute | solution.py:538
  4.7 8.2 %collective-permute-start.1 = (f32[66,1024]{1,0:T(8,128)S(1)}, f32[66,1024]{1,0:T(8,128)S(1)}, u32[]{:S(2)}, u32[]{:S(2)}) collective-permute-start(f32[66,1024]{1,0:T(8,128)S(1)} %get-tuple-element.71), channel_id=1, source_target_pairs={{0,1},{1,0},{2,3},{3,2},{4,5},{5,4},{6,7},{7,6},{8,9},{9,8},{10,11... | collective-permute-start | bytes 811016 | tf_op jit(solution)/shard_map/ppermute | solution.py:539
  14.1 6.3 %collective-permute-start.2 = (f32[40,1024]{1,0:T(8,128)S(1)}, f32[40,1024]{1,0:T(8,128)S(1)}, u32[]{:S(2)}, u32[]{:S(2)}) collective-permute-start(f32[40,1024]{1,0:T(8,128)S(1)} %get-tuple-element.80), channel_id=1, source_target_pairs={{0,15},{1,2},{2,1},{3,4},{4,3},{5,6},{6,5},{7,8},{8,7},{9,10},{10,... | collective-permute-start | bytes 491528 | tf_op jit(solution)/shard_map/ppermute | solution.py:538
  14.2 6.2 %collective-permute-start.3 = (f32[40,1024]{1,0:T(8,128)S(1)}, f32[40,1024]{1,0:T(8,128)S(1)}, u32[]{:S(2)}, u32[]{:S(2)}) collective-permute-start(f32[40,1024]{1,0:T(8,128)S(1)} %get-tuple-element.79), channel_id=1, source_target_pairs={{0,1},{1,0},{2,3},{3,2},{4,5},{5,4},{6,7},{7,6},{8,9},{9,8},{10,11... | collective-permute-start | bytes 491528 | tf_op jit(solution)/shard_map/ppermute | solution.py:539
  17.2 8.0 %copy-start.2 = (s32[32]{0:T(128)S(1)}, s32[32]{0:T(128)}, u32[]{:S(2)}) copy-start(s32[32]{0:T(128)} %param.19) | copy-start | bytes 388
  18.0 9.0 %copy-start.3 = (f32[5]{0:T(128)S(1)}, f32[5]{0:T(128)}, u32[]{:S(2)}) copy-start(f32[5]{0:T(128)} %param.16) | copy-start | bytes 64
  21.4 6.5 %copy-start.1 = (f32[8192]{0:T(1024)S(1)}, f32[8192]{0:T(1024)}, u32[]{:S(2)}) copy-start(f32[8192]{0:T(1024)} %param.18) | copy-start | bytes 98308
  21.4 6.4 %collective-permute-start.4 = (f32[40,1024]{1,0:T(8,128)S(1)}, f32[40,1024]{1,0:T(8,128)S(1)}, u32[]{:S(2)}, u32[]{:S(2)}) collective-permute-start(f32[40,1024]{1,0:T(8,128)S(1)} %get-tuple-element.76), channel_id=1, source_target_pairs={{0,15},{1,2},{2,1},{3,4},{4,3},{5,6},{6,5},{7,8},{8,7},{9,10},{10,... | collective-permute-start | bytes 491528 | tf_op jit(solution)/shard_map/ppermute | solution.py:538
  21.5 6.3 %collective-permute-start.5 = (f32[40,1024]{1,0:T(8,128)S(1)}, f32[40,1024]{1,0:T(8,128)S(1)}, u32[]{:S(2)}, u32[]{:S(2)}) collective-permute-start(f32[40,1024]{1,0:T(8,128)S(1)} %get-tuple-element.75), channel_id=1, source_target_pairs={{0,1},{1,0},{2,3},{3,2},{4,5},{5,4},{6,7},{7,6},{8,9},{9,8},{10,11... | collective-permute-start | bytes 491528 | tf_op jit(solution)/shard_map/ppermute | solution.py:539
  30.3 19.4 %all-to-all-start = ((f32[16,2,1152]{2,1,0:T(2,128)}), f32[16,2,1152]{2,1,0:T(2,128)S(1)}, u32[]{:S(2)}, u32[]{:S(2)}) async-start(f32[16,2,1152]{2,1,0:T(2,128)} %get-tuple-element.60), calls=%async_computation | async-start | bytes 294912 | tf_op jit(solution)/shard_map/all_to_all | solution.py:599
  50.6 5.7 %collective-permute-start.6 = (f32[4,2048]{1,0:T(4,128)S(1)}, f32[4,2048]{1,0:T(4,128)S(1)}, u32[]{:S(2)}, u32[]{:S(2)}) collective-permute-start(f32[4,2048]{1,0:T(4,128)S(1)} %get-tuple-element.66), channel_id=1, source_target_pairs={{0,2},{1,3},{2,0},{3,1},{4,6},{5,7},{6,4},{7,5},{8,10},{9,11},{10,... | collective-permute-start | bytes 98312 | tf_op jit(solution)/shard_map/ppermute | solution.py:614
  51.5 16.6 %all-to-all-start.1 = ((f32[16,2,2,512]{3,2,1,0:T(2,128)}), f32[16,2,2,512]{3,2,1,0:T(2,128)S(1)}, u32[]{:S(2)}, u32[]{:S(2)}) async-start(f32[16,2,2,512]{3,2,1,0:T(2,128)} %get-tuple-element.65), calls=%async_computation.1 | async-start | bytes 262144 | tf_op jit(solution)/shard_map/all_to_all | solution.py:619
  56.3 4.4 %collective-permute-start.7 = (f32[4,128]{1,0:T(4,128)S(1)}, f32[4,128]{1,0:T(4,128)S(1)}, u32[]{:S(2)}, u32[]{:S(2)}) collective-permute-start(f32[4,128]{1,0:T(4,128)S(1)} %slice_add_fusion), channel_id=1, source_target_pairs={{0,4},{1,5},{2,6},{3,7},{4,0},{5,1},{6,2},{7,3},{8,12},{9,13},{10,... | collective-permute-start | bytes 6152 | tf_op jit(solution)/shard_map/ppermute | solution.py:614
  56.8 4.9 %collective-permute-start.8 = (f32[4,128]{1,0:T(4,128)S(1)}, f32[4,128]{1,0:T(4,128)S(1)}, u32[]{:S(2)}, u32[]{:S(2)}) collective-permute-start(f32[4,128]{1,0:T(4,128)S(1)} %slice_add_fusion), channel_id=1, source_target_pairs={{0,8},{1,9},{2,10},{3,11},{4,12},{5,13},{6,14},{7,15},{8,0},{9,1},... | collective-permute-start | bytes 6152 | tf_op jit(solution)/shard_map/ppermute | solution.py:614
  60.7 3.9 %collective-permute-start.9 = (f32[4,128]{1,0:T(4,128)S(1)}, f32[4,128]{1,0:T(4,128)S(1)}, u32[]{:S(2)}, u32[]{:S(2)}) collective-permute-start(f32[4,128]{1,0:T(4,128)S(1)} %slice_add_fusion), channel_id=1, source_target_pairs={{0,12},{1,13},{2,14},{3,15},{4,8},{5,9},{6,10},{7,11},{8,4},{9,5},... | collective-permute-start | bytes 6152 | tf_op jit(solution)/shard_map/ppermute | solution.py:614
  64.7 3.4 %collective-permute-start.10 = (f32[4,128]{1,0:T(4,128)S(1)}, f32[4,128]{1,0:T(4,128)S(1)}, u32[]{:S(2)}, u32[]{:S(2)}) collective-permute-start(f32[4,128]{1,0:T(4,128)S(1)} %add_add_fusion), channel_id=1, source_target_pairs={{0,1},{1,0},{2,3},{3,2},{4,5},{5,4},{6,7},{7,6},{8,9},{9,8},{10,11... | collective-permute-start | bytes 6152 | tf_op jit(solution)/shard_map/ppermute | solution.py:614
